TPU v7x, 32 devices: a whole 2x2x4 slice. The times are simulated.
32 devices in a mesh: phi: 8 (over z, x), row: 4 (over y, core).
Axes of the slice: x: 2, y: 2, z: 4, core: 2. Of those that a mesh axis runs over, the one named last changes fastest.
Arguments:
- density: float32 [128, 32, 512], P('phi', None, 'row'), may hold values from 0.5 to 2
- velocity: float32 [3, 128, 32, 512], P(None, 'phi', None, 'row'), may hold values from -0.3 to 0.3
- shifts: int32 [64], P('row'), may hold values from 0 to 31, as said below
- fractions: float32 [64], P('row'), may hold values from 0 to 1
Outputs:
- density_out: float32 [128, 32, 512], P('phi', None, 'row')
- stepped_velocity: float32 [3, 128, 32, 512], P(None, 'phi', None, 'row')
- image: float32 [1024, 1024], P(('phi', 'row'))
Inputs may be any that keep to these rules, and one draw needn't show every extreme that they name: `shifts`: some band has shift 0 and some band has shift 32 - 1.
All inputs are finite; a program needn't handle non-finite values.
Results may differ from a plain program's by a relative error of at most 0.000071.
Values sent between devices are 32-bit elements; how exact they have to be, the bound alone decides.
No kernel may reach another device: no remote copies, remote signals or barrier semaphores. Data moves between devices by JAX's collectives and lax.ppermute only.
A program may use at most 64 MiB of HBM per device.

v0:
```python
import jax
import jax.numpy as jnp
from jax import lax
from jax.sharding import PartitionSpec as P

BAND = 8
STEPS = 2
NPIX = 1024


SPEED = 1.5
COURANT = 0.05
KAPPA = 1.5
R_INNER = 0.2


def padded(cells, sides, width, closed):
    for axis, dim in sides:
        count = lax.axis_size(axis)
        ends = count if closed else count - 1
        head = lax.slice_in_dim(cells, 0, width, axis=dim)
        tail = lax.slice_in_dim(cells, cells.shape[dim] - width, cells.shape[dim], axis=dim)
        cells = jnp.concatenate(
            [
                lax.ppermute(tail, axis, [(i, (i + 1) % count) for i in range(ends)]),
                cells,
                lax.ppermute(head, axis, [((i + 1) % count, i) for i in range(ends)]),
            ],
            axis=dim,
        )
    return cells


def passed_along(value, axis, steps):
    count = lax.axis_size(axis)
    pairs = [(source, (source + steps) % count) for source in range(count)]
    return lax.ppermute(value, axis, pairs)


def conserved(prim):
    rho = prim[0]
    return jnp.stack([rho, rho * prim[1], rho * prim[2], rho * prim[3]])


def divergence(extended, axis, comp):
    cons = conserved(extended)
    flux = cons * extended[comp][None]
    flux = flux.at[comp].add(extended[0])
    size = extended.shape[axis]
    low_c = lax.slice_in_dim(cons, 0, size - 1, axis=axis)
    high_c = lax.slice_in_dim(cons, 1, size, axis=axis)
    low_f = lax.slice_in_dim(flux, 0, size - 1, axis=axis)
    high_f = lax.slice_in_dim(flux, 1, size, axis=axis)
    face = 0.5 * (low_f + high_f) - 0.5 * SPEED * (high_c - low_c)
    return lax.slice_in_dim(face, 1, size - 1, axis=axis) - lax.slice_in_dim(
        face, 0, size - 2, axis=axis
    )


def advance(prim, ext_phi, padded_polar_grid, ext_radial):
    total = (
        divergence(ext_phi, 1, 2)
        + divergence(padded_polar_grid, 2, 3)
        + divergence(ext_radial, 3, 1)
    )
    fresh = conserved(prim) - COURANT * total
    rho = fresh[0]
    return jnp.stack([rho, fresh[1] / rho, fresh[2] / rho, fresh[3] / rho])


def column_light(rho, radial_index, total_radial):
    polar = rho.shape[1]
    dtau = KAPPA / polar * rho
    above = jnp.cumsum(dtau, axis=1) - dtau
    theta = (jnp.arange(polar, dtype=jnp.int32).astype(jnp.float32) + 0.5) / polar
    tilt = 1.0 + 0.5 * jnp.cos(jnp.pi * theta)
    radius = R_INNER + (radial_index.astype(jnp.float32) + 0.5) * (1.0 - R_INNER) / total_radial
    source = (1.0 / jnp.sqrt(radius))[None, None, :] * tilt[None, :, None]
    return jnp.sum(source * (1.0 - jnp.exp(-dtau)) * jnp.exp(-above), axis=1)


def pixel_corners(pixel_rows, npix, nphi, nrad):
    yy = ((pixel_rows.astype(jnp.float32) + 0.5) / npix * 2.0 - 1.0)[:, None]
    xx = ((jnp.arange(npix, dtype=jnp.int32).astype(jnp.float32) + 0.5) / npix * 2.0 - 1.0)[None, :]
    dist = jnp.sqrt(xx * xx + yy * yy)
    upos = (dist - R_INNER) / (1.0 - R_INNER) * nrad - 0.5
    radial_floor_index = jnp.floor(upos)
    radial_fraction = upos - radial_floor_index
    radial_lower_index = radial_floor_index.astype(jnp.int32)
    angle = jnp.arctan2(yy, xx)
    vpos = (angle + jnp.pi) / (2.0 * jnp.pi) * nphi - 0.5
    lfloor = jnp.floor(vpos)
    polar_fraction = vpos - lfloor
    polar_lower_index = lfloor.astype(jnp.int32) % nphi
    polar_upper_index = (polar_lower_index + 1) % nphi
    return [
        (polar_lower_index, radial_lower_index, (1.0 - polar_fraction) * (1.0 - radial_fraction)),
        (polar_upper_index, radial_lower_index, polar_fraction * (1.0 - radial_fraction)),
        (polar_lower_index, radial_lower_index + 1, (1.0 - polar_fraction) * radial_fraction),
        (polar_upper_index, radial_lower_index + 1, polar_fraction * radial_fraction),
    ]


def sample_block(table, corners, l_first, k_first):
    nl, nk = table.shape
    flat = table.reshape(-1)
    total = jnp.zeros(corners[0][2].shape, table.dtype)
    for lidx, kidx, weight in corners:
        lloc = lidx - l_first
        kloc = kidx - k_first
        valid = (lloc >= 0) & (lloc < nl) & (kloc >= 0) & (kloc < nk)
        spot = jnp.clip(lloc, 0, nl - 1) * nk + jnp.clip(kloc, 0, nk - 1)
        total = total + jnp.where(valid, weight * jnp.take(flat, spot), 0.0)
    return total


def body(density, velocity, shifts, fractions):
    cycle = lax.axis_size("phi")
    bands = lax.axis_size("row")
    cells = density.shape[0]
    radial = density.shape[2]
    nphi = cells * cycle
    nrad = radial * bands
    prim = jnp.concatenate([density[None], velocity], axis=0)
    shift_col = jnp.repeat(shifts, BAND)
    frac_col = jnp.repeat(fractions, BAND)
    whole = shift_col // cells
    remain = shift_col % cells
    levels = (cycle // 4 - 1).bit_length()
    for step in range(STEPS):
        ext_phi = padded(prim, (("phi", 1),), 1, True)
        ext_radial = padded(prim, (("row", 3),), 1, False)
        padded_polar_grid = jnp.pad(prim, ((0, 0), (0, 0), (1, 1), (0, 0)))
        prim = advance(prim, ext_phi, padded_polar_grid, ext_radial)
        for level in range(levels):
            moved = passed_along(prim, "phi", 2**level)
            taken = whole // 2**level % 2 == 1
            prim = jnp.where(taken[None, None, None, :], moved, prim)
        left = passed_along(prim, "phi", 1)
        joined = jnp.concatenate([left, prim], axis=1)
        lead = lax.slice_in_dim(joined, cells, 2 * cells, axis=1)
        trail = lax.slice_in_dim(joined, cells - 1, 2 * cells - 1, axis=1)
        for offset in range(1, cells):
            picked = (remain == offset)[None, None, None, :]
            lead = jnp.where(
                picked, lax.slice_in_dim(joined, cells - offset, 2 * cells - offset, axis=1), lead
            )
            trail = jnp.where(
                picked,
                lax.slice_in_dim(joined, cells - offset - 1, 2 * cells - offset - 1, axis=1),
                trail,
            )
        prim = (1.0 - frac_col) * lead + frac_col * trail
    radial_index = lax.axis_index("row") * radial + jnp.arange(radial, dtype=jnp.int32)
    intensity = column_light(prim[0], radial_index, nrad)
    rows_dev = NPIX // (cycle * bands)
    first_row = (lax.axis_index("phi") * bands + lax.axis_index("row")) * rows_dev
    pixel_rows = first_row + jnp.arange(rows_dev, dtype=jnp.int32)
    table = lax.all_gather(intensity, "row", axis=1, tiled=True)
    table = lax.all_gather(table, "phi", axis=0, tiled=True)
    image = sample_block(table, pixel_corners(pixel_rows, NPIX, nphi, nrad), 0, 0)
    return (prim[0], prim[1:], image)


def solution(mesh):
    in_specs = (P("phi", None, "row"), P(None, "phi", None, "row"), P("row"), P("row"))
    out_specs = (P("phi", None, "row"), P(None, "phi", None, "row"), P(("phi", "row"), None))
    return jax.shard_map(body, mesh=mesh, in_specs=in_specs, out_specs=out_specs, check_vma=False)
```

profile of v0, /device:TPU:0, one launch (start us, length us, event | category | flops | bytes accessed | tf_op | source)
XLA Modules:
  0.0 935.0 jit_solution(6371216492219314542)
XLA Ops:
  0.6 1.6 copy.28
  2.3 1.0 fusion.76
  3.6 1.1 copy.36
  4.7 1.3 collective-permute-start.3
  6.0 1.1 copy.35
  7.1 3.6 collective-permute-start.2
  10.7 0.7 fusion.103
  11.5 6.0 collective-permute-start.1
  19.3 1.2 fusion.19
  20.5 1.2 fusion.99
  22.5 0.7 copy.49
  23.2 1.3 copy.38
  24.5 1.3 copy.37
  25.8 0.9 pad_maximum_fusion.2
  27.8 1.1 fusion.4
  28.9 1.1 pad_maximum_fusion.6
  31.0 0.7 copy-done
  33.4 0.7 broadcast_clamp_fusion
  34.0 26.6 %collective-permute-done.4 = f32[4,16,32,128]{3,1,2,0:T(8,128)S(1)} collective-permute-done((f32[4,16,32,128]{3,1,2,0:T(8,128)S(1)}, f32[4,16,32,128]{3,1,2,0:T(8,128)S(1)}, u32[]{:S(2)}, u32[]{:S(2)}) %collective-permute-start.4) | collective-permute-done | bytes 1048608 | tf_op jit(solution)/shard_map/ppermute | solution.py:37
  61.0 0.7 broadcast_clamp_fusion.1
  61.7 26.5 %collective-permute-done.5 = f32[4,16,32,128]{3,1,2,0:T(8,128)S(1)} collective-permute-done((f32[4,16,32,128]{3,1,2,0:T(8,128)S(1)}, f32[4,16,32,128]{3,1,2,0:T(8,128)S(1)}, u32[]{:S(2)}, u32[]{:S(2)}) %collective-permute-start.5) | collective-permute-done | bytes 1048608 | tf_op jit(solution)/shard_map/ppermute | solution.py:37
  88.3 3.5 multiply_add_fusion.1
  92.2 1.0 fusion.80
  93.3 0.7 fusion.112
  94.5 1.3 collective-permute-start.9
  95.8 1.1 copy.39
  96.9 3.6 collective-permute-start.8
  100.5 1.4 broadcast_multiply_fusion.4
  102.3 0.9 fusion.111
  103.2 2.0 collective-permute-start.6
  105.2 1.3 copy.42
  106.5 2.2 copy.41
  108.7 2.1 pad_maximum_fusion.4
  111.9 1.1 fusion.1
  113.0 1.1 pad_maximum_fusion.8
  116.6 0.7 copy-done.8
  117.5 25.6 %collective-permute-done.10 = f32[4,16,32,128]{3,1,2,0:T(8,128)S(1)} collective-permute-done((f32[4,16,32,128]{3,1,2,0:T(8,128)S(1)}, f32[4,16,32,128]{3,1,2,0:T(8,128)S(1)}, u32[]{:S(2)}, u32[]{:S(2)}) %collective-permute-start.10) | collective-permute-done | bytes 1048608 | tf_op jit(solution)/shard_map/ppermute | solution.py:37
  143.6 25.6 %collective-permute-done.11 = f32[4,16,32,128]{3,1,2,0:T(8,128)S(1)} collective-permute-done((f32[4,16,32,128]{3,1,2,0:T(8,128)S(1)}, f32[4,16,32,128]{3,1,2,0:T(8,128)S(1)}, u32[]{:S(2)}, u32[]{:S(2)}) %collective-permute-start.11) | collective-permute-done | bytes 1048608 | tf_op jit(solution)/shard_map/ppermute | solution.py:37
  169.4 3.5 multiply_add_fusion
  173.0 0.8 copy.43
  173.8 1.1 copy.44
  175.0 5.2 all_gather.6
  180.2 30.7 %all_gather.7 = f32[128,512]{1,0:T(8,128)S(1)} all-gather(f32[16,512]{1,0:T(8,128)S(1)} %all_gather.6), channel_id=1, replica_groups=mesh['phi'=8,'row'=4] {'phi'}, dimensions={0}, use_global_device_ids=true | all-gather | bytes 294912 | tf_op jit(solution)/shard_map/all_gather | solution.py:160
  211.0 180.5 %gather_fusion.3 = f32[32768]{0:T(1024)S(1)} fusion(f32[65536]{0:T(1024)S(1)} %bitcast.59, s32[32768]{0:T(1024)S(1)} %copy-done.9), kind=kCustom, calls=%fused_computation.3.clone | custom fusion | bytes 393216 | tf_op jit(solution)/shard_map/jit(_take)/gather | solution.py:113
  391.6 180.5 %gather_fusion.2 = f32[32768]{0:T(1024)S(1)} fusion(f32[65536]{0:T(1024)S(1)} %bitcast.60, s32[32768]{0:T(1024)S(1)} %copy-done.10), kind=kCustom, calls=%fused_computation.2.clone | custom fusion | bytes 393216 | tf_op jit(solution)/shard_map/jit(_take)/gather | solution.py:113
  572.2 180.5 %gather_fusion.1 = f32[32768]{0:T(1024)S(1)} fusion(f32[65536]{0:T(1024)S(1)} %bitcast.61, s32[32768]{0:T(1024)S(1)} %broadcast_clamp_fusion.2), kind=kCustom, calls=%fused_computation.1.clone | custom fusion | bytes 393216 | tf_op jit(solution)/shard_map/jit(_take)/gather | solution.py:113
  752.8 180.5 %gather_fusion = f32[32768]{0:T(1024)S(1)} fusion(f32[65536]{0:T(1024)S(1)} %bitcast.62, s32[32768]{0:T(1024)S(1)} %broadcast_clamp_fusion.3), kind=kCustom, calls=%fused_computation.clone | custom fusion | bytes 393216 | tf_op jit(solution)/shard_map/jit(_take)/gather | solution.py:113
  933.5 1.5 fusion.85
  (172 shorter events, 12.4 us)
Async XLA Ops:
  4.7 18.5 %collective-permute-start.3 = (f32[4,16,32,1]{2,1,3,0:T(8,128)}, f32[4,16,32,1]{2,1,3,0:T(8,128)}, u32[]{:S(2)}, u32[]{:S(2)}) collective-permute-start(f32[4,16,32,1]{2,1,3,0:T(8,128)} %copy.36), channel_id=1, source_target_pairs={{1,0},{2,1},{3,2},{5,4},{6,5},{7,6},{9,8},{10,9},{11,10},{13,12},{... | collective-permute-start | bytes 24584 | tf_op jit(solution)/shard_map/ppermute | solution.py:27
  7.1 17.4 %collective-permute-start.2 = (f32[4,16,32,1]{2,1,3,0:T(8,128)}, f32[4,16,32,1]{2,1,3,0:T(8,128)}, u32[]{:S(2)}, u32[]{:S(2)}) collective-permute-start(f32[4,16,32,1]{2,1,3,0:T(8,128)} %copy.35), channel_id=1, source_target_pairs={{0,1},{1,2},{2,3},{4,5},{5,6},{6,7},{8,9},{9,10},{10,11},{12,13},{... | collective-permute-start | bytes 24584 | tf_op jit(solution)/shard_map/ppermute | solution.py:25
  11.5 17.4 %collective-permute-start.1 = (f32[4,1,32,128]{3,1,2,0:T(1,128)}, f32[4,1,32,128]{3,1,2,0:T(1,128)}, u32[]{:S(2)}, u32[]{:S(2)}) collective-permute-start(f32[4,1,32,128]{3,1,2,0:T(1,128)} %get-tuple-element.144), channel_id=1, source_target_pairs={{4,0},{8,4},{12,8},{16,12},{20,16},{24,20},{28,24},{0,28},{5,1},{9... | collective-permute-start | bytes 196616 | tf_op jit(solution)/shard_map/ppermute | solution.py:27
  17.5 11.5 %collective-permute-start = (f32[4,1,32,128]{3,1,2,0:T(1,128)}, f32[4,1,32,128]{3,1,2,0:T(1,128)}, u32[]{:S(2)}, u32[]{:S(2)}) collective-permute-start(f32[4,1,32,128]{3,1,2,0:T(1,128)} %get-tuple-element.143), channel_id=1, source_target_pairs={{0,4},{4,8},{8,12},{12,16},{16,20},{20,24},{24,28},{28,0},{1,5},{5... | collective-permute-start | bytes 196616 | tf_op jit(solution)/shard_map/ppermute | solution.py:25
  17.6 2.9 copy-start.12
  19.3 3.0 copy-start.51
  32.6 28.1 %collective-permute-start.4 = (f32[4,16,32,128]{3,1,2,0:T(8,128)S(1)}, f32[4,16,32,128]{3,1,2,0:T(8,128)S(1)}, u32[]{:S(2)}, u32[]{:S(2)}) collective-permute-start(f32[4,16,32,128]{3,1,2,0:T(8,128)S(1)} %pad_maximum_fusion.14), channel_id=1, source_target_pairs={{0,4},{4,8},{8,12},{12,16},{16,20},{20,24},{24,28},{28,0},{1,5},{5... | collective-permute-start | bytes 3145736 | tf_op jit(solution)/shard_map/ppermute | solution.py:37
  33.1 55.1 %copy-start.16 = (pred[128]{0:T(512)(128)(4,1)}, pred[128]{0:T(512)(128)(4,1)S(1)}, u32[]{:S(2)}) copy-start(pred[128]{0:T(512)(128)(4,1)S(1)} %get-tuple-element.158) | copy-start | bytes 388
  33.2 55.1 %copy-start.18 = (pred[128]{0:T(512)(128)(4,1)}, pred[128]{0:T(512)(128)(4,1)S(1)}, u32[]{:S(2)}) copy-start(pred[128]{0:T(512)(128)(4,1)S(1)} %get-tuple-element.159) | copy-start | bytes 388
  33.2 55.1 %copy-start.20 = (pred[128]{0:T(512)(128)(4,1)}, pred[128]{0:T(512)(128)(4,1)S(1)}, u32[]{:S(2)}) copy-start(pred[128]{0:T(512)(128)(4,1)S(1)} %get-tuple-element.160) | copy-start | bytes 388
  33.2 55.1 %copy-start.22 = (pred[128]{0:T(512)(128)(4,1)}, pred[128]{0:T(512)(128)(4,1)S(1)}, u32[]{:S(2)}) copy-start(pred[128]{0:T(512)(128)(4,1)S(1)} %get-tuple-element.161) | copy-start | bytes 388
  33.2 55.1 %copy-start.24 = (pred[128]{0:T(512)(128)(4,1)}, pred[128]{0:T(512)(128)(4,1)S(1)}, u32[]{:S(2)}) copy-start(pred[128]{0:T(512)(128)(4,1)S(1)} %get-tuple-element.162) | copy-start | bytes 388
  33.2 55.1 %copy-start.26 = (pred[128]{0:T(512)(128)(4,1)}, pred[128]{0:T(512)(128)(4,1)S(1)}, u32[]{:S(2)}) copy-start(pred[128]{0:T(512)(128)(4,1)S(1)} %get-tuple-element.163) | copy-start | bytes 388
  33.2 55.1 %copy-start.28 = (pred[128]{0:T(512)(128)(4,1)}, pred[128]{0:T(512)(128)(4,1)S(1)}, u32[]{:S(2)}) copy-start(pred[128]{0:T(512)(128)(4,1)S(1)} %get-tuple-element.164) | copy-start | bytes 388
  33.2 55.1 %copy-start.30 = (pred[128]{0:T(512)(128)(4,1)}, pred[128]{0:T(512)(128)(4,1)S(1)}, u32[]{:S(2)}) copy-start(pred[128]{0:T(512)(128)(4,1)S(1)} %get-tuple-element.165) | copy-start | bytes 388
  33.2 55.1 %copy-start.32 = (pred[128]{0:T(512)(128)(4,1)}, pred[128]{0:T(512)(128)(4,1)S(1)}, u32[]{:S(2)}) copy-start(pred[128]{0:T(512)(128)(4,1)S(1)} %get-tuple-element.166) | copy-start | bytes 388
  33.2 55.1 %copy-start.34 = (pred[128]{0:T(512)(128)(4,1)}, pred[128]{0:T(512)(128)(4,1)S(1)}, u32[]{:S(2)}) copy-start(pred[128]{0:T(512)(128)(4,1)S(1)} %get-tuple-element.167) | copy-start | bytes 388
  33.2 55.1 %copy-start.36 = (pred[128]{0:T(512)(128)(4,1)}, pred[128]{0:T(512)(128)(4,1)S(1)}, u32[]{:S(2)}) copy-start(pred[128]{0:T(512)(128)(4,1)S(1)} %get-tuple-element.168) | copy-start | bytes 388
  33.3 55.1 %copy-start.38 = (pred[128]{0:T(512)(128)(4,1)}, pred[128]{0:T(512)(128)(4,1)S(1)}, u32[]{:S(2)}) copy-start(pred[128]{0:T(512)(128)(4,1)S(1)} %get-tuple-element.169) | copy-start | bytes 388
  33.3 55.1 %copy-start.40 = (pred[128]{0:T(512)(128)(4,1)}, pred[128]{0:T(512)(128)(4,1)S(1)}, u32[]{:S(2)}) copy-start(pred[128]{0:T(512)(128)(4,1)S(1)} %get-tuple-element.170) | copy-start | bytes 388
  60.8 27.5 %collective-permute-start.5 = (f32[4,16,32,128]{3,1,2,0:T(8,128)S(1)}, f32[4,16,32,128]{3,1,2,0:T(8,128)S(1)}, u32[]{:S(2)}, u32[]{:S(2)}) collective-permute-start(f32[4,16,32,128]{3,1,2,0:T(8,128)S(1)} %broadcast_select_fusion.1), channel_id=1, source_target_pairs={{0,4},{4,8},{8,12},{12,16},{16,20},{20,24},{24,28},{28,0},{1,5},{5... | collective-permute-start | bytes 3145736 | tf_op jit(solution)/shard_map/ppermute | solution.py:37
  61.0 27.3 %copy-start.48 = (f32[128]{0:T(128)}, f32[128]{0:T(128)S(1)}, u32[]{:S(2)}) copy-start(f32[128]{0:T(128)S(1)} %broadcast_subtract_fusion) | copy-start | bytes 1540
  94.5 10.7 %collective-permute-start.9 = (f32[4,16,32,1]{2,1,3,0:T(8,128)S(1)}, f32[4,16,32,1]{2,1,3,0:T(8,128)}, u32[]{:S(2)}, u32[]{:S(2)}) collective-permute-start(f32[4,16,32,1]{2,1,3,0:T(8,128)S(1)} %copy.40), channel_id=1, source_target_pairs={{1,0},{2,1},{3,2},{5,4},{6,5},{7,6},{9,8},{10,9},{11,10},{13,12},{... | collective-permute-start | bytes 24584 | tf_op jit(solution)/shard_map/ppermute | solution.py:27
  96.9 9.6 %collective-permute-start.8 = (f32[4,16,32,1]{2,1,3,0:T(8,128)}, f32[4,16,32,1]{2,1,3,0:T(8,128)}, u32[]{:S(2)}, u32[]{:S(2)}) collective-permute-start(f32[4,16,32,1]{2,1,3,0:T(8,128)} %copy.39), channel_id=1, source_target_pairs={{0,1},{1,2},{2,3},{4,5},{5,6},{6,7},{8,9},{9,10},{10,11},{12,13},{... | collective-permute-start | bytes 24584 | tf_op jit(solution)/shard_map/ppermute | solution.py:25
  102.0 11.0 %collective-permute-start.7 = (f32[4,1,32,128]{3,1,2,0:T(1,128)}, f32[4,1,32,128]{3,1,2,0:T(1,128)S(1)}, u32[]{:S(2)}, u32[]{:S(2)}) collective-permute-start(f32[4,1,32,128]{3,1,2,0:T(1,128)} %get-tuple-element.128), channel_id=1, source_target_pairs={{4,0},{8,4},{12,8},{16,12},{20,16},{24,20},{28,24},{0,28},{5,1},{9... | collective-permute-start | bytes 196616 | tf_op jit(solution)/shard_map/ppermute | solution.py:27
  103.2 9.8 %collective-permute-start.6 = (f32[4,1,32,128]{3,1,2,0:T(1,128)}, f32[4,1,32,128]{3,1,2,0:T(1,128)}, u32[]{:S(2)}, u32[]{:S(2)}) collective-permute-start(f32[4,1,32,128]{3,1,2,0:T(1,128)} %get-tuple-element.127), channel_id=1, source_target_pairs={{0,4},{4,8},{8,12},{12,16},{16,20},{20,24},{24,28},{28,0},{1,5},{5... | collective-permute-start | bytes 196616 | tf_op jit(solution)/shard_map/ppermute | solution.py:25
  116.4 26.7 %collective-permute-start.10 = (f32[4,16,32,128]{3,1,2,0:T(8,128)S(1)}, f32[4,16,32,128]{3,1,2,0:T(8,128)S(1)}, u32[]{:S(2)}, u32[]{:S(2)}) collective-permute-start(f32[4,16,32,128]{3,1,2,0:T(8,128)S(1)} %pad_maximum_fusion.15), channel_id=1, source_target_pairs={{0,4},{4,8},{8,12},{12,16},{16,20},{20,24},{24,28},{28,0},{1,5},{5... | collective-permute-start | bytes 3145736 | tf_op jit(solution)/shard_map/ppermute | solution.py:37
  117.4 51.9 %copy-start.17 = (pred[128]{0:T(512)(128)(4,1)S(1)}, pred[128]{0:T(512)(128)(4,1)}, u32[]{:S(2)}) copy-start(pred[128]{0:T(512)(128)(4,1)} %copy-done.16) | copy-start | bytes 388
  117.4 51.9 %copy-start.19 = (pred[128]{0:T(512)(128)(4,1)S(1)}, pred[128]{0:T(512)(128)(4,1)}, u32[]{:S(2)}) copy-start(pred[128]{0:T(512)(128)(4,1)} %copy-done.18) | copy-start | bytes 388
  117.4 51.9 %copy-start.21 = (pred[128]{0:T(512)(128)(4,1)S(1)}, pred[128]{0:T(512)(128)(4,1)}, u32[]{:S(2)}) copy-start(pred[128]{0:T(512)(128)(4,1)} %copy-done.20) | copy-start | bytes 388
  117.4 51.9 %copy-start.23 = (pred[128]{0:T(512)(128)(4,1)S(1)}, pred[128]{0:T(512)(128)(4,1)}, u32[]{:S(2)}) copy-start(pred[128]{0:T(512)(128)(4,1)} %copy-done.22) | copy-start | bytes 388
  117.4 51.9 %copy-start.25 = (pred[128]{0:T(512)(128)(4,1)S(1)}, pred[128]{0:T(512)(128)(4,1)}, u32[]{:S(2)}) copy-start(pred[128]{0:T(512)(128)(4,1)} %copy-done.24) | copy-start | bytes 388
  117.4 51.9 %copy-start.27 = (pred[128]{0:T(512)(128)(4,1)S(1)}, pred[128]{0:T(512)(128)(4,1)}, u32[]{:S(2)}) copy-start(pred[128]{0:T(512)(128)(4,1)} %copy-done.26) | copy-start | bytes 388
  117.4 51.9 %copy-start.29 = (pred[128]{0:T(512)(128)(4,1)S(1)}, pred[128]{0:T(512)(128)(4,1)}, u32[]{:S(2)}) copy-start(pred[128]{0:T(512)(128)(4,1)} %copy-done.28) | copy-start | bytes 388
  117.4 51.9 %copy-start.31 = (pred[128]{0:T(512)(128)(4,1)S(1)}, pred[128]{0:T(512)(128)(4,1)}, u32[]{:S(2)}) copy-start(pred[128]{0:T(512)(128)(4,1)} %copy-done.30) | copy-start | bytes 388
  117.5 51.9 %copy-start.33 = (pred[128]{0:T(512)(128)(4,1)S(1)}, pred[128]{0:T(512)(128)(4,1)}, u32[]{:S(2)}) copy-start(pred[128]{0:T(512)(128)(4,1)} %copy-done.32) | copy-start | bytes 388
  117.5 51.9 %copy-start.35 = (pred[128]{0:T(512)(128)(4,1)S(1)}, pred[128]{0:T(512)(128)(4,1)}, u32[]{:S(2)}) copy-start(pred[128]{0:T(512)(128)(4,1)} %copy-done.34) | copy-start | bytes 388
  117.5 51.9 %copy-start.37 = (pred[128]{0:T(512)(128)(4,1)S(1)}, pred[128]{0:T(512)(128)(4,1)}, u32[]{:S(2)}) copy-start(pred[128]{0:T(512)(128)(4,1)} %copy-done.36) | copy-start | bytes 388
  117.5 51.9 %copy-start.39 = (pred[128]{0:T(512)(128)(4,1)S(1)}, pred[128]{0:T(512)(128)(4,1)}, u32[]{:S(2)}) copy-start(pred[128]{0:T(512)(128)(4,1)} %copy-done.38) | copy-start | bytes 388
  117.5 51.9 %copy-start.41 = (pred[128]{0:T(512)(128)(4,1)S(1)}, pred[128]{0:T(512)(128)(4,1)}, u32[]{:S(2)}) copy-start(pred[128]{0:T(512)(128)(4,1)} %copy-done.40) | copy-start | bytes 388
  117.5 51.9 %copy-start.49 = (f32[128]{0:T(128)S(1)}, f32[128]{0:T(128)}, u32[]{:S(2)}) copy-start(f32[128]{0:T(128)} %copy-done.48) | copy-start | bytes 1540
  143.3 26.0 %collective-permute-start.11 = (f32[4,16,32,128]{3,1,2,0:T(8,128)S(1)}, f32[4,16,32,128]{3,1,2,0:T(8,128)S(1)}, u32[]{:S(2)}, u32[]{:S(2)}) collective-permute-start(f32[4,16,32,128]{3,1,2,0:T(8,128)S(1)} %broadcast_select_fusion), channel_id=1, source_target_pairs={{0,4},{4,8},{8,12},{12,16},{16,20},{20,24},{24,28},{28,0},{1,5},{5... | collective-permute-start | bytes 3145736 | tf_op jit(solution)/shard_map/ppermute | solution.py:37
  173.0 38.0 %copy-start.9 = (s32[32768]{0:T(1024)S(1)}, s32[32768]{0:T(1024)}, u32[]{:S(2)}) copy-start(s32[32768]{0:T(1024)} %broadcast_clamp_fusion) | copy-start | bytes 393220
  211.0 180.6 %copy-start.10 = (s32[32768]{0:T(1024)S(1)}, s32[32768]{0:T(1024)}, u32[]{:S(2)}) copy-start(s32[32768]{0:T(1024)} %broadcast_clamp_fusion.1) | copy-start | bytes 393220
  752.8 180.6 %copy-start.13 = (f32[1024]{0:T(1024)S(1)}, f32[1024]{0:T(1024)}, u32[]{:S(2)}) copy-start(f32[1024]{0:T(1024)} %copy-done.12) | copy-start | bytes 12292
  752.8 180.6 %copy-start.15 = (f32[1024]{0:T(1024)S(1)}, f32[1024]{0:T(1024)}, u32[]{:S(2)}) copy-start(f32[1024]{0:T(1024)} %copy-done.14) | copy-start | bytes 12292
  752.8 180.6 %copy-start.45 = (f32[32]{0:T(128)S(1)}, f32[32]{0:T(128)}, u32[]{:S(2)}) copy-start(f32[32]{0:T(128)} %copy-done.44) | copy-start | bytes 388
  752.8 180.6 %copy-start.47 = (f32[32]{0:T(128)S(1)}, f32[32]{0:T(128)}, u32[]{:S(2)}) copy-start(f32[32]{0:T(128)} %copy-done.46) | copy-start | bytes 388
  (16 other events, 20.4 us)
where the time goes:
time: 936 us; the launch traced here: 935 us
  local copies, waits for them, and re-layouts  742 us (79%)
  waiting for transfers between devices  104 us (11%)
  blocking collectives  35.9 us (4%)
  other arithmetic  32.3 us (3%)
  starting transfers between devices  18.5 us (2%)
    gather x8, local copies, waits for them, and re-layouts, sample_block(): total = total + jnp.where(valid, weight * jnp.take(flat, spot), 0.0)  722 us
    ppermute x4, waiting for transfers between devices, passed_along(): return lax.ppermute(value, axis, pairs)  104 us
    all_gather x1, blocking collectives, body(): table = lax.all_gather(table, 'phi', axis=0, tiled=True)  30.7 us
  transfers between devices with their start and end apart: 12, of which 4 were waited for; matrix products, arithmetic and copies ran while one was open for 3% of the time, Pallas kernels for 0%

commit v1 on v0

v1 whole, which is shorter than its diff:
```python
import functools

import jax
import jax.numpy as jnp
import numpy as np
from jax import lax
from jax.experimental import pallas as pl
from jax.experimental.pallas import tpu as pltpu
from jax.sharding import PartitionSpec as P

BAND = 8
STEPS = 2
NPIX = 1024


SPEED = 1.5
COURANT = 0.05
KAPPA = 1.5
R_INNER = 0.2

FIELDS = 4
INNER = 8
HALO = STEPS
LANES = 128
VMEM_LIMIT = 48 * 1024 * 1024


def params():
    return pltpu.CompilerParams(vmem_limit_bytes=VMEM_LIMIT)


def vmem(count):
    return [pl.BlockSpec(memory_space=pltpu.VMEM)] * count


def smem(count):
    return [pl.BlockSpec(memory_space=pltpu.SMEM)] * count


def field_ref(density_ref, velocity_ref, field):
    return density_ref if field == 0 else velocity_ref.at[field - 1]


def pack_kernel(density_ref, velocity_ref, rows_ref):
    cells, polar, radial = density_ref.shape
    groups = polar // INNER
    for field in range(FIELDS):
        source = field_ref(density_ref, velocity_ref, field)
        for group in range(groups):
            block = source[:, pl.ds(group, INNER, stride=groups), :]
            turned = block.reshape(cells * INNER, radial).T
            rows_ref[pl.ds(field * groups + group, radial, stride=FIELDS * groups), :] = turned


def unpack_kernel(rows_ref, density_ref, velocity_ref):
    cells, polar, radial = density_ref.shape
    groups = polar // INNER
    for field in range(FIELDS):
        target = field_ref(density_ref, velocity_ref, field)
        for group in range(groups):
            turned = rows_ref[pl.ds(field * groups + group, radial, stride=FIELDS * groups), :]
            block = turned.T.reshape(cells, INNER, radial)
            target[:, pl.ds(group, INNER, stride=groups), :] = block


def evolve_kernel(cells, cycle, columns, nrad, groups, swap, shift_ref, frac_ref, place_ref, tilt_ref, in_ref, out_ref, light_ref, work_ref, lit_ref):
    extended = columns + 2 * HALO
    per_column = FIELDS * groups
    first = place_ref[0]
    first_global = place_ref[1]
    lane = lax.broadcasted_iota(jnp.int32, (cycle, LANES), 1)
    inner = lane % INNER

    def upper_azimuth(x):
        z = pltpu.roll(x, LANES - INNER, 1)
        return jnp.where(lane < LANES - INNER, z, pltpu.roll(z, cycle - 1, 0))

    def lower_azimuth(x):
        z = pltpu.roll(x, INNER, 1)
        return jnp.where(lane >= INNER, z, pltpu.roll(z, 1, 0))

    def upper_polar(x):
        last = jnp.where(inner == INNER - 1, 0.0, pltpu.roll(x[0], LANES - 1, 1))
        return x[1:] + [last]

    def lower_polar(x):
        head = jnp.where(inner == 0, 0.0, pltpu.roll(x[-1], 1, 1))
        return [head] + x[:-1]

    def conserved(prim):
        return [prim[0]] + [[r * v for r, v in zip(prim[0], prim[k])] for k in (1, 2, 3)]

    half = 0.5 * COURANT
    damp = 0.5 * SPEED * COURANT

    def face_part(cons, speed, comp, sign):
        factor = [half * u + sign * damp for u in speed]
        parts = [[c * m for c, m in zip(cons[k], factor)] for k in range(FIELDS)]
        parts[comp] = [p + half * r for p, r in zip(parts[comp], cons[0])]
        return parts

    def contributions(prim):
        cons = conserved(prim)
        a_phi = face_part(cons, prim[2], 2, -1.0)
        b_phi = face_part(cons, prim[2], 2, 1.0)
        a_th = face_part(cons, prim[3], 3, -1.0)
        b_th = face_part(cons, prim[3], 3, 1.0)
        keep = 1.0 - 3.0 * SPEED * COURANT
        pend = []
        for k in range(FIELDS):
            up_t = upper_polar(a_th[k])
            low_t = lower_polar(b_th[k])
            pend.append([
                keep * cons[k][g] - (upper_azimuth(a_phi[k][g]) - lower_azimuth(b_phi[k][g])) - (up_t[g] - low_t[g])
                for g in range(groups)
            ])
        return pend, face_part(cons, prim[1], 1, -1.0), face_part(cons, prim[1], 1, 1.0)

    def combine(x, y, sign):
        return [[p + sign * q for p, q in zip(a, b)] for a, b in zip(x, y)]

    def finish(fresh, col):
        number = first_global + col - HALO
        valid = (number >= 0) & (number < nrad)
        band = (first + col - HALO + BAND) // BAND
        shift = shift_ref[band]
        weight = frac_ref[band]
        turn = shift // cells
        step = INNER * (shift % cells)
        inside = lane >= step
        inverse = [1.0 / r for r in fresh[0]]
        prim = [fresh[0]] + [[m * i for m, i in zip(fresh[k], inverse)] for k in (1, 2, 3)]
        moved = []
        for k in range(FIELDS):
            row = []
            for x in prim[k]:
                x = jnp.where(valid, x, 0.0)
                x = (1.0 - weight) * x + weight * lower_azimuth(x)
                z = pltpu.roll(x, step, 1)
                z = jnp.where(inside, z, pltpu.roll(z, 1, 0))
                row.append(pltpu.roll(z, turn, 0))
            moved.append(row)
        return moved

    def step_columns(read, write, low, high):
        prim = read(low)
        before = face_part(conserved(prim), prim[1], 1, 1.0)
        pend, _, after = contributions(read(low + 1))
        pend = combine(pend, before, 1.0)

        def body(col, carry):
            pend, before = carry
            fresh_pend, a_rad, b_rad = contributions(read(col))
            write(col - 1, finish(combine(pend, a_rad, -1.0), col - 1))
            return combine(fresh_pend, before, 1.0), b_rad

        pend, _ = lax.fori_loop(low + 2, high - 1, body, (pend, after))
        prim = read(high - 1)
        a_rad = face_part(conserved(prim), prim[1], 1, -1.0)
        write(high - 2, finish(combine(pend, a_rad, -1.0), high - 2))

    def read_input(col):
        return [
            [in_ref[pl.ds(col * per_column + k * groups + g, cycle, stride=extended * per_column), :] for g in range(groups)]
            for k in range(FIELDS)
        ]

    def read_work(col):
        return [[work_ref[col * per_column + k * groups + g] for g in range(groups)] for k in range(FIELDS)]

    def write_work(col, prim):
        for k in range(FIELDS):
            for g in range(groups):
                work_ref[col * per_column + k * groups + g] = prim[k][g]

    def write_output(col, prim):
        own = col - HALO
        for k in range(FIELDS):
            for g in range(groups):
                out_ref[pl.ds(own * per_column + k * groups + g, cycle, stride=columns * per_column), :] = prim[k][g]
        dtau = [(KAPPA / (groups * INNER)) * r for r in prim[0]]
        total = dtau[0]
        for d in dtau[1:]:
            total = total + d
        run = total
        for d in (1, 2, 4):
            run = run + jnp.where(inner >= d, pltpu.roll(run, d, 1), 0.0)
        above = run - total
        light = jnp.zeros_like(total)
        for g in range(groups):
            light = light + tilt_ref[pl.ds(g, 1), :] * (1.0 - jnp.exp(-dtau[g])) * jnp.exp(-above)
            above = above + dtau[g]
        for d in (1, 2, 4):
            light = light + pltpu.roll(light, LANES - d, 1)
        number = jnp.full((cycle, LANES), first_global + own, jnp.int32).astype(jnp.float32)
        radius = R_INNER + (number + 0.5) * (1.0 - R_INNER) / nrad
        light = light * (1.0 / jnp.sqrt(radius))
        slot = own % INNER
        light = pltpu.roll(light, slot, 1)
        lit_ref[own // INNER] = jnp.where(inner == slot, light, lit_ref[own // INNER])

    lit_ref[...] = jnp.zeros_like(lit_ref)
    step_columns(read_input, write_work, 0, extended)
    step_columns(read_work, write_output, 1, extended - 1)
    if swap:
        sub = lax.broadcasted_iota(jnp.int32, (cycle, LANES), 0)
        for h in range(columns // INNER):
            x = lit_ref[h]
            for d in (1, 2, 4):
                low_sub = (sub & d) == 0
                low_lane = (lane & d) == 0
                ahead = pltpu.roll(pltpu.roll(x, cycle - d, 0), d, 1)
                back = pltpu.roll(pltpu.roll(x, d, 0), LANES - d, 1)
                x = jnp.where(low_sub == low_lane, x, jnp.where(low_sub, ahead, back))
            light_ref[pl.ds(h * INNER, INNER), :] = x
    else:
        light_ref[...] = lit_ref[...]


def pixel_tiles(first_row, rows_dev, npix, nphi, nrad):
    tile_rows = min(8, rows_dev)
    tile_cols = LANES // tile_rows
    across = npix // tile_cols
    tiles = rows_dev // tile_rows * across
    tile = lax.broadcasted_iota(jnp.int32, (tiles, LANES), 0)
    pixel = lax.broadcasted_iota(jnp.int32, (tiles, LANES), 1)
    row = first_row + tile // across * tile_rows + pixel // tile_cols
    col = tile % across * tile_cols + pixel % tile_cols
    yy = (row.astype(jnp.float32) + 0.5) / npix * 2.0 - 1.0
    xx = (col.astype(jnp.float32) + 0.5) / npix * 2.0 - 1.0
    dist = jnp.sqrt(xx * xx + yy * yy)
    upos = (dist - R_INNER) / (1.0 - R_INNER) * nrad - 0.5
    floor_u = jnp.floor(upos)
    frac_u = upos - floor_u
    lower = jnp.clip(floor_u.astype(jnp.int32), -2, nrad) + LANES
    angle = jnp.arctan2(yy, xx)
    vpos = (angle + jnp.pi) / (2.0 * jnp.pi) * nphi - 0.5
    window = jnp.min(lower, axis=1) // (LANES // 2)
    window = jnp.clip(window, 0, (nrad + LANES) // (LANES // 2))
    start = jnp.clip(jnp.floor(jnp.min(vpos, axis=1)).astype(jnp.int32) + 8, 0, nphi + 8)
    spot = jnp.clip(lower - window[:, None] * (LANES // 2), 0, LANES - 2)
    return start, window, spot, frac_u, vpos + 8.0 - start[:, None].astype(jnp.float32)


def window_rows(rows_dev, npix, nphi):
    tile_rows = min(8, rows_dev)
    tile_cols = LANES // tile_rows
    diagonal = 2.0 * np.hypot(tile_rows, tile_cols) / npix
    span = diagonal / (R_INNER - diagonal) / (2.0 * np.pi) * nphi
    return -(-int(np.ceil(span) + 2) // 8) * 8


def image_kernel(cells, cycle, nphi, nrad, rows, tile_rows, across, start_ref, window_ref, table_ref, spot_ref, frac_ref, vpos_ref, out_ref, turned_ref, wide_ref):
    blocks = nrad // LANES
    for k in range(blocks):
        for l in range(nphi // LANES):
            turned_ref[pl.ds(k * nphi + l * LANES, LANES), :] = table_ref[
                pl.ds(k * LANES, LANES), pl.ds(l * LANES, LANES)
            ].T
    half = LANES // 2
    windows = 2 * (blocks + 2) - 1
    tall = wide_ref.shape[0] // windows

    def fill(s, carry):
        zero = jnp.zeros((cells, LANES), jnp.float32)
        value = [zero] + [turned_ref[pl.ds(k * nphi + s, cells, stride=cycle), :] for k in range(blocks)] + [zero]
        for w in range(windows):
            piece = value[w // 2]
            if w % 2:
                piece = jnp.concatenate([piece[:, half:], value[w // 2 + 1][:, :half]], axis=1)
            wide_ref[pl.ds((8 + s * cells) * windows + w, cells, stride=windows), :] = piece
        return carry

    lax.fori_loop(0, cycle, fill, 0)
    pad = tall - nphi - 8
    wide_ref[pl.ds(0, 8 * windows), :] = wide_ref[pl.ds(nphi * windows, 8 * windows), :]
    wide_ref[pl.ds((nphi + 8) * windows, pad * windows), :] = wide_ref[pl.ds(8 * windows, pad * windows), :]

    sub = lax.broadcasted_iota(jnp.int32, (8, LANES), 0)
    lane = lax.broadcasted_iota(jnp.int32, (8, LANES), 1)

    def one_tile(tile):
        start = start_ref[tile]
        at = start * windows + window_ref[tile]
        spot = jnp.broadcast_to(spot_ref[pl.ds(tile, 1), :], (8, LANES))
        frac = jnp.broadcast_to(frac_ref[pl.ds(tile, 1), :], (8, LANES))
        vpos = jnp.broadcast_to(vpos_ref[pl.ds(tile, 1), :], (8, LANES))
        total = None
        for r in range(0, rows, 8):
            block = wide_ref[pl.ds(at + r * windows, 8, stride=windows), :]
            low = jnp.take_along_axis(block, spot, axis=1)
            high = jnp.take_along_axis(block, spot + 1, axis=1)
            weight = jnp.maximum(0.0, 1.0 - jnp.abs((sub + r).astype(jnp.float32) - vpos))
            part = weight * (low + frac * (high - low))
            total = part if total is None else total + part
        for d in (4, 2, 1):
            total = total + pltpu.roll(total, d, 0)
        return total

    def group(index, carry):
        result = jnp.zeros((8, LANES), jnp.float32)
        for t in range(8):
            result = jnp.where(sub == t, one_tile(index * 8 + t), result)
        if tile_rows == 8:
            width = LANES // 8
            for d in (1, 2, 4):
                low_sub = (sub & d) == 0
                low_lane = (lane & (d * width)) == 0
                ahead = pltpu.roll(pltpu.roll(result, 8 - d, 0), d * width, 1)
                back = pltpu.roll(pltpu.roll(result, d, 0), LANES - d * width, 1)
                result = jnp.where(low_sub == low_lane, result, jnp.where(low_sub, ahead, back))
            per_row = across // 8
            out_ref[pl.ds(pl.multiple_of(index // per_row * 8, 8), 8), pl.ds(pl.multiple_of(index % per_row * LANES, LANES), LANES)] = result
        else:
            out_ref[pl.ds(pl.multiple_of(index * 8, 8), 8), :] = result
        return carry

    lax.fori_loop(0, spot_ref.shape[0] // 8, group, 0)


def draw_image(table, geometry, cells, cycle, rows_dev, npix, nphi, nrad):
    start, window, spot, frac_u, vpos = geometry
    tiles = spot.shape[0]
    tile_rows = min(8, rows_dev)
    tile_cols = LANES // tile_rows
    across = npix // tile_cols
    rows = window_rows(rows_dev, npix, nphi)
    windows = 2 * (nrad // LANES + 2) - 1
    shape = (rows_dev, npix) if tile_rows == 8 else (tiles, LANES)
    image = pl.pallas_call(
        functools.partial(image_kernel, cells, cycle, nphi, nrad, rows, tile_rows, across),
        out_shape=jax.ShapeDtypeStruct(shape, jnp.float32),
        in_specs=smem(2) + vmem(4),
        out_specs=pl.BlockSpec(memory_space=pltpu.VMEM),
        scratch_shapes=[
            pltpu.VMEM((nphi * (nrad // LANES), LANES), jnp.float32),
            pltpu.VMEM(((nphi + 16 + rows) * windows, LANES), jnp.float32),
        ],
        compiler_params=params(),
        name="image",
    )(start, window, table, spot, frac_u, vpos)
    if tile_rows == 8:
        return image
    image = image.reshape(rows_dev // tile_rows, across, tile_rows, tile_cols)
    return jnp.swapaxes(image, 1, 2).reshape(rows_dev, npix)


def body(density, velocity, shifts, fractions):
    cycle = lax.axis_size("phi")
    bands = lax.axis_size("row")
    cells, polar, radial = density.shape
    groups = polar // INNER
    per_column = FIELDS * groups
    columns = radial // cycle
    extended = columns + 2 * HALO
    nphi = cells * cycle
    nrad = radial * bands
    place = lax.axis_index("phi")
    row = lax.axis_index("row")

    rows = pl.pallas_call(
        pack_kernel,
        out_shape=jax.ShapeDtypeStruct((radial * per_column, LANES), jnp.float32),
        in_specs=vmem(2),
        out_specs=pl.BlockSpec(memory_space=pltpu.VMEM),
        compiler_params=params(),
        name="pack",
    )(density, velocity)
    edge = HALO * per_column

    def with_band(block, band):
        extra = jnp.stack([shifts[band].astype(jnp.float32), fractions[band]])
        return jnp.concatenate([block, jnp.pad(extra[:, None], ((0, 6), (0, LANES - 1)))])

    left = lax.ppermute(with_band(rows[-edge:], -1), "row", [(i, i + 1) for i in range(bands - 1)])
    right = lax.ppermute(with_band(rows[:edge], 0), "row", [(i + 1, i) for i in range(bands - 1)])
    ext_shift = jnp.concatenate([left[edge, :1].astype(jnp.int32), shifts, right[edge, :1].astype(jnp.int32)])
    ext_frac = jnp.concatenate([left[edge + 1, :1], fractions, right[edge + 1, :1]])
    rows = jnp.concatenate([left[:edge], rows, right[:edge]])
    stride = columns * per_column
    chunks = jnp.stack([rows[q * stride:q * stride + extended * per_column] for q in range(cycle)])
    ring = lax.all_to_all(chunks, "phi", 0, 0, tiled=True)

    swap = cycle == INNER and columns % INNER == 0
    slots = -(-columns // INNER)
    theta = (np.arange(polar) + 0.5) / polar
    tilt = (1.0 + 0.5 * np.cos(np.pi * theta)).reshape(INNER, groups).T
    tilt = jnp.asarray(np.tile(tilt, (1, LANES // INNER)), jnp.float32)
    where = jnp.stack([place * columns, row * radial + place * columns])
    rows, light = pl.pallas_call(
        functools.partial(evolve_kernel, cells, cycle, columns, nrad, groups, swap),
        out_shape=(
            jax.ShapeDtypeStruct((cycle * columns * per_column, LANES), jnp.float32),
            jax.ShapeDtypeStruct((columns, LANES) if swap else (slots, cycle, LANES), jnp.float32),
        ),
        in_specs=smem(3) + vmem(2),
        out_specs=tuple(vmem(2)),
        scratch_shapes=[
            pltpu.VMEM((extended * per_column, cycle, LANES), jnp.float32),
            pltpu.VMEM((slots, cycle, LANES), jnp.float32),
        ],
        compiler_params=params(),
        name="evolve",
    )(ext_shift, ext_frac, where, tilt, ring.reshape(cycle * extended * per_column, LANES))
    if not swap:
        light = light.reshape(slots, cycle, cells, INNER).transpose(0, 3, 2, 1).reshape(slots * INNER, nphi)[:columns]

    table = lax.all_gather(light, "phi", axis=0, tiled=True)
    table = lax.all_gather(table, "row", axis=0, tiled=True)
    back = lax.all_to_all(rows.reshape(cycle, columns * per_column, LANES), "phi", 0, 0, tiled=True)
    density_out, velocity_out = pl.pallas_call(
        unpack_kernel,
        out_shape=(
            jax.ShapeDtypeStruct(density.shape, jnp.float32),
            jax.ShapeDtypeStruct(velocity.shape, jnp.float32),
        ),
        in_specs=vmem(1),
        out_specs=tuple(vmem(2)),
        compiler_params=params(),
        name="unpack",
    )(back.reshape(radial * per_column, LANES))

    rows_dev = NPIX // (cycle * bands)
    first_row = (place * bands + row) * rows_dev
    geometry = pixel_tiles(first_row, rows_dev, NPIX, nphi, nrad)
    image = draw_image(table, geometry, cells, cycle, rows_dev, NPIX, nphi, nrad)
    return (density_out, velocity_out, image)


def solution(mesh):
    in_specs = (P("phi", None, "row"), P(None, "phi", None, "row"), P("row"), P("row"))
    out_specs = (P("phi", None, "row"), P(None, "phi", None, "row"), P(("phi", "row"), None))
    return jax.shard_map(body, mesh=mesh, in_specs=in_specs, out_specs=out_specs, check_vma=False)
```

time: 936 us -> 144 us (0.15)
  local copies, waits for them, and re-layouts: 742 us -> 10.1 us
  waiting for transfers between devices: 104 us -> 28.2 us
  Pallas kernels: 0 us -> 30.5 us
  other arithmetic: 32.3 us -> 5.92 us
  blocking collectives: 35.9 us -> 50.5 us
    gather x8 -> x0, local copies, waits for them, and re-layouts: 722 us -> none  [sample_block(): total = total + jnp.where(valid, weight * jnp.take(flat, spot), 0.0)]
    ppermute x12 -> x2, waiting for transfers between devices: 104 us -> 0.01 us  [the longest x1 0.01 us: body(): lax.ppermute(with_band(rows[-edge:], -1), 'row', [(i, i + 1) for i in ran...]
    pallas_call x0 -> x4, Pallas kernels: none -> 30.5 us  [the longest x1 16.1 us: body(): pl.pallas_call(functools.partial(evolve_kernel, cells, cycle, columns, nr...]
    all_to_all x0 -> x2, waiting for transfers between devices: none -> 28.2 us  [the longest x1 28.2 us: body(): ring = lax.all_to_all(chunks, 'phi', 0, 0, tiled=True)]
    ppermute x12 -> x2, starting transfers between devices: 18.5 us -> 3.63 us  [the longest x1 2.35 us: body(): lax.ppermute(with_band(rows[-edge:], -1), 'row', [(i, i + 1) for i in ran...]
    all_gather x2, blocking collectives: 35.9 us -> 50.5 us  [the longest x1 44.8 us: body(): table = lax.all_gather(light, 'phi', axis=0, tiled=True)]
    all_to_all x0 -> x2, starting transfers between devices: none -> 11 us  [the longest x1 6.77 us: body(): ring = lax.all_to_all(chunks, 'phi', 0, 0, tiled=True)]
  transfers between devices with their start and end apart: 12 -> 4, of which waited for: 4 -> 1; matrix products, arithmetic and copies ran while one was open for 3% -> 6% of each run, Pallas kernels for 0% -> 9%
where the time goes in v1:
time: 144 us; the launch traced here: 143 us
  blocking collectives  50.5 us (35%)
  Pallas kernels  30.5 us (21%)
  waiting for transfers between devices  28.2 us (20%)
  starting transfers between devices  14.6 us (10%)
  local copies, waits for them, and re-layouts  10.1 us (7%)
  other arithmetic  5.92 us (4%)
  between operations  3.34 us (2%)
    all_gather x1, blocking collectives, body(): table = lax.all_gather(light, 'phi', axis=0, tiled=True)  44.8 us
    all_to_all x1, waiting for transfers between devices, body(): ring = lax.all_to_all(chunks, 'phi', 0, 0, tiled=True)  28.2 us
    pallas_call x1, Pallas kernels, body(): pl.pallas_call(functools.partial(evolve_kernel, cells, cycle, columns, nr...  16.1 us
    pallas_call x1, Pallas kernels, draw_image(): pl.pallas_call(functools.partial(image_kernel, cells, cycle, nphi, nrad,...  12.6 us
    all_to_all x1, starting transfers between devices, body(): ring = lax.all_to_all(chunks, 'phi', 0, 0, tiled=True)  6.77 us
    unnamed x16, local copies, waits for them, and re-layouts  6.16 us
    all_gather x1, blocking collectives, body(): table = lax.all_gather(table, 'row', axis=0, tiled=True)  5.77 us
    all_to_all x1, starting transfers between devices, body(): lax.all_to_all(rows.reshape(cycle, columns * per_column, LANES), 'phi', 0...  4.25 us
  transfers between devices with their start and end apart: 4, of which 1 were waited for; matrix products, arithmetic and copies ran while one was open for 6% of the time, Pallas kernels for 9%

profile of v1, /device:TPU:0, one launch (start us, length us, event | category | flops | bytes accessed | tf_op | source)
XLA Modules:
  0.0 143.1 jit_solution(7598995533743047380)
XLA Ops:
  0.6 1.3 fusion.22
  1.9 1.3 fusion.21
  4.5 0.0 copy-start
  4.5 1.1 copy-done
  5.7 0.0 copy-start.1
  5.7 0.9 copy-done.1
  6.6 0.4 pack.1
  7.1 1.4 maximum_bitcast_fusion
  8.4 0.1 copy.8
  8.5 2.3 %collective-permute-start = (f32[40,128]{1,0:T(8,128)S(1)}, f32[40,128]{1,0:T(8,128)S(1)}, u32[]{:S(2)}, u32[]{:S(2)}) collective-permute-start(f32[40,128]{1,0:T(8,128)S(1)} %select_maximum_fusion.1), channel_id=1, source_target_pairs={{0,1},{1,2},{2,3},{4,5},{5,6},{6,7},{8,9},{9,10},{10,11},{12,13},{... | collective-permute-start | bytes 61448 | tf_op jit(solution)/shard_map/ppermute | solution.py:375
  10.9 0.1 copy.9
  11.0 1.3 collective-permute-start.1
  12.3 0.0 collective-permute-done
  12.3 0.7 fusion.9
  13.0 0.7 fusion.7
  13.7 0.7 fusion.6
  14.3 0.7 fusion.5
  15.0 0.7 fusion.4
  15.7 0.7 fusion.3
  16.4 0.7 fusion.2
  17.1 0.0 collective-permute-done.1
  17.1 0.7 fusion.1
  17.7 0.0 copy-start.3
  17.7 0.0 copy-start.4
  17.7 0.0 copy-start.2
  17.7 6.8 %all-to-all-start = ((f32[8,320,128]{2,1,0:T(8,128)}), f32[8,320,128]{2,1,0:T(8,128)S(1)}, u32[]{:S(2)}, u32[]{:S(2)}) async-start(f32[8,320,128]{2,1,0:T(8,128)} %fusion.1), calls=%async_computation | async-start | bytes 2621440 | tf_op jit(solution)/shard_map/all_to_all | solution.py:382
  24.5 0.1 pad_add_fusion.1.place_ref
  24.6 0.5 fusion.20
  25.8 0.6 fusion.19
  27.0 0.0 copy-done.3
  27.0 0.1 pad_add_fusion.shift_ref
  27.1 0.0 copy-done.4
  27.1 1.4 pad_maximum_fusion.2.frac_ref
  28.4 28.2 %all-to-all-done = f32[8,320,128]{2,1,0:T(8,128)S(1)} async-done(((f32[8,320,128]{2,1,0:T(8,128)}), f32[8,320,128]{2,1,0:T(8,128)S(1)}, u32[]{:S(2)}, u32[]{:S(2)}) %all-to-all-start) | async-done | bytes 1310752 | tf_op jit(solution)/shard_map/all_to_all | solution.py:382
  56.6 0.0 copy-done.2
  56.6 16.1 %evolve.1 = (f32[2048,128]{1,0:T(8,128)}, f32[16,128]{1,0:T(8,128)S(1)}) custom-call(s32[18]{0:T(128)S(1)} %pad_add_fusion.shift_ref, f32[18]{0:T(128)S(1)} %pad_maximum_fusion.2.frac_ref, s32[2]{0:T(128)S(1)} %pad_add_fusion.1.place_ref, f32[4,128]{1,0:T(4,128)S(1)} %copy-done.2, f32[2560,128]{1,0:T(8,128)S(1)} %bitcast.45), custom_call_target="tpu_custom_call" | custom-call | tf_op jit(solution)/shard_map/evolve/pallas_call | solution.py:390
  72.7 4.2 %all-to-all-start.1 = ((f32[8,256,128]{2,1,0:T(8,128)}), f32[8,256,128]{2,1,0:T(8,128)S(1)}, u32[]{:S(2)}, u32[]{:S(2)}) async-start(f32[8,256,128]{2,1,0:T(8,128)} %bitcast.17), calls=%async_computation.1 | async-start | bytes 2097152 | tf_op jit(solution)/shard_map/all_to_all | solution.py:410
  77.0 0.5 add_reduce_fusion
  77.5 0.4 fusion.12
  77.9 0.3 subtract_clamp_fusion.spot_ref
  78.2 0.4 add_subtract_fusion
  78.7 44.8 %all_gather.6 = f32[128,128]{1,0:T(8,128)S(1)} all-gather(f32[16,128]{1,0:T(8,128)S(1)} %get-tuple-element.10), channel_id=1, replica_groups=mesh['phi'=8,'row'=4] {'phi'}, dimensions={0}, use_global_device_ids=true | all-gather | bytes 73728 | tf_op jit(solution)/shard_map/all_gather | solution.py:408
  123.4 5.8 %all_gather.7.table_ref = f32[512,128]{1,0:T(8,128)S(1)} all-gather(f32[128,128]{1,0:T(8,128)S(1)} %all_gather.6), channel_id=1, replica_groups=mesh['phi'=8,'row'=4] {'row'}, dimensions={0}, use_global_device_ids=true | all-gather | bytes 327680 | tf_op jit(solution)/shard_map/all_gather | solution.py:409
  129.2 12.6 %image.1 = f32[32,1024]{1,0:T(8,128)} custom-call(s32[256]{0:T(256)S(1)} %get-tuple-element.22.start_ref, s32[256]{0:T(256)S(1)} %get-tuple-element.12.window_ref, f32[512,128]{1,0:T(8,128)S(1)} %all_gather.7.table_ref, s32[256,128]{1,0:T(8,128)S(1)} %subtract_clamp_fusion.spot_ref, f32[256,128]{1,0:T(8,128)S(1)} %get-tuple-element.20.frac_ref, ...), custom_call_target="tpu_custom_call" | custom-call | tf_op jit(solution)/shard_map/image/pallas_call | solution.py:330
  141.8 0.0 all-to-all-done.1
  141.8 1.3 unpack.1
  (13 shorter events, 0.1 us)
Async XLA Ops:
  4.5 1.1 copy-start
  5.7 0.9 copy-start.1
  8.5 3.7 %collective-permute-start = (f32[40,128]{1,0:T(8,128)S(1)}, f32[40,128]{1,0:T(8,128)S(1)}, u32[]{:S(2)}, u32[]{:S(2)}) collective-permute-start(f32[40,128]{1,0:T(8,128)S(1)} %select_maximum_fusion.1), channel_id=1, source_target_pairs={{0,1},{1,2},{2,3},{4,5},{5,6},{6,7},{8,9},{9,10},{10,11},{12,13},{... | collective-permute-start | bytes 61448 | tf_op jit(solution)/shard_map/ppermute | solution.py:375
  11.0 6.1 %collective-permute-start.1 = (f32[40,128]{1,0:T(8,128)S(1)}, f32[40,128]{1,0:T(8,128)S(1)}, u32[]{:S(2)}, u32[]{:S(2)}) collective-permute-start(f32[40,128]{1,0:T(8,128)S(1)} %select_maximum_fusion), channel_id=1, source_target_pairs={{1,0},{2,1},{3,2},{5,4},{6,5},{7,6},{9,8},{10,9},{11,10},{13,12},{... | collective-permute-start | bytes 61448 | tf_op jit(solution)/shard_map/ppermute | solution.py:376
  17.7 9.2 %copy-start.3 = (s32[16]{0:T(128)S(1)}, s32[16]{0:T(128)}, u32[]{:S(2)}) copy-start(s32[16]{0:T(128)} %param.7) | copy-start | bytes 196
  17.7 9.3 %copy-start.4 = (f32[16]{0:T(128)S(1)}, f32[16]{0:T(128)}, u32[]{:S(2)}) copy-start(f32[16]{0:T(128)} %param.8) | copy-start | bytes 196
  17.7 38.9 %copy-start.2 = (f32[4,128]{1,0:T(4,128)S(1)}, f32[4,128]{1,0:T(4,128)}, u32[]{:S(2)}) copy-start(f32[4,128]{1,0:T(4,128)} %constant.140.clone.tilt_ref) | copy-start | bytes 6148
  17.7 38.9 %all-to-all-start = ((f32[8,320,128]{2,1,0:T(8,128)}), f32[8,320,128]{2,1,0:T(8,128)S(1)}, u32[]{:S(2)}, u32[]{:S(2)}) async-start(f32[8,320,128]{2,1,0:T(8,128)} %fusion.1), calls=%async_computation | async-start | bytes 2621440 | tf_op jit(solution)/shard_map/all_to_all | solution.py:382
  72.7 69.1 %all-to-all-start.1 = ((f32[8,256,128]{2,1,0:T(8,128)}), f32[8,256,128]{2,1,0:T(8,128)S(1)}, u32[]{:S(2)}, u32[]{:S(2)}) async-start(f32[8,256,128]{2,1,0:T(8,128)} %bitcast.17), calls=%async_computation.1 | async-start | bytes 2097152 | tf_op jit(solution)/shard_map/all_to_all | solution.py:410

commit v2 on v1

--- a/solution.py
+++ b/solution.py
@@ -22,6 +22,7 @@
 INNER = 8
 HALO = STEPS
 LANES = 128
+PARTS = 1
 VMEM_LIMIT = 48 * 1024 * 1024
 
 
@@ -41,33 +42,92 @@
     return density_ref if field == 0 else velocity_ref.at[field - 1]
 
 
-def pack_kernel(density_ref, velocity_ref, rows_ref):
+def pack_kernel(last, shift_ref, frac_ref, density_ref, velocity_ref, rows_ref, left_ref, right_ref, field_refs, arrived):
     cells, polar, radial = density_ref.shape
     groups = polar // INNER
+    per_column = FIELDS * groups
+    copies = []
     for field in range(FIELDS):
-        source = field_ref(density_ref, velocity_ref, field)
+        copy = pltpu.make_async_copy(field_ref(density_ref, velocity_ref, field), field_refs.at[field], arrived.at[field])
+        copy.start()
+        copies.append(copy)
+    for field in range(FIELDS):
+        copies[field].wait()
         for group in range(groups):
-            block = source[:, pl.ds(group, INNER, stride=groups), :]
+            block = field_refs[field, :, pl.ds(group, INNER, stride=groups), :]
             turned = block.reshape(cells * INNER, radial).T
-            rows_ref[pl.ds(field * groups + group, radial, stride=FIELDS * groups), :] = turned
-
-
-def unpack_kernel(rows_ref, density_ref, velocity_ref):
+            rows_ref[pl.ds(field * groups + group, radial, stride=per_column), :] = turned
+    edge = HALO * per_column
+    sub = lax.broadcasted_iota(jnp.int32, (8, LANES), 0)
+    for ref, at, band in ((left_ref, 0, 0), (right_ref, radial * per_column - edge, last)):
+        ref[pl.ds(0, edge), :] = rows_ref[pl.ds(at, edge), :]
+        ref[pl.ds(edge, 8), :] = jnp.where(sub == 0, shift_ref[band].astype(jnp.float32), frac_ref[band])
+
+
+def chunk_kernel(cycle, spans, place_ref, rows_ref, left_ref, right_ref, *chunk_refs):
+    edge = left_ref.shape[0] - 8
+    per_column = edge // HALO
+    stride = rows_ref.shape[0] // cycle
+    place = place_ref[0]
+    for j in range(cycle):
+        owner = place ^ j
+        for part, (low, high) in enumerate(spans):
+            target = chunk_refs[part * cycle + j]
+            for col in range(low, high):
+                at = (col - HALO) * per_column
+                slot = pl.ds((col - low) * per_column, per_column)
+                start = pl.multiple_of(jnp.clip(owner * stride + at, 0, rows_ref.shape[0] - per_column), per_column)
+                value = rows_ref[pl.ds(start, per_column), :]
+                if col < HALO:
+                    value = jnp.where(owner == 0, left_ref[pl.ds(col * per_column, per_column), :], value)
+                if at >= stride:
+                    value = jnp.where(owner == cycle - 1, right_ref[pl.ds(at - stride, per_column), :], value)
+                target[slot, :] = value
+
+
+def unpack_kernel(cycle, spans, place_ref, *refs):
+    count = len(spans) * cycle
+    chunk_refs = refs[:count]
+    density_ref, velocity_ref, rows_ref, field_refs, leaving = refs[count:]
     cells, polar, radial = density_ref.shape
     groups = polar // INNER
+    per_column = FIELDS * groups
+    stride = radial // cycle * per_column
+    place = place_ref[0]
+    for j in range(cycle):
+        owner = place ^ j
+        for part, (low, high) in enumerate(spans):
+            size = (high - low) * per_column
+            at = pl.multiple_of(owner * stride + low * per_column, per_column)
+            rows_ref[pl.ds(at, size), :] = chunk_refs[part * cycle + j][...]
+    copies = []
     for field in range(FIELDS):
-        target = field_ref(density_ref, velocity_ref, field)
         for group in range(groups):
-            turned = rows_ref[pl.ds(field * groups + group, radial, stride=FIELDS * groups), :]
+            turned = rows_ref[pl.ds(field * groups + group, radial, stride=per_column), :]
             block = turned.T.reshape(cells, INNER, radial)
-            target[:, pl.ds(group, INNER, stride=groups), :] = block
-
-
-def evolve_kernel(cells, cycle, columns, nrad, groups, swap, shift_ref, frac_ref, place_ref, tilt_ref, in_ref, out_ref, light_ref, work_ref, lit_ref):
+            field_refs[field, :, pl.ds(group, INNER, stride=groups), :] = block
+        copy = pltpu.make_async_copy(field_refs.at[field], field_ref(density_ref, velocity_ref, field), leaving.at[field])
+        copy.start()
+        copies.append(copy)
+    for copy in copies:
+        copy.wait()
+
+
+def evolve_kernel(cells, cycle, first_column, columns, nrad, groups, segments, shift_ref, frac_ref, place_ref, tilt_ref, *refs):
     extended = columns + 2 * HALO
     per_column = FIELDS * groups
-    first = place_ref[0]
-    first_global = place_ref[1]
+    count = len(segments) * cycle
+    chunk_refs = refs[:count]
+    out_refs = refs[count:count + cycle]
+    light_ref, full_ref, work_ref, done_ref = refs[count + cycle:]
+    swap = len(light_ref.shape) == 2
+    place = place_ref[0]
+    first = place_ref[1] + first_column
+    first_global = place_ref[2] + first_column
+    for j in range(cycle):
+        for index, (low, high, at) in enumerate(segments):
+            size = (high - low) * per_column
+            full_ref[pl.ds(low * per_column * cycle + (place ^ j), size, stride=cycle), :] = chunk_refs[index * cycle + j][pl.ds(at, size), :]
     lane = lax.broadcasted_iota(jnp.int32, (cycle, LANES), 1)
     inner = lane % INNER
 
@@ -154,30 +214,30 @@
             write(col - 1, finish(combine(pend, a_rad, -1.0), col - 1))
             return combine(fresh_pend, before, 1.0), b_rad
 
-        pend, _ = lax.fori_loop(low + 2, high - 1, body, (pend, after))
+        pend, _ = lax.fori_loop(low + 2, high - 1, body, (pend, after), unroll=2)
         prim = read(high - 1)
         a_rad = face_part(conserved(prim), prim[1], 1, -1.0)
         write(high - 2, finish(combine(pend, a_rad, -1.0), high - 2))
 
+    def at(col, k, g):
+        return pl.multiple_of((col * per_column + k * groups + g) * cycle, cycle)
+
     def read_input(col):
-        return [
-            [in_ref[pl.ds(col * per_column + k * groups + g, cycle, stride=extended * per_column), :] for g in range(groups)]
-            for k in range(FIELDS)
-        ]
+        return [[full_ref[pl.ds(at(col, k, g), cycle), :] for g in range(groups)] for k in range(FIELDS)]
 
     def read_work(col):
-        return [[work_ref[col * per_column + k * groups + g] for g in range(groups)] for k in range(FIELDS)]
+        return [[work_ref[pl.ds(at(col, k, g), cycle), :] for g in range(groups)] for k in range(FIELDS)]
 
     def write_work(col, prim):
         for k in range(FIELDS):
             for g in range(groups):
-                work_ref[col * per_column + k * groups + g] = prim[k][g]
+                work_ref[pl.ds(at(col, k, g), cycle), :] = prim[k][g]
 
     def write_output(col, prim):
         own = col - HALO
         for k in range(FIELDS):
             for g in range(groups):
-                out_ref[pl.ds(own * per_column + k * groups + g, cycle, stride=columns * per_column), :] = prim[k][g]
+                done_ref[pl.ds(at(own, k, g), cycle), :] = prim[k][g]
         dtau = [(KAPPA / (groups * INNER)) * r for r in prim[0]]
         total = dtau[0]
         for d in dtau[1:]:
@@ -197,15 +257,21 @@
         light = light * (1.0 / jnp.sqrt(radius))
         slot = own % INNER
         light = pltpu.roll(light, slot, 1)
-        lit_ref[own // INNER] = jnp.where(inner == slot, light, lit_ref[own // INNER])
-
-    lit_ref[...] = jnp.zeros_like(lit_ref)
+        if swap:
+            spot = pl.ds(pl.multiple_of(own // INNER * INNER, INNER), INNER)
+            light_ref[spot, :] = jnp.where(inner == slot, light, light_ref[spot, :])
+        else:
+            light_ref[own // INNER] = jnp.where(inner == slot, light, light_ref[own // INNER])
+
+    light_ref[...] = jnp.zeros_like(light_ref)
     step_columns(read_input, write_work, 0, extended)
     step_columns(read_work, write_output, 1, extended - 1)
+    for j in range(cycle):
+        out_refs[j][...] = done_ref[pl.ds(place ^ j, columns * per_column, stride=cycle), :]
     if swap:
         sub = lax.broadcasted_iota(jnp.int32, (cycle, LANES), 0)
         for h in range(columns // INNER):
-            x = lit_ref[h]
+            x = light_ref[pl.ds(h * INNER, INNER), :]
             for d in (1, 2, 4):
                 low_sub = (sub & d) == 0
                 low_lane = (lane & d) == 0
@@ -213,8 +279,6 @@
                 back = pltpu.roll(pltpu.roll(x, d, 0), LANES - d, 1)
                 x = jnp.where(low_sub == low_lane, x, jnp.where(low_sub, ahead, back))
             light_ref[pl.ds(h * INNER, INNER), :] = x
-    else:
-        light_ref[...] = lit_ref[...]
 
 
 def pixel_tiles(first_row, rows_dev, npix, nphi, nrad):
@@ -345,6 +409,20 @@
     return jnp.swapaxes(image, 1, 2).reshape(rows_dev, npix)
 
 
+def exchange(chunks, axis):
+    size = lax.axis_size(axis)
+    far_first = sorted(range(1, size), reverse=True)
+    got = {j: lax.ppermute(chunks[j], axis, [(i, i ^ j) for i in range(size)]) for j in far_first}
+    return [chunks[0]] + [got[j] for j in range(1, size)]
+
+
+def gather_kernel(size, place_ref, *refs):
+    out_ref = refs[size]
+    count = refs[0].shape[0]
+    for j in range(size):
+        out_ref[pl.ds(pl.multiple_of((place_ref[0] ^ j) * count, count), count), :] = refs[j][...]
+
+
 def body(density, velocity, shifts, fractions):
     cycle = lax.axis_size("phi")
     bands = lax.axis_size("row")
@@ -352,73 +430,112 @@
     groups = polar // INNER
     per_column = FIELDS * groups
     columns = radial // cycle
-    extended = columns + 2 * HALO
     nphi = cells * cycle
     nrad = radial * bands
     place = lax.axis_index("phi")
     row = lax.axis_index("row")
-
-    rows = pl.pallas_call(
-        pack_kernel,
-        out_shape=jax.ShapeDtypeStruct((radial * per_column, LANES), jnp.float32),
-        in_specs=vmem(2),
-        out_specs=pl.BlockSpec(memory_space=pltpu.VMEM),
+    where = jnp.stack([place, place * columns, row * radial + place * columns])
+    block = (FIELDS, cells, polar, radial)
+
+    edge = HALO * per_column
+    rows, left, right = pl.pallas_call(
+        functools.partial(pack_kernel, shifts.shape[0] - 1),
+        out_shape=(
+            jax.ShapeDtypeStruct((radial * per_column, LANES), jnp.float32),
+            jax.ShapeDtypeStruct((edge + 8, LANES), jnp.float32),
+            jax.ShapeDtypeStruct((edge + 8, LANES), jnp.float32),
+        ),
+        in_specs=smem(2) + [pl.BlockSpec(memory_space=pl.ANY)] * 2,
+        out_specs=tuple(vmem(3)),
+        scratch_shapes=[pltpu.VMEM(block, jnp.float32), pltpu.SemaphoreType.DMA((FIELDS,))],
         compiler_params=params(),
         name="pack",
-    )(density, velocity)
-    edge = HALO * per_column
-
-    def with_band(block, band):
-        extra = jnp.stack([shifts[band].astype(jnp.float32), fractions[band]])
-        return jnp.concatenate([block, jnp.pad(extra[:, None], ((0, 6), (0, LANES - 1)))])
-
-    left = lax.ppermute(with_band(rows[-edge:], -1), "row", [(i, i + 1) for i in range(bands - 1)])
-    right = lax.ppermute(with_band(rows[:edge], 0), "row", [(i + 1, i) for i in range(bands - 1)])
-    ext_shift = jnp.concatenate([left[edge, :1].astype(jnp.int32), shifts, right[edge, :1].astype(jnp.int32)])
-    ext_frac = jnp.concatenate([left[edge + 1, :1], fractions, right[edge + 1, :1]])
-    rows = jnp.concatenate([left[:edge], rows, right[:edge]])
-    stride = columns * per_column
-    chunks = jnp.stack([rows[q * stride:q * stride + extended * per_column] for q in range(cycle)])
-    ring = lax.all_to_all(chunks, "phi", 0, 0, tiled=True)
-
-    swap = cycle == INNER and columns % INNER == 0
-    slots = -(-columns // INNER)
+    )(shifts, fractions, density, velocity)
+    below = lax.ppermute(right, "row", [(i, i + 1) for i in range(bands - 1)])
+    above = lax.ppermute(left, "row", [(i + 1, i) for i in range(bands - 1)])
+    ext_shift = jnp.concatenate([below[edge, :1].astype(jnp.int32), shifts, above[edge, :1].astype(jnp.int32)])
+    ext_frac = jnp.concatenate([below[edge + 1, :1], fractions, above[edge + 1, :1]])
+
+    cuts = [columns * p // PARTS for p in range(PARTS + 1)] if columns % (PARTS * INNER) == 0 else [0, columns]
+    spans = list(zip(cuts[:-1], cuts[1:]))
+    sent = [(low + 2 * HALO if low else 0, high + 2 * HALO) for low, high in spans]
+    chunks = pl.pallas_call(
+        functools.partial(chunk_kernel, cycle, sent),
+        out_shape=[jax.ShapeDtypeStruct(((high - low) * per_column, LANES), jnp.float32) for low, high in sent for _ in range(cycle)],
+        in_specs=smem(1) + vmem(3),
+        out_specs=vmem(len(spans) * cycle),
+        compiler_params=params(),
+        name="chunk",
+    )(where, rows, below, above)
     theta = (np.arange(polar) + 0.5) / polar
     tilt = (1.0 + 0.5 * np.cos(np.pi * theta)).reshape(INNER, groups).T
     tilt = jnp.asarray(np.tile(tilt, (1, LANES // INNER)), jnp.float32)
-    where = jnp.stack([place * columns, row * radial + place * columns])
-    rows, light = pl.pallas_call(
-        functools.partial(evolve_kernel, cells, cycle, columns, nrad, groups, swap),
-        out_shape=(
-            jax.ShapeDtypeStruct((cycle * columns * per_column, LANES), jnp.float32),
-            jax.ShapeDtypeStruct((columns, LANES) if swap else (slots, cycle, LANES), jnp.float32),
-        ),
-        in_specs=smem(3) + vmem(2),
-        out_specs=tuple(vmem(2)),
-        scratch_shapes=[
-            pltpu.VMEM((extended * per_column, cycle, LANES), jnp.float32),
-            pltpu.VMEM((slots, cycle, LANES), jnp.float32),
-        ],
-        compiler_params=params(),
-        name="evolve",
-    )(ext_shift, ext_frac, where, tilt, ring.reshape(cycle * extended * per_column, LANES))
-    if not swap:
-        light = light.reshape(slots, cycle, cells, INNER).transpose(0, 3, 2, 1).reshape(slots * INNER, nphi)[:columns]
-
-    table = lax.all_gather(light, "phi", axis=0, tiled=True)
+
+    rings = [exchange(chunks[p * cycle:(p + 1) * cycle], "phi") for p in range(len(spans))]
+    back = []
+    lights = []
+    for p, (low, high) in enumerate(spans):
+        width = high - low
+        swap = cycle == INNER and width % INNER == 0
+        segments = []
+        taken = []
+        for index, (begin, end) in enumerate(sent):
+            begin_here, end_here = max(begin, low), min(end, high + 2 * HALO)
+            if begin_here < end_here:
+                segments.append((begin_here - low, end_here - low, (begin_here - begin) * per_column))
+                taken += rings[index]
+        chunk = jax.ShapeDtypeStruct((width * per_column, LANES), jnp.float32)
+        slots = -(-width // INNER)
+        wide = (width + 2 * HALO) * per_column * cycle
+        *out, light = pl.pallas_call(
+            functools.partial(evolve_kernel, cells, cycle, low, width, nrad, groups, segments),
+            out_shape=[chunk] * cycle + [jax.ShapeDtypeStruct((width, LANES) if swap else (slots, cycle, LANES), jnp.float32)],
+            in_specs=smem(3) + vmem(1 + len(taken)),
+            out_specs=vmem(cycle + 1),
+            scratch_shapes=[
+                pltpu.VMEM((wide, LANES), jnp.float32),
+                pltpu.VMEM((wide, LANES), jnp.float32),
+                pltpu.VMEM((width * per_column * cycle, LANES), jnp.float32),
+            ],
+            compiler_params=params(),
+            name="evolve",
+        )(ext_shift, ext_frac, where, tilt, *taken)
+        if not swap:
+            light = light.reshape(slots, cycle, cells, INNER).transpose(0, 3, 2, 1).reshape(slots * INNER, nphi)[:width]
+        lights.append(light)
+        back += exchange(out, "phi")
+
+    light = jnp.concatenate(lights)
+    if columns % 8 == 0:
+        pieces = exchange([light] * cycle, "phi")
+        table = pl.pallas_call(
+            functools.partial(gather_kernel, cycle),
+            out_shape=jax.ShapeDtypeStruct((radial, nphi), jnp.float32),
+            in_specs=smem(1) + vmem(cycle),
+            out_specs=pl.BlockSpec(memory_space=pltpu.VMEM),
+            compiler_params=params(),
+            name="gather",
+        )(where, *pieces)
+    else:
+        table = lax.all_gather(light, "phi", axis=0, tiled=True)
     table = lax.all_gather(table, "row", axis=0, tiled=True)
-    back = lax.all_to_all(rows.reshape(cycle, columns * per_column, LANES), "phi", 0, 0, tiled=True)
+
     density_out, velocity_out = pl.pallas_call(
-        unpack_kernel,
+        functools.partial(unpack_kernel, cycle, spans),
         out_shape=(
             jax.ShapeDtypeStruct(density.shape, jnp.float32),
             jax.ShapeDtypeStruct(velocity.shape, jnp.float32),
         ),
-        in_specs=vmem(1),
-        out_specs=tuple(vmem(2)),
+        in_specs=smem(1) + vmem(len(back)),
+        out_specs=[pl.BlockSpec(memory_space=pl.ANY)] * 2,
+        scratch_shapes=[
+            pltpu.VMEM((radial * per_column, LANES), jnp.float32),
+            pltpu.VMEM(block, jnp.float32),
+            pltpu.SemaphoreType.DMA((FIELDS,)),
+        ],
         compiler_params=params(),
         name="unpack",
-    )(back.reshape(radial * per_column, LANES))
+    )(where, *back)
 
     rows_dev = NPIX // (cycle * bands)
     first_row = (place * bands + row) * rows_dev

time: 144 us -> 106 us (0.74)
  blocking collectives: 50.5 us -> 5.79 us
  starting transfers between devices: 14.6 us -> 44.5 us
  waiting for transfers between devices: 28.2 us -> 16.9 us
  local copies, waits for them, and re-layouts: 10.1 us -> 5.73 us
  Pallas kernels: 30.5 us -> 27.3 us
  other arithmetic: 5.92 us -> 3.17 us
    all_gather x1 -> x0, blocking collectives: 44.8 us -> none  [body(): table = lax.all_gather(light, 'phi', axis=0, tiled=True)]
    ppermute x2 -> x23, starting transfers between devices: 3.63 us -> 44.5 us  [the longest x21 40.8 us: exchange(): lax.ppermute(chunks[j], axis, [(i, i ^ j) for i in range(size)])]
    all_to_all x2 -> x0, waiting for transfers between devices: 28.2 us -> none  [the longest x1 28.2 us: body(): ring = lax.all_to_all(chunks, 'phi', 0, 0, tiled=True)]
    ppermute x2 -> x23, waiting for transfers between devices: 0.01 us -> 16.9 us  [the longest x21 14.1 us: exchange(): lax.ppermute(chunks[j], axis, [(i, i ^ j) for i in range(size)])]
    all_to_all x2 -> x0, starting transfers between devices: 11 us -> none  [the longest x1 6.77 us: body(): ring = lax.all_to_all(chunks, 'phi', 0, 0, tiled=True)]
    pallas_call x3 -> x5, Pallas kernels: 17.8 us -> 14.7 us  [the longest x1 10.3 us: body(): pl.pallas_call(functools.partial(evolve_kernel, cells, cycle, low, width,...]
    slice x7 -> x2, local copies, waits for them, and re-layouts: 3.73 us -> 1.04 us  [the longest x1 0.52 us: body(): below[edge + 1, :1]]
    unnamed x16 -> x14, local copies, waits for them, and re-layouts: 6.16 us -> 4.69 us
  transfers between devices with their start and end apart: 4 -> 23, of which waited for: 1 -> 5; matrix products, arithmetic and copies ran while one was open for 6% -> 4% of each run, Pallas kernels for 9% -> 12%
where the time goes in v2:
time: 106 us
  starting transfers between devices  44.5 us (42%)
  Pallas kernels  27.3 us (26%)
  waiting for transfers between devices  16.9 us (16%)
  blocking collectives  5.79 us (5%)
  local copies, waits for them, and re-layouts  5.73 us (5%)
  other arithmetic  3.17 us (3%)
  between operations  2.12 us (2%)
    ppermute x21, starting transfers between devices, exchange(): lax.ppermute(chunks[j], axis, [(i, i ^ j) for i in range(size)])  40.8 us
    ppermute x21, waiting for transfers between devices, exchange(): lax.ppermute(chunks[j], axis, [(i, i ^ j) for i in range(size)])  14.1 us
    pallas_call x1, Pallas kernels, draw_image(): pl.pallas_call(functools.partial(image_kernel, cells, cycle, nphi, nrad,...  12.6 us
    pallas_call x1, Pallas kernels, body(): pl.pallas_call(functools.partial(evolve_kernel, cells, cycle, low, width,...  10.3 us
    all_gather x1, blocking collectives, body(): table = lax.all_gather(table, 'row', axis=0, tiled=True)  5.79 us
    unnamed x14, local copies, waits for them, and re-layouts  4.69 us
    ppermute x1, waiting for transfers between devices, body(): above = lax.ppermute(left, 'row', [(i + 1, i) for i in range(bands - 1)])  2.83 us
    ppermute x1, starting transfers between devices, body(): below = lax.ppermute(right, 'row', [(i, i + 1) for i in range(bands - 1)])  2.36 us
  transfers between devices with their start and end apart: 23, of which 5 were waited for; matrix products, arithmetic and copies ran while one was open for 4% of the time, Pallas kernels for 12%

profile of v2, /device:TPU:0, one launch (start us, length us, event | category | flops | bytes accessed | tf_op | source)
XLA Modules:
  0.0 105.5 jit_solution(11852175142624651985)
XLA Ops:
  0.6 1.1 %copy-done = f32[3,16,32,128]{3,2,1,0:T(8,128)S(1)} copy-done((f32[3,16,32,128]{3,2,1,0:T(8,128)S(1)}, f32[3,16,32,128]{3,2,1,0:T(8,128)}, u32[]{:S(2)}) %copy-start) | copy-done | bytes 786456
  1.8 0.9 copy-done.1
  2.7 0.7 copy-done.2
  3.4 0.7 copy-done.4
  4.0 1.3 %pack.1 = (f32[2048,128]{1,0:T(8,128)S(1)}, f32[40,128]{1,0:T(8,128)S(1)}, f32[40,128]{1,0:T(8,128)S(1)}) custom-call(s32[16]{0:T(128)S(1)} %copy-done.4, f32[16]{0:T(128)S(1)} %copy-done.2, f32[16,32,128]{2,1,0:T(8,128)S(1)} %copy-done.1, f32[3,16,32,128]{3,2,1,0:T(8,128)S(1)} %copy-done), custom_call_target="tpu_custom_call" | custom-call | tf_op jit(solution)/shard_map/pack/pallas_call | solution.py:441
  5.3 2.4 %collective-permute-start = (f32[40,128]{1,0:T(8,128)S(1)}, f32[40,128]{1,0:T(8,128)S(1)}, u32[]{:S(2)}, u32[]{:S(2)}) collective-permute-start(f32[40,128]{1,0:T(8,128)S(1)} %get-tuple-element.25), channel_id=1, source_target_pairs={{0,1},{1,2},{2,3},{4,5},{5,6},{6,7},{8,9},{9,10},{10,11},{12,13},{... | collective-permute-start | bytes 61448 | tf_op jit(solution)/shard_map/ppermute | solution.py:454
  7.7 1.3 %collective-permute-start.1 = (f32[40,128]{1,0:T(8,128)S(1)}, f32[40,128]{1,0:T(8,128)S(1)}, u32[]{:S(2)}, u32[]{:S(2)}) collective-permute-start(f32[40,128]{1,0:T(8,128)S(1)} %get-tuple-element.26), channel_id=1, source_target_pairs={{1,0},{2,1},{3,2},{5,4},{6,5},{7,6},{9,8},{10,9},{11,10},{13,12},{... | collective-permute-start | bytes 61448 | tf_op jit(solution)/shard_map/ppermute | solution.py:455
  9.0 0.5 add_reduce_fusion
  9.5 0.4 add_subtract_fusion
  10.0 0.1 pad_add_fusion.place_ref
  10.1 2.8 %collective-permute-done.1.right_ref = f32[40,128]{1,0:T(8,128)S(1)} collective-permute-done((f32[40,128]{1,0:T(8,128)S(1)}, f32[40,128]{1,0:T(8,128)S(1)}, u32[]{:S(2)}, u32[]{:S(2)}) %collective-permute-start.1) | collective-permute-done | bytes 20512 | tf_op jit(solution)/shard_map/ppermute | solution.py:455
  12.9 0.8 chunk.1
  13.7 1.6 %collective-permute-start.2 = (f32[320,128]{1,0:T(8,128)S(1)}, f32[320,128]{1,0:T(8,128)S(1)}, u32[]{:S(2)}, u32[]{:S(2)}) collective-permute-start(f32[320,128]{1,0:T(8,128)S(1)} %get-tuple-element.29), channel_id=1, source_target_pairs={{0,4},{4,0},{8,12},{12,8},{16,20},{20,16},{24,28},{28,24},{1,5},{5... | collective-permute-start | bytes 491528 | tf_op jit(solution)/shard_map/ppermute | solution.py:415
  15.3 1.6 %collective-permute-start.3 = (f32[320,128]{1,0:T(8,128)S(1)}, f32[320,128]{1,0:T(8,128)S(1)}, u32[]{:S(2)}, u32[]{:S(2)}) collective-permute-start(f32[320,128]{1,0:T(8,128)S(1)} %get-tuple-element.30), channel_id=1, source_target_pairs={{0,8},{4,12},{8,0},{12,4},{16,24},{20,28},{24,16},{28,20},{1,9},{5... | collective-permute-start | bytes 491528 | tf_op jit(solution)/shard_map/ppermute | solution.py:415
  16.8 0.4 collective-permute-start.4
  17.3 2.6 %collective-permute-start.5 = (f32[320,128]{1,0:T(8,128)S(1)}, f32[320,128]{1,0:T(8,128)S(1)}, u32[]{:S(2)}, u32[]{:S(2)}) collective-permute-start(f32[320,128]{1,0:T(8,128)S(1)} %get-tuple-element.32), channel_id=1, source_target_pairs={{0,16},{4,20},{8,24},{12,28},{16,0},{20,4},{24,8},{28,12},{1,17},{... | collective-permute-start | bytes 491528 | tf_op jit(solution)/shard_map/ppermute | solution.py:415
  19.9 1.3 %collective-permute-start.6 = (f32[320,128]{1,0:T(8,128)S(1)}, f32[320,128]{1,0:T(8,128)S(1)}, u32[]{:S(2)}, u32[]{:S(2)}) collective-permute-start(f32[320,128]{1,0:T(8,128)S(1)} %get-tuple-element.33), channel_id=1, source_target_pairs={{0,20},{4,16},{8,28},{12,24},{16,4},{20,0},{24,12},{28,8},{1,21},{... | collective-permute-start | bytes 491528 | tf_op jit(solution)/shard_map/ppermute | solution.py:415
  21.1 0.5 fusion.8
  21.6 0.5 fusion.9
  22.2 3.6 %collective-permute-start.7 = (f32[320,128]{1,0:T(8,128)S(1)}, f32[320,128]{1,0:T(8,128)S(1)}, u32[]{:S(2)}, u32[]{:S(2)}) collective-permute-start(f32[320,128]{1,0:T(8,128)S(1)} %get-tuple-element.34), channel_id=1, source_target_pairs={{0,24},{4,28},{8,16},{12,20},{16,8},{20,12},{24,0},{28,4},{1,25},{... | collective-permute-start | bytes 491528 | tf_op jit(solution)/shard_map/ppermute | solution.py:415
  25.8 0.2 collective-permute-start.8
  26.0 0.7 copy-done.3
  26.6 1.4 %pad_maximum_fusion.frac_ref = f32[18]{0:T(128)S(1)} fusion(f32[1]{0:T(128)} %bitcast.6, f32[16]{0:T(128)S(1)} %copy-done.3, f32[1]{0:T(128)} %bitcast.5), kind=kLoop, calls=%fused_computation.32 | loop fusion | flops 36 | bytes 144 | tf_op jit(solution)/shard_map/concatenate | solution.py:457
  29.3 0.6 copy-done.5
  29.9 0.1 pad_add_fusion.1.shift_ref
  30.0 0.1 collective-permute-done.4.refs_3_
  30.1 13.0 %collective-permute-done.6.refs_5_ = f32[320,128]{1,0:T(8,128)S(1)} collective-permute-done((f32[320,128]{1,0:T(8,128)S(1)}, f32[320,128]{1,0:T(8,128)S(1)}, u32[]{:S(2)}, u32[]{:S(2)}) %collective-permute-start.6) | collective-permute-done | bytes 163872 | tf_op jit(solution)/shard_map/ppermute | solution.py:415
  43.1 10.3 %evolve.1 = (f32[256,128]{1,0:T(8,128)S(1)}, f32[256,128]{1,0:T(8,128)S(1)}, f32[256,128]{1,0:T(8,128)S(1)}, f32[256,128]{1,0:T(8,128)S(1)}, f32[256,128]{1,0:T(...) custom-call(s32[18]{0:T(128)S(1)} %pad_add_fusion.1.shift_ref, ...), custom_call_target="tpu_custom_call" | custom-call | tf_op jit(solution)/shard_map/evolve/pallas_call | solution.py:490
  53.4 1.0 collective-permute-start.16
  54.4 7.6 %collective-permute-start.17 = (f32[16,128]{1,0:T(8,128)S(1)}, f32[16,128]{1,0:T(8,128)S(1)}, u32[]{:S(2)}, u32[]{:S(2)}) collective-permute-start(f32[16,128]{1,0:T(8,128)S(1)} %get-tuple-element.46.refs_0_), channel_id=1, source_target_pairs={{0,8},{4,12},{8,0},{12,4},{16,24},{20,28},{24,16},{28,20},{1,9},{5... | collective-permute-start | bytes 24584 | tf_op jit(solution)/shard_map/ppermute | solution.py:415
  62.0 0.5 collective-permute-start.18
  62.5 4.2 %collective-permute-start.19 = (f32[16,128]{1,0:T(8,128)S(1)}, f32[16,128]{1,0:T(8,128)S(1)}, u32[]{:S(2)}, u32[]{:S(2)}) collective-permute-start(f32[16,128]{1,0:T(8,128)S(1)} %get-tuple-element.46.refs_0_), channel_id=1, source_target_pairs={{0,16},{4,20},{8,24},{12,28},{16,0},{20,4},{24,8},{28,12},{1,17},{... | collective-permute-start | bytes 24584 | tf_op jit(solution)/shard_map/ppermute | solution.py:415
  66.7 0.4 fusion.2
  67.1 2.3 %collective-permute-start.21 = (f32[16,128]{1,0:T(8,128)S(1)}, f32[16,128]{1,0:T(8,128)S(1)}, u32[]{:S(2)}, u32[]{:S(2)}) collective-permute-start(f32[16,128]{1,0:T(8,128)S(1)} %get-tuple-element.46.refs_0_), channel_id=1, source_target_pairs={{0,24},{4,28},{8,16},{12,20},{16,8},{20,12},{24,0},{28,4},{1,25},{... | collective-permute-start | bytes 24584 | tf_op jit(solution)/shard_map/ppermute | solution.py:415
  69.5 2.4 %collective-permute-start.22 = (f32[16,128]{1,0:T(8,128)S(1)}, f32[16,128]{1,0:T(8,128)S(1)}, u32[]{:S(2)}, u32[]{:S(2)}) collective-permute-start(f32[16,128]{1,0:T(8,128)S(1)} %get-tuple-element.46.refs_0_), channel_id=1, source_target_pairs={{0,28},{4,24},{8,20},{12,16},{16,12},{20,8},{24,4},{28,0},{1,29},{... | collective-permute-start | bytes 24584 | tf_op jit(solution)/shard_map/ppermute | solution.py:415
  71.9 2.1 %collective-permute-start.11 = (f32[256,128]{1,0:T(8,128)S(1)}, f32[256,128]{1,0:T(8,128)S(1)}, u32[]{:S(2)}, u32[]{:S(2)}) collective-permute-start(f32[256,128]{1,0:T(8,128)S(1)} %get-tuple-element.39), channel_id=1, source_target_pairs={{0,12},{4,8},{8,4},{12,0},{16,28},{20,24},{24,20},{28,16},{1,13},{... | collective-permute-start | bytes 393224 | tf_op jit(solution)/shard_map/ppermute | solution.py:415
  74.0 1.1 %collective-permute-start.12 = (f32[256,128]{1,0:T(8,128)S(1)}, f32[256,128]{1,0:T(8,128)S(1)}, u32[]{:S(2)}, u32[]{:S(2)}) collective-permute-start(f32[256,128]{1,0:T(8,128)S(1)} %get-tuple-element.40), channel_id=1, source_target_pairs={{0,16},{4,20},{8,24},{12,28},{16,0},{20,4},{24,8},{28,12},{1,17},{... | collective-permute-start | bytes 393224 | tf_op jit(solution)/shard_map/ppermute | solution.py:415
  75.1 2.7 %collective-permute-start.13 = (f32[256,128]{1,0:T(8,128)S(1)}, f32[256,128]{1,0:T(8,128)S(1)}, u32[]{:S(2)}, u32[]{:S(2)}) collective-permute-start(f32[256,128]{1,0:T(8,128)S(1)} %get-tuple-element.41), channel_id=1, source_target_pairs={{0,20},{4,16},{8,28},{12,24},{16,4},{20,0},{24,12},{28,8},{1,21},{... | collective-permute-start | bytes 393224 | tf_op jit(solution)/shard_map/ppermute | solution.py:415
  77.8 2.4 %collective-permute-start.14 = (f32[256,128]{1,0:T(8,128)S(1)}, f32[256,128]{1,0:T(8,128)S(1)}, u32[]{:S(2)}, u32[]{:S(2)}) collective-permute-start(f32[256,128]{1,0:T(8,128)S(1)} %get-tuple-element.42), channel_id=1, source_target_pairs={{0,24},{4,28},{8,16},{12,20},{16,8},{20,12},{24,0},{28,4},{1,25},{... | collective-permute-start | bytes 393224 | tf_op jit(solution)/shard_map/ppermute | solution.py:415
  80.2 0.5 collective-permute-done.10.refs_2_
  80.6 1.5 %collective-permute-start.15 = (f32[256,128]{1,0:T(8,128)S(1)}, f32[256,128]{1,0:T(8,128)S(1)}, u32[]{:S(2)}, u32[]{:S(2)}) collective-permute-start(f32[256,128]{1,0:T(8,128)S(1)} %get-tuple-element.43), channel_id=1, source_target_pairs={{0,28},{4,24},{8,20},{12,16},{16,12},{20,8},{24,4},{28,0},{1,29},{... | collective-permute-start | bytes 393224 | tf_op jit(solution)/shard_map/ppermute | solution.py:415
  82.2 0.5 collective-permute-done.11.refs_3_
  82.6 1.8 %collective-permute-start.9 = (f32[256,128]{1,0:T(8,128)S(1)}, f32[256,128]{1,0:T(8,128)S(1)}, u32[]{:S(2)}, u32[]{:S(2)}) collective-permute-start(f32[256,128]{1,0:T(8,128)S(1)} %get-tuple-element.37), channel_id=1, source_target_pairs={{0,4},{4,0},{8,12},{12,8},{16,20},{20,16},{24,28},{28,24},{1,5},{5... | collective-permute-start | bytes 393224 | tf_op jit(solution)/shard_map/ppermute | solution.py:415
  84.4 0.3 subtract_clamp_fusion.spot_ref
  84.8 0.6 gather.1
  85.3 5.8 %all_gather.3.table_ref = f32[512,128]{1,0:T(8,128)S(1)} all-gather(f32[128,128]{1,0:T(8,128)S(1)} %gather.1), channel_id=1, replica_groups=mesh['phi'=8,'row'=4] {'row'}, dimensions={0}, use_global_device_ids=true | all-gather | bytes 327680 | tf_op jit(solution)/shard_map/all_gather | solution.py:521
  91.1 12.6 %image.1 = f32[32,1024]{1,0:T(8,128)} custom-call(s32[256]{0:T(256)S(1)} %get-tuple-element.56.start_ref, s32[256]{0:T(256)S(1)} %get-tuple-element.48.window_ref, f32[512,128]{1,0:T(8,128)S(1)} %all_gather.3.table_ref, s32[256,128]{1,0:T(8,128)S(1)} %subtract_clamp_fusion.spot_ref, f32[256,128]{1,0:T(8,128)S(1)} %get-tuple-element.54.frac_ref, ...), custom_call_target="tpu_custom_call" | custom-call | tf_op jit(solution)/shard_map/image/pallas_call | solution.py:394
  103.8 1.8 %unpack.1 = (f32[16,32,128]{2,1,0:T(8,128)}, f32[3,16,32,128]{3,2,1,0:T(8,128)}) custom-call(s32[3]{0:T(128)S(1)} %pad_add_fusion.place_ref, f32[256,128]{1,0:T(8,128)S(1)} %get-tuple-element.36.refs_0_, f32[256,128]{1,0:T(8,128)S(1)} %collective-permute-done.9.refs_1_, f32[256,128]{1,0:T(8,128)S(1)} %collective-permute-done.10.refs_2_, ...), custom_call_target="tpu_custom_call" | custom-call | tf_op jit(solution)/shard_map/unpack/pallas_call | solution.py:523
  (36 shorter events, 0.2 us)
Async XLA Ops:
  0.6 1.1 %copy-start = (f32[3,16,32,128]{3,2,1,0:T(8,128)S(1)}, f32[3,16,32,128]{3,2,1,0:T(8,128)}, u32[]{:S(2)}) copy-start(f32[3,16,32,128]{3,2,1,0:T(8,128)} %velocity_ref.1) | copy-start | bytes 2359300
  1.8 0.9 copy-start.1
  2.7 0.7 copy-start.2
  3.4 0.7 copy-start.4
  5.3 4.8 %collective-permute-start = (f32[40,128]{1,0:T(8,128)S(1)}, f32[40,128]{1,0:T(8,128)S(1)}, u32[]{:S(2)}, u32[]{:S(2)}) collective-permute-start(f32[40,128]{1,0:T(8,128)S(1)} %get-tuple-element.25), channel_id=1, source_target_pairs={{0,1},{1,2},{2,3},{4,5},{5,6},{6,7},{8,9},{9,10},{10,11},{12,13},{... | collective-permute-start | bytes 61448 | tf_op jit(solution)/shard_map/ppermute | solution.py:454
  7.7 5.2 %collective-permute-start.1 = (f32[40,128]{1,0:T(8,128)S(1)}, f32[40,128]{1,0:T(8,128)S(1)}, u32[]{:S(2)}, u32[]{:S(2)}) collective-permute-start(f32[40,128]{1,0:T(8,128)S(1)} %get-tuple-element.26), channel_id=1, source_target_pairs={{1,0},{2,1},{3,2},{5,4},{6,5},{7,6},{9,8},{10,9},{11,10},{13,12},{... | collective-permute-start | bytes 61448 | tf_op jit(solution)/shard_map/ppermute | solution.py:455
  13.7 8.5 %collective-permute-start.2 = (f32[320,128]{1,0:T(8,128)S(1)}, f32[320,128]{1,0:T(8,128)S(1)}, u32[]{:S(2)}, u32[]{:S(2)}) collective-permute-start(f32[320,128]{1,0:T(8,128)S(1)} %get-tuple-element.29), channel_id=1, source_target_pairs={{0,4},{4,0},{8,12},{12,8},{16,20},{20,16},{24,28},{28,24},{1,5},{5... | collective-permute-start | bytes 491528 | tf_op jit(solution)/shard_map/ppermute | solution.py:415
  15.3 10.5 %collective-permute-start.3 = (f32[320,128]{1,0:T(8,128)S(1)}, f32[320,128]{1,0:T(8,128)S(1)}, u32[]{:S(2)}, u32[]{:S(2)}) collective-permute-start(f32[320,128]{1,0:T(8,128)S(1)} %get-tuple-element.30), channel_id=1, source_target_pairs={{0,8},{4,12},{8,0},{12,4},{16,24},{20,28},{24,16},{28,20},{1,9},{5... | collective-permute-start | bytes 491528 | tf_op jit(solution)/shard_map/ppermute | solution.py:415
  16.8 13.3 %collective-permute-start.4 = (f32[320,128]{1,0:T(8,128)S(1)}, f32[320,128]{1,0:T(8,128)S(1)}, u32[]{:S(2)}, u32[]{:S(2)}) collective-permute-start(f32[320,128]{1,0:T(8,128)S(1)} %get-tuple-element.31), channel_id=1, source_target_pairs={{0,12},{4,8},{8,4},{12,0},{16,28},{20,24},{24,20},{28,16},{1,13},{... | collective-permute-start | bytes 491528 | tf_op jit(solution)/shard_map/ppermute | solution.py:415
  17.3 12.8 %collective-permute-start.5 = (f32[320,128]{1,0:T(8,128)S(1)}, f32[320,128]{1,0:T(8,128)S(1)}, u32[]{:S(2)}, u32[]{:S(2)}) collective-permute-start(f32[320,128]{1,0:T(8,128)S(1)} %get-tuple-element.32), channel_id=1, source_target_pairs={{0,16},{4,20},{8,24},{12,28},{16,0},{20,4},{24,8},{28,12},{1,17},{... | collective-permute-start | bytes 491528 | tf_op jit(solution)/shard_map/ppermute | solution.py:415
  19.9 23.2 %collective-permute-start.6 = (f32[320,128]{1,0:T(8,128)S(1)}, f32[320,128]{1,0:T(8,128)S(1)}, u32[]{:S(2)}, u32[]{:S(2)}) collective-permute-start(f32[320,128]{1,0:T(8,128)S(1)} %get-tuple-element.33), channel_id=1, source_target_pairs={{0,20},{4,16},{8,28},{12,24},{16,4},{20,0},{24,12},{28,8},{1,21},{... | collective-permute-start | bytes 491528 | tf_op jit(solution)/shard_map/ppermute | solution.py:415
  22.2 20.9 %collective-permute-start.7 = (f32[320,128]{1,0:T(8,128)S(1)}, f32[320,128]{1,0:T(8,128)S(1)}, u32[]{:S(2)}, u32[]{:S(2)}) collective-permute-start(f32[320,128]{1,0:T(8,128)S(1)} %get-tuple-element.34), channel_id=1, source_target_pairs={{0,24},{4,28},{8,16},{12,20},{16,8},{20,12},{24,0},{28,4},{1,25},{... | collective-permute-start | bytes 491528 | tf_op jit(solution)/shard_map/ppermute | solution.py:415
  25.8 17.3 %collective-permute-start.8 = (f32[320,128]{1,0:T(8,128)S(1)}, f32[320,128]{1,0:T(8,128)S(1)}, u32[]{:S(2)}, u32[]{:S(2)}) collective-permute-start(f32[320,128]{1,0:T(8,128)S(1)} %get-tuple-element.35), channel_id=1, source_target_pairs={{0,28},{4,24},{8,20},{12,16},{16,12},{20,8},{24,4},{28,0},{1,29},{... | collective-permute-start | bytes 491528 | tf_op jit(solution)/shard_map/ppermute | solution.py:415
  26.0 0.7 copy-start.3
  29.3 0.7 copy-start.5
  29.9 13.2 %copy-start.6 = (f32[4,128]{1,0:T(4,128)S(1)}, f32[4,128]{1,0:T(4,128)}, u32[]{:S(2)}) copy-start(f32[4,128]{1,0:T(4,128)} %constant.138.clone.tilt_ref) | copy-start | bytes 6148
  53.4 13.7 %collective-permute-start.16 = (f32[16,128]{1,0:T(8,128)S(1)}, f32[16,128]{1,0:T(8,128)S(1)}, u32[]{:S(2)}, u32[]{:S(2)}) collective-permute-start(f32[16,128]{1,0:T(8,128)S(1)} %get-tuple-element.46.refs_0_), channel_id=1, source_target_pairs={{0,4},{4,0},{8,12},{12,8},{16,20},{20,16},{24,28},{28,24},{1,5},{5... | collective-permute-start | bytes 24584 | tf_op jit(solution)/shard_map/ppermute | solution.py:415
  54.4 15.1 %collective-permute-start.17 = (f32[16,128]{1,0:T(8,128)S(1)}, f32[16,128]{1,0:T(8,128)S(1)}, u32[]{:S(2)}, u32[]{:S(2)}) collective-permute-start(f32[16,128]{1,0:T(8,128)S(1)} %get-tuple-element.46.refs_0_), channel_id=1, source_target_pairs={{0,8},{4,12},{8,0},{12,4},{16,24},{20,28},{24,16},{28,20},{1,9},{5... | collective-permute-start | bytes 24584 | tf_op jit(solution)/shard_map/ppermute | solution.py:415
  62.0 9.9 %collective-permute-start.18 = (f32[16,128]{1,0:T(8,128)S(1)}, f32[16,128]{1,0:T(8,128)S(1)}, u32[]{:S(2)}, u32[]{:S(2)}) collective-permute-start(f32[16,128]{1,0:T(8,128)S(1)} %get-tuple-element.46.refs_0_), channel_id=1, source_target_pairs={{0,12},{4,8},{8,4},{12,0},{16,28},{20,24},{24,20},{28,16},{1,13},{... | collective-permute-start | bytes 24584 | tf_op jit(solution)/shard_map/ppermute | solution.py:415
  62.5 9.3 %collective-permute-start.19 = (f32[16,128]{1,0:T(8,128)S(1)}, f32[16,128]{1,0:T(8,128)S(1)}, u32[]{:S(2)}, u32[]{:S(2)}) collective-permute-start(f32[16,128]{1,0:T(8,128)S(1)} %get-tuple-element.46.refs_0_), channel_id=1, source_target_pairs={{0,16},{4,20},{8,24},{12,28},{16,0},{20,4},{24,8},{28,12},{1,17},{... | collective-permute-start | bytes 24584 | tf_op jit(solution)/shard_map/ppermute | solution.py:415
  67.1 6.9 %collective-permute-start.20 = (f32[16,128]{1,0:T(8,128)S(1)}, f32[16,128]{1,0:T(8,128)S(1)}, u32[]{:S(2)}, u32[]{:S(2)}) collective-permute-start(f32[16,128]{1,0:T(8,128)S(1)} %get-tuple-element.46.refs_0_), channel_id=1, source_target_pairs={{0,20},{4,16},{8,28},{12,24},{16,4},{20,0},{24,12},{28,8},{1,21},{... | collective-permute-start | bytes 24584 | tf_op jit(solution)/shard_map/ppermute | solution.py:415
  67.1 7.9 %collective-permute-start.21 = (f32[16,128]{1,0:T(8,128)S(1)}, f32[16,128]{1,0:T(8,128)S(1)}, u32[]{:S(2)}, u32[]{:S(2)}) collective-permute-start(f32[16,128]{1,0:T(8,128)S(1)} %get-tuple-element.46.refs_0_), channel_id=1, source_target_pairs={{0,24},{4,28},{8,16},{12,20},{16,8},{20,12},{24,0},{28,4},{1,25},{... | collective-permute-start | bytes 24584 | tf_op jit(solution)/shard_map/ppermute | solution.py:415
  69.5 8.3 %collective-permute-start.22 = (f32[16,128]{1,0:T(8,128)S(1)}, f32[16,128]{1,0:T(8,128)S(1)}, u32[]{:S(2)}, u32[]{:S(2)}) collective-permute-start(f32[16,128]{1,0:T(8,128)S(1)} %get-tuple-element.46.refs_0_), channel_id=1, source_target_pairs={{0,28},{4,24},{8,20},{12,16},{16,12},{20,8},{24,4},{28,0},{1,29},{... | collective-permute-start | bytes 24584 | tf_op jit(solution)/shard_map/ppermute | solution.py:415
  71.9 8.8 %collective-permute-start.10 = (f32[256,128]{1,0:T(8,128)S(1)}, f32[256,128]{1,0:T(8,128)S(1)}, u32[]{:S(2)}, u32[]{:S(2)}) collective-permute-start(f32[256,128]{1,0:T(8,128)S(1)} %get-tuple-element.38), channel_id=1, source_target_pairs={{0,8},{4,12},{8,0},{12,4},{16,24},{20,28},{24,16},{28,20},{1,9},{5... | collective-permute-start | bytes 393224 | tf_op jit(solution)/shard_map/ppermute | solution.py:415
  71.9 10.7 %collective-permute-start.11 = (f32[256,128]{1,0:T(8,128)S(1)}, f32[256,128]{1,0:T(8,128)S(1)}, u32[]{:S(2)}, u32[]{:S(2)}) collective-permute-start(f32[256,128]{1,0:T(8,128)S(1)} %get-tuple-element.39), channel_id=1, source_target_pairs={{0,12},{4,8},{8,4},{12,0},{16,28},{20,24},{24,20},{28,16},{1,13},{... | collective-permute-start | bytes 393224 | tf_op jit(solution)/shard_map/ppermute | solution.py:415
  74.0 29.7 %collective-permute-start.12 = (f32[256,128]{1,0:T(8,128)S(1)}, f32[256,128]{1,0:T(8,128)S(1)}, u32[]{:S(2)}, u32[]{:S(2)}) collective-permute-start(f32[256,128]{1,0:T(8,128)S(1)} %get-tuple-element.40), channel_id=1, source_target_pairs={{0,16},{4,20},{8,24},{12,28},{16,0},{20,4},{24,8},{28,12},{1,17},{... | collective-permute-start | bytes 393224 | tf_op jit(solution)/shard_map/ppermute | solution.py:415
  75.1 28.6 %collective-permute-start.13 = (f32[256,128]{1,0:T(8,128)S(1)}, f32[256,128]{1,0:T(8,128)S(1)}, u32[]{:S(2)}, u32[]{:S(2)}) collective-permute-start(f32[256,128]{1,0:T(8,128)S(1)} %get-tuple-element.41), channel_id=1, source_target_pairs={{0,20},{4,16},{8,28},{12,24},{16,4},{20,0},{24,12},{28,8},{1,21},{... | collective-permute-start | bytes 393224 | tf_op jit(solution)/shard_map/ppermute | solution.py:415
  77.8 25.9 %collective-permute-start.14 = (f32[256,128]{1,0:T(8,128)S(1)}, f32[256,128]{1,0:T(8,128)S(1)}, u32[]{:S(2)}, u32[]{:S(2)}) collective-permute-start(f32[256,128]{1,0:T(8,128)S(1)} %get-tuple-element.42), channel_id=1, source_target_pairs={{0,24},{4,28},{8,16},{12,20},{16,8},{20,12},{24,0},{28,4},{1,25},{... | collective-permute-start | bytes 393224 | tf_op jit(solution)/shard_map/ppermute | solution.py:415
  80.6 23.1 %collective-permute-start.15 = (f32[256,128]{1,0:T(8,128)S(1)}, f32[256,128]{1,0:T(8,128)S(1)}, u32[]{:S(2)}, u32[]{:S(2)}) collective-permute-start(f32[256,128]{1,0:T(8,128)S(1)} %get-tuple-element.43), channel_id=1, source_target_pairs={{0,28},{4,24},{8,20},{12,16},{16,12},{20,8},{24,4},{28,0},{1,29},{... | collective-permute-start | bytes 393224 | tf_op jit(solution)/shard_map/ppermute | solution.py:415
  82.6 21.1 %collective-permute-start.9 = (f32[256,128]{1,0:T(8,128)S(1)}, f32[256,128]{1,0:T(8,128)S(1)}, u32[]{:S(2)}, u32[]{:S(2)}) collective-permute-start(f32[256,128]{1,0:T(8,128)S(1)} %get-tuple-element.37), channel_id=1, source_target_pairs={{0,4},{4,0},{8,12},{12,8},{16,20},{20,16},{24,28},{28,24},{1,5},{5... | collective-permute-start | bytes 393224 | tf_op jit(solution)/shard_map/ppermute | solution.py:415

commit v3 on v1

--- a/solution.py
+++ b/solution.py
@@ -23,6 +23,7 @@
 HALO = STEPS
 LANES = 128
 VMEM_LIMIT = 48 * 1024 * 1024
+PACK_LIMIT = 62 * 1024 * 1024
 
 
 def params():
@@ -41,33 +42,73 @@
     return density_ref if field == 0 else velocity_ref.at[field - 1]
 
 
-def pack_kernel(density_ref, velocity_ref, rows_ref):
+def pack_kernel(density_ref, velocity_ref, *refs):
+    *chunk_refs, rows_ref, field_refs, arrived = refs
     cells, polar, radial = density_ref.shape
     groups = polar // INNER
+    per_column = FIELDS * groups
+    stride = radial // len(chunk_refs) * per_column
+    place = lax.axis_index("phi")
+    copies = [
+        pltpu.make_async_copy(field_ref(density_ref, velocity_ref, field), field_refs.at[field], arrived.at[field])
+        for field in range(FIELDS)
+    ]
+    for copy in copies:
+        copy.start()
     for field in range(FIELDS):
-        source = field_ref(density_ref, velocity_ref, field)
+        copies[field].wait()
         for group in range(groups):
-            block = source[:, pl.ds(group, INNER, stride=groups), :]
+            block = field_refs[field, :, pl.ds(group, INNER, stride=groups), :]
             turned = block.reshape(cells * INNER, radial).T
-            rows_ref[pl.ds(field * groups + group, radial, stride=FIELDS * groups), :] = turned
-
-
-def unpack_kernel(rows_ref, density_ref, velocity_ref):
+            rows_ref[pl.ds(field * groups + group, radial, stride=per_column), :] = turned
+    for j, chunk_ref in enumerate(chunk_refs):
+        chunk_ref[...] = rows_ref[pl.ds(pl.multiple_of(partner(place, j, len(chunk_refs)) * stride, stride), stride), :]
+
+
+def halo_kernel(cycle, columns, shift_ref, frac_ref, *refs):
+    chunk_refs, piece_refs = refs[:cycle], refs[cycle:]
+    rows = chunk_refs[0].shape[0]
+    edge = HALO * rows // columns
+    place = lax.axis_index("phi")
+    sub = lax.broadcasted_iota(jnp.int32, (8, LANES), 0)
+    odd = place % 2
+    for ref, upper in zip(piece_refs, (odd == 0, odd == 1)):
+        at = pl.multiple_of(jnp.where(upper, rows - edge, 0), 8)
+        for j in range(cycle):
+            ref[pl.ds(partner(place, j, cycle), edge, stride=cycle), :] = chunk_refs[j][pl.ds(at, edge), :]
+        band = (place * columns + jnp.where(upper, columns - 1, 0)) // BAND
+        ref[pl.ds(edge * cycle, 8), :] = jnp.where(sub == 0, shift_ref[band].astype(jnp.float32), frac_ref[band])
+
+
+def unpack_kernel(cycle, cuts, *refs):
+    *chunk_refs, density_ref, velocity_ref, rows_ref, field_refs, leaving = refs
+    first_refs, rest_refs = chunk_refs[:cycle], chunk_refs[cycle:]
     cells, polar, radial = density_ref.shape
     groups = polar // INNER
+    per_column = FIELDS * groups
+    stride = radial // cycle * per_column
+    place = lax.axis_index("phi")
+    rest = iter(rest_refs)
+    for j, cut in enumerate(cuts):
+        at = partner(place, j, cycle) * stride
+        rows_ref[pl.ds(pl.multiple_of(at, per_column), cut), :] = first_refs[j][pl.ds(0, cut), :]
+        if cut < stride:
+            rows_ref[pl.ds(pl.multiple_of(at + cut, per_column), stride - cut), :] = next(rest)[...]
+    copies = []
     for field in range(FIELDS):
-        target = field_ref(density_ref, velocity_ref, field)
         for group in range(groups):
-            turned = rows_ref[pl.ds(field * groups + group, radial, stride=FIELDS * groups), :]
+            turned = rows_ref[pl.ds(field * groups + group, radial, stride=per_column), :]
             block = turned.T.reshape(cells, INNER, radial)
-            target[:, pl.ds(group, INNER, stride=groups), :] = block
-
-
-def evolve_kernel(cells, cycle, columns, nrad, groups, swap, shift_ref, frac_ref, place_ref, tilt_ref, in_ref, out_ref, light_ref, work_ref, lit_ref):
-    extended = columns + 2 * HALO
-    per_column = FIELDS * groups
-    first = place_ref[0]
-    first_global = place_ref[1]
+            field_refs[field, :, pl.ds(group, INNER, stride=groups), :] = block
+        copy = pltpu.make_async_copy(field_refs.at[field], field_ref(density_ref, velocity_ref, field), leaving.at[field])
+        copy.start()
+        copies.append(copy)
+    for copy in copies:
+        copy.wait()
+
+
+def stepper(cells, cycle, columns, nrad, groups, band_of):
+    first_global = (lax.axis_index("row") * cycle + lax.axis_index("phi")) * columns
     lane = lax.broadcasted_iota(jnp.int32, (cycle, LANES), 1)
     inner = lane % INNER
 
@@ -117,14 +158,12 @@
         return pend, face_part(cons, prim[1], 1, -1.0), face_part(cons, prim[1], 1, 1.0)
 
     def combine(x, y, sign):
-        return [[p + sign * q for p, q in zip(a, b)] for a, b in zip(x, y)]
+        return [[p + q if sign > 0 else p - q for p, q in zip(a, b)] for a, b in zip(x, y)]
 
     def finish(fresh, col):
         number = first_global + col - HALO
         valid = (number >= 0) & (number < nrad)
-        band = (first + col - HALO + BAND) // BAND
-        shift = shift_ref[band]
-        weight = frac_ref[band]
+        shift, weight = band_of(col)
         turn = shift // cells
         step = INNER * (shift % cells)
         inside = lane >= step
@@ -154,31 +193,101 @@
             write(col - 1, finish(combine(pend, a_rad, -1.0), col - 1))
             return combine(fresh_pend, before, 1.0), b_rad
 
-        pend, _ = lax.fori_loop(low + 2, high - 1, body, (pend, after))
+        pend, _ = lax.fori_loop(low + 2, high - 1, body, (pend, after), unroll=4)
         prim = read(high - 1)
         a_rad = face_part(conserved(prim), prim[1], 1, -1.0)
         write(high - 2, finish(combine(pend, a_rad, -1.0), high - 2))
 
-    def read_input(col):
-        return [
-            [in_ref[pl.ds(col * per_column + k * groups + g, cycle, stride=extended * per_column), :] for g in range(groups)]
-            for k in range(FIELDS)
-        ]
-
-    def read_work(col):
-        return [[work_ref[col * per_column + k * groups + g] for g in range(groups)] for k in range(FIELDS)]
-
-    def write_work(col, prim):
-        for k in range(FIELDS):
-            for g in range(groups):
-                work_ref[col * per_column + k * groups + g] = prim[k][g]
-
-    def write_output(col, prim):
-        own = col - HALO
-        for k in range(FIELDS):
-            for g in range(groups):
-                out_ref[pl.ds(own * per_column + k * groups + g, cycle, stride=columns * per_column), :] = prim[k][g]
-        dtau = [(KAPPA / (groups * INNER)) * r for r in prim[0]]
+    return step_columns
+
+
+def block_rows(cycle, groups):
+    def at(col, k, g):
+        return pl.ds(pl.multiple_of(((col * FIELDS + k) * groups + g) * cycle, cycle), cycle)
+
+    def reader(ref, first=0):
+        return lambda col: [[ref[at(col - first, k, g), :] for g in range(groups)] for k in range(FIELDS)]
+
+    def writer(ref, first=0):
+        def write(col, prim):
+            for k in range(FIELDS):
+                for g in range(groups):
+                    ref[at(col - first, k, g), :] = prim[k][g]
+
+        return write
+
+    return at, reader, writer
+
+
+def inner_kernel(cells, cycle, columns, nrad, groups, shift_ref, frac_ref, *refs):
+    chunk_refs, (work_ref, own_ref) = refs[:cycle], refs[cycle:]
+    per_column = FIELDS * groups
+    _, reader, writer = block_rows(cycle, groups)
+    place = lax.axis_index("phi")
+    for j in range(cycle):
+        own_ref[pl.ds(partner(place, j, cycle), columns * per_column, stride=cycle), :] = chunk_refs[j][...]
+
+    def band_of(col):
+        band = (place * columns + col - HALO) // BAND
+        return shift_ref[band], frac_ref[band]
+
+    step_columns = stepper(cells, cycle, columns, nrad, groups, band_of)
+    if columns > 2:
+        step_columns(reader(own_ref, HALO), writer(work_ref, HALO + 1), HALO, HALO + columns)
+
+
+def outer_kernel(cells, cycle, columns, nrad, groups, cuts, shift_ref, frac_ref, tilt_ref, first_ref, second_ref, inner_ref, *refs):
+    chunk_refs, refs = refs[:cycle], refs[cycle:]
+    *out_refs, strip_ref, work_ref, done_ref = refs
+    first_refs, rest_refs = out_refs[:cycle], out_refs[cycle:]
+    swap = first_refs[0].shape[0] > cuts[0]
+    per_column = FIELDS * groups
+    edge = HALO * per_column * cycle
+    at, reader, writer = block_rows(cycle, groups)
+    place = lax.axis_index("phi")
+    first_global = (lax.axis_index("row") * cycle + place) * columns
+
+    odd = place % 2 == 1
+
+    def carried(rows):
+        return rows.astype(jnp.int32)[0, 0], rows[1, 0]
+
+    tails = [ref[pl.ds(edge, 8), :] for ref in (first_ref, second_ref)]
+    below = carried(jnp.where(odd, tails[0], tails[1]))
+    above = carried(jnp.where(odd, tails[1], tails[0]))
+
+    def band_of(col):
+        band = jnp.clip((place * columns + col - HALO) // BAND, 0, shift_ref.shape[0] - 1)
+        low, high = col < HALO, col >= HALO + columns
+        shift = jnp.where(low, below[0], jnp.where(high, above[0], shift_ref[band]))
+        weight = jnp.where(low, below[1], jnp.where(high, above[1], frac_ref[band]))
+        return shift, weight
+
+    step_columns = stepper(cells, cycle, columns, nrad, groups, band_of)
+    strip_ref[pl.ds(pl.multiple_of(jnp.where(odd, 0, 3 * edge), 8), edge), :] = first_ref[pl.ds(0, edge), :]
+    strip_ref[pl.ds(pl.multiple_of(jnp.where(odd, 3 * edge, 0), 8), edge), :] = second_ref[pl.ds(0, edge), :]
+    rows = columns * per_column
+    for j in range(cycle):
+        slab = partner(place, j, cycle)
+        strip_ref[pl.ds(edge + slab, edge // cycle, stride=cycle), :] = chunk_refs[j][pl.ds(0, edge // cycle), :]
+        strip_ref[pl.ds(2 * edge + slab, edge // cycle, stride=cycle), :] = chunk_refs[j][pl.ds(rows - edge // cycle, edge // cycle), :]
+    kept = (columns - 2) * per_column * cycle
+    if kept:
+        work_ref[pl.ds((HALO + 1) * per_column * cycle, kept), :] = inner_ref[pl.ds(0, kept), :]
+    step_columns(reader(strip_ref), writer(work_ref), 0, 2 * HALO)
+    step_columns(reader(strip_ref, columns - 2 * HALO), writer(work_ref), columns, columns + 2 * HALO)
+    step_columns(reader(work_ref), writer(done_ref, HALO), 1, columns + 2 * HALO - 1)
+    rest = iter(rest_refs)
+    for j, cut in enumerate(cuts):
+        slab = partner(place, j, cycle)
+        first_refs[j][pl.ds(0, cut), :] = done_ref[pl.ds(slab, cut, stride=cycle), :]
+        if cut < rows:
+            next(rest)[...] = done_ref[pl.ds(cut * cycle + slab, rows - cut, stride=cycle), :]
+    lane = lax.broadcasted_iota(jnp.int32, (cycle, LANES), 1)
+    inner = lane % INNER
+
+    def column_light(own):
+        dtau = [(KAPPA / (groups * INNER)) * done_ref[at(own, 0, g), :] for g in range(groups)]
         total = dtau[0]
         for d in dtau[1:]:
             total = total + d
@@ -194,27 +303,25 @@
             light = light + pltpu.roll(light, LANES - d, 1)
         number = jnp.full((cycle, LANES), first_global + own, jnp.int32).astype(jnp.float32)
         radius = R_INNER + (number + 0.5) * (1.0 - R_INNER) / nrad
-        light = light * (1.0 / jnp.sqrt(radius))
-        slot = own % INNER
-        light = pltpu.roll(light, slot, 1)
-        lit_ref[own // INNER] = jnp.where(inner == slot, light, lit_ref[own // INNER])
-
-    lit_ref[...] = jnp.zeros_like(lit_ref)
-    step_columns(read_input, write_work, 0, extended)
-    step_columns(read_work, write_output, 1, extended - 1)
-    if swap:
-        sub = lax.broadcasted_iota(jnp.int32, (cycle, LANES), 0)
-        for h in range(columns // INNER):
-            x = lit_ref[h]
+        return pltpu.roll(light * (1.0 / jnp.sqrt(radius)), own % INNER, 1)
+
+    for h in range(-(-columns // INNER)):
+        slots = range(min(INNER, columns - h * INNER))
+        x = jnp.zeros((cycle, LANES), jnp.float32)
+        for slot, light in [(slot, column_light(h * INNER + slot)) for slot in slots]:
+            x = jnp.where(inner == slot, light, x)
+        if swap:
+            sub = lax.broadcasted_iota(jnp.int32, (cycle, LANES), 0)
             for d in (1, 2, 4):
                 low_sub = (sub & d) == 0
                 low_lane = (lane & d) == 0
                 ahead = pltpu.roll(pltpu.roll(x, cycle - d, 0), d, 1)
                 back = pltpu.roll(pltpu.roll(x, d, 0), LANES - d, 1)
                 x = jnp.where(low_sub == low_lane, x, jnp.where(low_sub, ahead, back))
-            light_ref[pl.ds(h * INNER, INNER), :] = x
-    else:
-        light_ref[...] = lit_ref[...]
+            for ref, cut in zip(first_refs, cuts):
+                ref[pl.ds(cut + h * INNER, INNER), :] = x
+        else:
+            rest_refs[0][h] = x
 
 
 def pixel_tiles(first_row, rows_dev, npix, nphi, nrad):
@@ -250,13 +357,16 @@
     return -(-int(np.ceil(span) + 2) // 8) * 8
 
 
-def image_kernel(cells, cycle, nphi, nrad, rows, tile_rows, across, start_ref, window_ref, table_ref, spot_ref, frac_ref, vpos_ref, out_ref, turned_ref, wide_ref):
+def image_kernel(cells, cycle, nphi, nrad, rows, tile_rows, across, start_ref, window_ref, spot_ref, frac_ref, vpos_ref, *refs):
+    *table_refs, out_ref, turned_ref, wide_ref = refs
     blocks = nrad // LANES
-    for k in range(blocks):
-        for l in range(nphi // LANES):
-            turned_ref[pl.ds(k * nphi + l * LANES, LANES), :] = table_ref[
-                pl.ds(k * LANES, LANES), pl.ds(l * LANES, LANES)
-            ].T
+    each = blocks // len(table_refs)
+    for j, table_ref in enumerate(table_refs):
+        for k in range(each):
+            block = partner(lax.axis_index("row"), j, len(table_refs)) * each + k
+            for l in range(nphi // LANES):
+                at = pl.multiple_of(block * nphi + l * LANES, LANES)
+                turned_ref[pl.ds(at, LANES), :] = table_ref[pl.ds(k * LANES, LANES), pl.ds(l * LANES, LANES)].T
     half = LANES // 2
     windows = 2 * (blocks + 2) - 1
     tall = wide_ref.shape[0] // windows
@@ -271,7 +381,7 @@
             wide_ref[pl.ds((8 + s * cells) * windows + w, cells, stride=windows), :] = piece
         return carry
 
-    lax.fori_loop(0, cycle, fill, 0)
+    lax.fori_loop(0, cycle, fill, 0, unroll=8)
     pad = tall - nphi - 8
     wide_ref[pl.ds(0, 8 * windows), :] = wide_ref[pl.ds(nphi * windows, 8 * windows), :]
     wide_ref[pl.ds((nphi + 8) * windows, pad * windows), :] = wide_ref[pl.ds(8 * windows, pad * windows), :]
@@ -293,14 +403,17 @@
             weight = jnp.maximum(0.0, 1.0 - jnp.abs((sub + r).astype(jnp.float32) - vpos))
             part = weight * (low + frac * (high - low))
             total = part if total is None else total + part
+        return total
+
+    def group(index, carry):
+        parts = [one_tile(index * 8 + t) for t in range(8)]
         for d in (4, 2, 1):
-            total = total + pltpu.roll(total, d, 0)
-        return total
-
-    def group(index, carry):
-        result = jnp.zeros((8, LANES), jnp.float32)
-        for t in range(8):
-            result = jnp.where(sub == t, one_tile(index * 8 + t), result)
+            upper = (sub & d) != 0
+            parts = [
+                jnp.where(upper, b, a) + jnp.where(upper, pltpu.roll(b, d, 0), pltpu.roll(a, 8 - d, 0))
+                for a, b in zip(parts[:d], parts[d:])
+            ]
+        result = parts[0]
         if tile_rows == 8:
             width = LANES // 8
             for d in (1, 2, 4):
@@ -315,10 +428,10 @@
             out_ref[pl.ds(pl.multiple_of(index * 8, 8), 8), :] = result
         return carry
 
-    lax.fori_loop(0, spot_ref.shape[0] // 8, group, 0)
-
-
-def draw_image(table, geometry, cells, cycle, rows_dev, npix, nphi, nrad):
+    lax.fori_loop(0, spot_ref.shape[0] // 8, group, 0, unroll=min(8, spot_ref.shape[0] // 8))
+
+
+def draw_image(tables, geometry, cells, cycle, rows_dev, npix, nphi, nrad):
     start, window, spot, frac_u, vpos = geometry
     tiles = spot.shape[0]
     tile_rows = min(8, rows_dev)
@@ -330,7 +443,7 @@
     image = pl.pallas_call(
         functools.partial(image_kernel, cells, cycle, nphi, nrad, rows, tile_rows, across),
         out_shape=jax.ShapeDtypeStruct(shape, jnp.float32),
-        in_specs=smem(2) + vmem(4),
+        in_specs=smem(2) + vmem(3 + len(tables)),
         out_specs=pl.BlockSpec(memory_space=pltpu.VMEM),
         scratch_shapes=[
             pltpu.VMEM((nphi * (nrad // LANES), LANES), jnp.float32),
@@ -338,11 +451,49 @@
         ],
         compiler_params=params(),
         name="image",
-    )(start, window, table, spot, frac_u, vpos)
+    )(start, window, spot, frac_u, vpos, *tables)
     if tile_rows == 8:
         return image
     image = image.reshape(rows_dev // tile_rows, across, tile_rows, tile_cols)
     return jnp.swapaxes(image, 1, 2).reshape(rows_dev, npix)
+
+
+def partner(place, index, size):
+    return place ^ ((size - index) % size)
+
+
+def swapped(piece, axis, index):
+    size = lax.axis_size(axis)
+    return lax.ppermute(piece, axis, [(p, partner(p, index, size)) for p in range(size)])
+
+
+def exchange(chunks, axis):
+    size = lax.axis_size(axis)
+    if size > INNER:
+        place, every = lax.axis_index(axis), jnp.arange(size)
+        sent = jnp.stack(chunks)[(size - (place ^ every)) % size]
+        got = lax.all_to_all(sent, axis, 0, 0, tiled=True)[partner(place, every, size)]
+        return [got[i] for i in range(size)]
+    return [chunks[0]] + [swapped(chunks[i], axis, i) for i in range(1, size)]
+
+
+def gather_kernel(cuts, *refs):
+    *piece_refs, out_ref = refs
+    size = len(cuts)
+    count = out_ref.shape[0] // size
+    for j, cut in enumerate(cuts):
+        out_ref[pl.ds(pl.multiple_of(partner(lax.axis_index("phi"), j, size) * count, count), count), :] = piece_refs[j][pl.ds(cut, count), :]
+
+
+def neighbour_columns(first, second):
+    cycle, bands = lax.axis_size("phi"), lax.axis_size("row")
+    order = [q * bands + r for r in range(bands) for q in range(cycle)]
+    pairs = list(zip(order[:-1], order[1:]))
+
+    def both_ways(piece, chosen):
+        return lax.ppermute(piece, ("phi", "row"), chosen + [(j, i) for i, j in chosen])
+
+    return both_ways(first, pairs[::2]), both_ways(second, pairs[1::2])
 
 
 def body(density, velocity, shifts, fractions):
@@ -352,78 +503,114 @@
     groups = polar // INNER
     per_column = FIELDS * groups
     columns = radial // cycle
-    extended = columns + 2 * HALO
     nphi = cells * cycle
     nrad = radial * bands
     place = lax.axis_index("phi")
     row = lax.axis_index("row")
-
-    rows = pl.pallas_call(
+    block = (FIELDS, cells, polar, radial)
+    hbm = pl.BlockSpec(memory_space=pltpu.HBM)
+
+    def f32(*shape):
+        return jax.ShapeDtypeStruct(shape, jnp.float32)
+
+    chunk = f32(columns * per_column, LANES)
+    chunks = pl.pallas_call(
         pack_kernel,
-        out_shape=jax.ShapeDtypeStruct((radial * per_column, LANES), jnp.float32),
-        in_specs=vmem(2),
-        out_specs=pl.BlockSpec(memory_space=pltpu.VMEM),
-        compiler_params=params(),
+        out_shape=[chunk] * cycle,
+        in_specs=[hbm] * 2,
+        out_specs=vmem(cycle),
+        scratch_shapes=[
+            pltpu.VMEM((radial * per_column, LANES), jnp.float32),
+            pltpu.VMEM(block, jnp.float32),
+            pltpu.SemaphoreType.DMA((FIELDS,)),
+        ],
+        compiler_params=pltpu.CompilerParams(vmem_limit_bytes=PACK_LIMIT),
         name="pack",
     )(density, velocity)
-    edge = HALO * per_column
-
-    def with_band(block, band):
-        extra = jnp.stack([shifts[band].astype(jnp.float32), fractions[band]])
-        return jnp.concatenate([block, jnp.pad(extra[:, None], ((0, 6), (0, LANES - 1)))])
-
-    left = lax.ppermute(with_band(rows[-edge:], -1), "row", [(i, i + 1) for i in range(bands - 1)])
-    right = lax.ppermute(with_band(rows[:edge], 0), "row", [(i + 1, i) for i in range(bands - 1)])
-    ext_shift = jnp.concatenate([left[edge, :1].astype(jnp.int32), shifts, right[edge, :1].astype(jnp.int32)])
-    ext_frac = jnp.concatenate([left[edge + 1, :1], fractions, right[edge + 1, :1]])
-    rows = jnp.concatenate([left[:edge], rows, right[:edge]])
-    stride = columns * per_column
-    chunks = jnp.stack([rows[q * stride:q * stride + extended * per_column] for q in range(cycle)])
-    ring = lax.all_to_all(chunks, "phi", 0, 0, tiled=True)
-
-    swap = cycle == INNER and columns % INNER == 0
-    slots = -(-columns // INNER)
+    ring = exchange(chunks, "phi")
+
+    column_rows = per_column * cycle
+    edge = HALO * column_rows
+    pieces = pl.pallas_call(
+        functools.partial(halo_kernel, cycle, columns),
+        out_shape=[f32(edge + 8, LANES)] * 2,
+        in_specs=smem(2) + vmem(cycle),
+        out_specs=vmem(2),
+        compiler_params=params(),
+        name="halo",
+    )(shifts, fractions, *ring)
+    first, second = neighbour_columns(*pieces)
+    inner = pl.pallas_call(
+        functools.partial(inner_kernel, cells, cycle, columns, nrad, groups),
+        out_shape=f32(max(columns - 2, 1) * column_rows, LANES),
+        in_specs=smem(2) + vmem(cycle),
+        out_specs=pl.BlockSpec(memory_space=pltpu.VMEM),
+        scratch_shapes=[pltpu.VMEM((columns * column_rows, LANES), jnp.float32)],
+        compiler_params=params(),
+        name="inner",
+    )(shifts, fractions, *ring)
     theta = (np.arange(polar) + 0.5) / polar
     tilt = (1.0 + 0.5 * np.cos(np.pi * theta)).reshape(INNER, groups).T
     tilt = jnp.asarray(np.tile(tilt, (1, LANES // INNER)), jnp.float32)
-    where = jnp.stack([place * columns, row * radial + place * columns])
-    rows, light = pl.pallas_call(
-        functools.partial(evolve_kernel, cells, cycle, columns, nrad, groups, swap),
-        out_shape=(
-            jax.ShapeDtypeStruct((cycle * columns * per_column, LANES), jnp.float32),
-            jax.ShapeDtypeStruct((columns, LANES) if swap else (slots, cycle, LANES), jnp.float32),
-        ),
-        in_specs=smem(3) + vmem(2),
-        out_specs=tuple(vmem(2)),
+    swap = cycle == INNER and columns % INNER == 0
+    rows = columns * per_column
+    cuts = [rows] * cycle
+    if swap:
+        for j in range(1, cycle // 2 + 1):
+            cuts[j] = columns // 2 * per_column
+        extra = [f32(rows - cut, LANES) for cut in cuts if cut < rows]
+    else:
+        slots = -(-columns // INNER)
+        extra = [f32(slots, cycle, LANES)]
+    out = pl.pallas_call(
+        functools.partial(outer_kernel, cells, cycle, columns, nrad, groups, cuts),
+        out_shape=[f32(cut + (columns if swap else 0), LANES) for cut in cuts] + extra,
+        in_specs=smem(2) + vmem(4 + cycle),
+        out_specs=vmem(cycle + len(extra)),
         scratch_shapes=[
-            pltpu.VMEM((extended * per_column, cycle, LANES), jnp.float32),
-            pltpu.VMEM((slots, cycle, LANES), jnp.float32),
+            pltpu.VMEM((4 * edge, LANES), jnp.float32),
+            pltpu.VMEM(((columns + 2 * HALO) * column_rows, LANES), jnp.float32),
+            pltpu.VMEM((columns * column_rows, LANES), jnp.float32),
         ],
         compiler_params=params(),
-        name="evolve",
-    )(ext_shift, ext_frac, where, tilt, ring.reshape(cycle * extended * per_column, LANES))
-    if not swap:
-        light = light.reshape(slots, cycle, cells, INNER).transpose(0, 3, 2, 1).reshape(slots * INNER, nphi)[:columns]
-
-    table = lax.all_gather(light, "phi", axis=0, tiled=True)
-    table = lax.all_gather(table, "row", axis=0, tiled=True)
-    back = lax.all_to_all(rows.reshape(cycle, columns * per_column, LANES), "phi", 0, 0, tiled=True)
-    density_out, velocity_out = pl.pallas_call(
-        unpack_kernel,
-        out_shape=(
-            jax.ShapeDtypeStruct(density.shape, jnp.float32),
-            jax.ShapeDtypeStruct(velocity.shape, jnp.float32),
-        ),
-        in_specs=vmem(1),
-        out_specs=tuple(vmem(2)),
-        compiler_params=params(),
-        name="unpack",
-    )(back.reshape(radial * per_column, LANES))
+        name="outer",
+    )(shifts, fractions, tilt, first, second, inner, *ring)
+    back = exchange(out[:cycle], "phi")
+    if swap:
+        table = pl.pallas_call(
+            functools.partial(gather_kernel, cuts),
+            out_shape=f32(radial, nphi),
+            in_specs=vmem(cycle),
+            out_specs=pl.BlockSpec(memory_space=pltpu.VMEM),
+            compiler_params=params(),
+            name="gather",
+        )(*back)
+        back += [
+            swapped(piece, "phi", j) for piece, j in zip(out[cycle:], [j for j in range(cycle) if cuts[j] < rows])
+        ]
+    else:
+        light = out[cycle].reshape(slots, cycle, cells, INNER).transpose(0, 3, 2, 1).reshape(slots * INNER, nphi)[:columns]
+        table = lax.all_gather(light, "phi", axis=0, tiled=True)
+    tables = exchange([table] * bands, "row")
 
     rows_dev = NPIX // (cycle * bands)
     first_row = (place * bands + row) * rows_dev
     geometry = pixel_tiles(first_row, rows_dev, NPIX, nphi, nrad)
-    image = draw_image(table, geometry, cells, cycle, rows_dev, NPIX, nphi, nrad)
+    image = draw_image(tables, geometry, cells, cycle, rows_dev, NPIX, nphi, nrad)
+    density_out, velocity_out = pl.pallas_call(
+        functools.partial(unpack_kernel, cycle, cuts),
+        out_shape=(f32(*density.shape), f32(*velocity.shape)),
+        in_specs=vmem(len(back)),
+        out_specs=[hbm] * 2,
+        scratch_shapes=[
+            pltpu.VMEM((radial * per_column, LANES), jnp.float32),
+            pltpu.VMEM(block, jnp.float32),
+            pltpu.SemaphoreType.DMA((FIELDS,)),
+        ],
+        compiler_params=params(),
+        name="unpack",
+    )(*back)
+
     return (density_out, velocity_out, image)
 
 

time: 144 us -> 81.1 us (0.56)
  blocking collectives: 50.5 us -> 0 us
  starting transfers between devices: 14.6 us -> 47.7 us
  Pallas kernels: 30.5 us -> 16.2 us
  waiting for transfers between devices: 28.2 us -> 14.6 us
  local copies, waits for them, and re-layouts: 10.1 us -> 0.02 us
  other arithmetic: 5.92 us -> 1.65 us
  between operations: 3.34 us -> 0.84 us
    all_gather x2 -> x0, blocking collectives: 50.5 us -> none  [the longest x1 44.8 us: body(): table = lax.all_gather(light, 'phi', axis=0, tiled=True)]
    ppermute x2 -> x23, starting transfers between devices: 3.63 us -> 47.7 us  [the longest x21 46.3 us: swapped(): lax.ppermute(piece, axis, [(p, partner(p, index, size)) for p in range(si...]
    all_to_all x2 -> x0, waiting for transfers between devices: 28.2 us -> none  [the longest x1 28.2 us: body(): ring = lax.all_to_all(chunks, 'phi', 0, 0, tiled=True)]
    ppermute x2 -> x23, waiting for transfers between devices: 0.01 us -> 14.6 us  [the longest x21 14.1 us: swapped(): lax.ppermute(piece, axis, [(p, partner(p, index, size)) for p in range(si...]
    all_to_all x2 -> x0, starting transfers between devices: 11 us -> none  [the longest x1 6.77 us: body(): ring = lax.all_to_all(chunks, 'phi', 0, 0, tiled=True)]
    pallas_call x1, Pallas kernels: 12.6 us -> 4.64 us  [draw_image(): pl.pallas_call(functools.partial(image_kernel, cells, cycle, nphi, nrad,...]
    pallas_call x3 -> x6, Pallas kernels: 17.8 us -> 11.5 us  [the longest x1 4.39 us: body(): pl.pallas_call(functools.partial(outer_kernel, cells, cycle, columns, nra...]
    unnamed x16 -> x8, local copies, waits for them, and re-layouts: 6.16 us -> 0.02 us
  transfers between devices with their start and end apart: 4 -> 23, of which waited for: 1 -> 10; matrix products, arithmetic and copies ran while one was open for 6% -> 2% of each run, Pallas kernels for 9% -> 5%
where the time goes in v3:
time: 81.1 us; the launch traced here: 80.9 us
  starting transfers between devices  47.7 us (59%)
  Pallas kernels  16.2 us (20%)
  waiting for transfers between devices  14.6 us (18%)
  other arithmetic  1.65 us (2%)
  between operations  0.84 us (1%)
    ppermute x21, starting transfers between devices, swapped(): lax.ppermute(piece, axis, [(p, partner(p, index, size)) for p in range(si...  46.3 us
    ppermute x21, waiting for transfers between devices, swapped(): lax.ppermute(piece, axis, [(p, partner(p, index, size)) for p in range(si...  14.1 us
    pallas_call x1, Pallas kernels, draw_image(): pl.pallas_call(functools.partial(image_kernel, cells, cycle, nphi, nrad,...  4.64 us
    pallas_call x1, Pallas kernels, body(): pl.pallas_call(functools.partial(outer_kernel, cells, cycle, columns, nra...  4.39 us
    pallas_call x1, Pallas kernels, body(): pl.pallas_call(functools.partial(inner_kernel, cells, cycle, columns, nra...  2.73 us
    pallas_call x1, Pallas kernels, body(): pl.pallas_call(pack_kernel, out_shape=[chunk] * cycle, in_specs=[hbm] * 2...  2.54 us
  transfers between devices with their start and end apart: 23, of which 10 were waited for; matrix products, arithmetic and copies ran while one was open for 2% of the time, Pallas kernels for 5%

profile of v3, /device:TPU:0, one launch (start us, length us, event | category | flops | bytes accessed | tf_op | source)
XLA Modules:
  0.0 80.9 jit_solution(5977837646611027464)
XLA Ops:
  0.6 2.5 %pack.1 = (f32[256,128]{1,0:T(8,128)}, f32[256,128]{1,0:T(8,128)}, f32[256,128]{1,0:T(8,128)}, f32[256,128]{1,0:T(8,128)}, f32[256,128]{1,0:T(8,128)}, /*index=5...) custom-call(f32[16,32,128]{2,1,0:T(8,128)} %density_ref.1, f32[3,16,32,128]{3,2,1,0:T(8,128)} %velocity_ref.1), custom_call_target="tpu_custom_call" | custom-call | tf_op jit(solution)/shard_map/pack/pallas_call | solution.py:517
  3.2 0.0 copy-start
  3.2 6.0 %collective-permute-start = (f32[256,128]{1,0:T(8,128)}, f32[256,128]{1,0:T(8,128)S(1)}, u32[]{:S(2)}, u32[]{:S(2)}) collective-permute-start(f32[256,128]{1,0:T(8,128)} %get-tuple-element.28), channel_id=1, source_target_pairs={{0,28},{4,24},{8,20},{12,16},{16,12},{20,8},{24,4},{28,0},{1,29},{... | collective-permute-start | bytes 393224 | tf_op jit(solution)/shard_map/ppermute | solution.py:467
  9.2 0.2 collective-permute-start.1
  9.5 0.8 collective-permute-start.2
  10.2 2.0 %collective-permute-start.3 = (f32[256,128]{1,0:T(8,128)}, f32[256,128]{1,0:T(8,128)S(1)}, u32[]{:S(2)}, u32[]{:S(2)}) collective-permute-start(f32[256,128]{1,0:T(8,128)} %get-tuple-element.31), channel_id=1, source_target_pairs={{0,16},{4,20},{8,24},{12,28},{16,0},{20,4},{24,8},{28,12},{1,17},{... | collective-permute-start | bytes 393224 | tf_op jit(solution)/shard_map/ppermute | solution.py:467
  12.2 2.3 %collective-permute-start.4 = (f32[256,128]{1,0:T(8,128)}, f32[256,128]{1,0:T(8,128)S(1)}, u32[]{:S(2)}, u32[]{:S(2)}) collective-permute-start(f32[256,128]{1,0:T(8,128)} %get-tuple-element.32), channel_id=1, source_target_pairs={{0,12},{4,8},{8,4},{12,0},{16,28},{20,24},{24,20},{28,16},{1,13},{... | collective-permute-start | bytes 393224 | tf_op jit(solution)/shard_map/ppermute | solution.py:467
  14.6 0.5 add_reduce_fusion
  15.1 10.1 %collective-permute-start.5 = (f32[256,128]{1,0:T(8,128)}, f32[256,128]{1,0:T(8,128)S(1)}, u32[]{:S(2)}, u32[]{:S(2)}) collective-permute-start(f32[256,128]{1,0:T(8,128)} %get-tuple-element.33), channel_id=1, source_target_pairs={{0,8},{4,12},{8,0},{12,4},{16,24},{20,28},{24,16},{28,20},{1,9},{5... | collective-permute-start | bytes 393224 | tf_op jit(solution)/shard_map/ppermute | solution.py:467
  25.2 0.0 collective-permute-done.1.refs_2_
  25.2 1.4 %collective-permute-start.6 = (f32[256,128]{1,0:T(8,128)}, f32[256,128]{1,0:T(8,128)S(1)}, u32[]{:S(2)}, u32[]{:S(2)}) collective-permute-start(f32[256,128]{1,0:T(8,128)} %get-tuple-element.34), channel_id=1, source_target_pairs={{0,4},{4,0},{8,12},{12,8},{16,20},{20,16},{24,28},{28,24},{1,5},{5... | collective-permute-start | bytes 393224 | tf_op jit(solution)/shard_map/ppermute | solution.py:467
  26.5 0.0 copy-start.2
  26.5 3.5 %collective-permute-done.2.refs_3_ = f32[256,128]{1,0:T(8,128)S(1)} collective-permute-done((f32[256,128]{1,0:T(8,128)}, f32[256,128]{1,0:T(8,128)S(1)}, u32[]{:S(2)}, u32[]{:S(2)}) %collective-permute-start.2) | collective-permute-done | bytes 131104 | tf_op jit(solution)/shard_map/ppermute | solution.py:467
  30.0 1.9 %collective-permute-done.3.refs_4_ = f32[256,128]{1,0:T(8,128)S(1)} collective-permute-done((f32[256,128]{1,0:T(8,128)}, f32[256,128]{1,0:T(8,128)S(1)}, u32[]{:S(2)}, u32[]{:S(2)}) %collective-permute-start.3) | collective-permute-done | bytes 131104 | tf_op jit(solution)/shard_map/ppermute | solution.py:467
  31.9 0.0 collective-permute-done.4.refs_5_
  31.9 1.2 %collective-permute-done.5.refs_6_ = f32[256,128]{1,0:T(8,128)S(1)} collective-permute-done((f32[256,128]{1,0:T(8,128)}, f32[256,128]{1,0:T(8,128)S(1)}, u32[]{:S(2)}, u32[]{:S(2)}) %collective-permute-start.5) | collective-permute-done | bytes 131104 | tf_op jit(solution)/shard_map/ppermute | solution.py:467
  33.1 0.6 halo.1
  33.7 0.7 collective-permute-start.7
  34.4 0.7 collective-permute-start.8
  35.1 0.4 add_subtract_fusion
  35.5 0.0 copy-start.3
  35.5 2.7 %inner.1.inner_ref = f32[1792,128]{1,0:T(8,128)S(1)} custom-call(s32[16]{0:T(128)S(1)} %copy-done.1, f32[16]{0:T(128)S(1)} %copy-done.2, f32[256,128]{1,0:T(8,128)S(1)} %copy-done, f32[256,128]{1,0:T(8,128)S(1)} %collective-permute-done.refs_1_, f32[256,128]{1,0:T(8,128)S(1)} %collective-permute-done.1.refs_2_, ...), custom_call_target="tpu_custom_call" | custom-call | tf_op jit(solution)/shard_map/inner/pallas_call | solution.py:543
  38.3 0.6 collective-permute-done.7.first_ref
  38.8 0.0 collective-permute-done.8.second_ref
  38.8 4.4 %outer.1 = (f32[272,128]{1,0:T(8,128)S(1)}, f32[144,128]{1,0:T(8,128)S(1)}, f32[144,128]{1,0:T(8,128)S(1)}, f32[144,128]{1,0:T(8,128)S(1)}, f32[144,128]{1,0:T(8...) custom-call(s32[16]{0:T(128)S(1)} %copy-done.1, ...), custom_call_target="tpu_custom_call" | custom-call | tf_op jit(solution)/shard_map/outer/pallas_call | solution.py:565
  43.2 5.9 %collective-permute-start.10 = (f32[144,128]{1,0:T(8,128)S(1)}, f32[144,128]{1,0:T(8,128)S(1)}, u32[]{:S(2)}, u32[]{:S(2)}) collective-permute-start(f32[144,128]{1,0:T(8,128)S(1)} %get-tuple-element.39), channel_id=1, source_target_pairs={{0,24},{4,28},{8,16},{12,20},{16,8},{20,12},{24,0},{28,4},{1,25},{... | collective-permute-start | bytes 221192 | tf_op jit(solution)/shard_map/ppermute | solution.py:467
  49.1 0.0 collective-permute-start.11
  49.1 4.8 %collective-permute-start.12 = (f32[144,128]{1,0:T(8,128)S(1)}, f32[144,128]{1,0:T(8,128)S(1)}, u32[]{:S(2)}, u32[]{:S(2)}) collective-permute-start(f32[144,128]{1,0:T(8,128)S(1)} %get-tuple-element.41), channel_id=1, source_target_pairs={{0,16},{4,20},{8,24},{12,28},{16,0},{20,4},{24,8},{28,12},{1,17},{... | collective-permute-start | bytes 221192 | tf_op jit(solution)/shard_map/ppermute | solution.py:467
  54.0 0.4 fusion.2
  54.3 1.5 %collective-permute-start.13 = (f32[272,128]{1,0:T(8,128)S(1)}, f32[272,128]{1,0:T(8,128)S(1)}, u32[]{:S(2)}, u32[]{:S(2)}) collective-permute-start(f32[272,128]{1,0:T(8,128)S(1)} %get-tuple-element.42), channel_id=1, source_target_pairs={{0,12},{4,8},{8,4},{12,0},{16,28},{20,24},{24,20},{28,16},{1,13},{... | collective-permute-start | bytes 417800 | tf_op jit(solution)/shard_map/ppermute | solution.py:467
  55.9 0.0 collective-permute-done.10.refs_2_
  55.9 1.8 %collective-permute-start.14 = (f32[272,128]{1,0:T(8,128)S(1)}, f32[272,128]{1,0:T(8,128)S(1)}, u32[]{:S(2)}, u32[]{:S(2)}) collective-permute-start(f32[272,128]{1,0:T(8,128)S(1)} %get-tuple-element.43), channel_id=1, source_target_pairs={{0,8},{4,12},{8,0},{12,4},{16,24},{20,28},{24,16},{28,20},{1,9},{5... | collective-permute-start | bytes 417800 | tf_op jit(solution)/shard_map/ppermute | solution.py:467
  57.6 1.0 %collective-permute-done.11.refs_3_ = f32[144,128]{1,0:T(8,128)S(1)} collective-permute-done((f32[144,128]{1,0:T(8,128)S(1)}, f32[144,128]{1,0:T(8,128)S(1)}, u32[]{:S(2)}, u32[]{:S(2)}) %collective-permute-start.11) | collective-permute-done | bytes 73760 | tf_op jit(solution)/shard_map/ppermute | solution.py:467
  58.7 1.1 %collective-permute-start.15 = (f32[272,128]{1,0:T(8,128)S(1)}, f32[272,128]{1,0:T(8,128)S(1)}, u32[]{:S(2)}, u32[]{:S(2)}) collective-permute-start(f32[272,128]{1,0:T(8,128)S(1)} %get-tuple-element.44), channel_id=1, source_target_pairs={{0,4},{4,0},{8,12},{12,8},{16,20},{20,16},{24,28},{28,24},{1,5},{5... | collective-permute-start | bytes 417800 | tf_op jit(solution)/shard_map/ppermute | solution.py:467
  59.7 0.9 %collective-permute-done.12.refs_4_ = f32[144,128]{1,0:T(8,128)S(1)} collective-permute-done((f32[144,128]{1,0:T(8,128)S(1)}, f32[144,128]{1,0:T(8,128)S(1)}, u32[]{:S(2)}, u32[]{:S(2)}) %collective-permute-start.12) | collective-permute-done | bytes 73760 | tf_op jit(solution)/shard_map/ppermute | solution.py:467
  60.6 3.1 %collective-permute-start.16 = (f32[128,128]{1,0:T(8,128)S(1)}, f32[128,128]{1,0:T(8,128)S(1)}, u32[]{:S(2)}, u32[]{:S(2)}) collective-permute-start(f32[128,128]{1,0:T(8,128)S(1)} %get-tuple-element.45), channel_id=1, source_target_pairs={{0,28},{4,24},{8,20},{12,16},{16,12},{20,8},{24,4},{28,0},{1,29},{... | collective-permute-start | bytes 196616 | tf_op jit(solution)/shard_map/ppermute | solution.py:467
  63.7 0.3 collective-permute-start.17
  64.0 1.9 %collective-permute-start.18 = (f32[128,128]{1,0:T(8,128)S(1)}, f32[128,128]{1,0:T(8,128)S(1)}, u32[]{:S(2)}, u32[]{:S(2)}) collective-permute-start(f32[128,128]{1,0:T(8,128)S(1)} %get-tuple-element.47), channel_id=1, source_target_pairs={{0,20},{4,16},{8,28},{12,24},{16,4},{20,0},{24,12},{28,8},{1,21},{... | collective-permute-start | bytes 196616 | tf_op jit(solution)/shard_map/ppermute | solution.py:467
  65.9 1.1 %collective-permute-done.14.refs_6_ = f32[272,128]{1,0:T(8,128)S(1)} collective-permute-done((f32[272,128]{1,0:T(8,128)S(1)}, f32[272,128]{1,0:T(8,128)S(1)}, u32[]{:S(2)}, u32[]{:S(2)}) %collective-permute-start.14) | collective-permute-done | bytes 139296 | tf_op jit(solution)/shard_map/ppermute | solution.py:467
  67.0 1.3 %collective-permute-start.19 = (f32[128,128]{1,0:T(8,128)S(1)}, f32[128,128]{1,0:T(8,128)S(1)}, u32[]{:S(2)}, u32[]{:S(2)}) collective-permute-start(f32[128,128]{1,0:T(8,128)S(1)} %get-tuple-element.48), channel_id=1, source_target_pairs={{0,16},{4,20},{8,24},{12,28},{16,0},{20,4},{24,8},{28,12},{1,17},{... | collective-permute-start | bytes 196616 | tf_op jit(solution)/shard_map/ppermute | solution.py:467
  68.3 0.1 collective-permute-start.20
  68.4 1.8 %collective-permute-start.21 = (f32[128,128]{1,0:T(8,128)S(1)}, f32[128,128]{1,0:T(8,128)S(1)}, u32[]{:S(2)}, u32[]{:S(2)}) collective-permute-start(f32[128,128]{1,0:T(8,128)S(1)} %gather.1.refs_0_), channel_id=1, source_target_pairs={{0,2},{1,3},{2,0},{3,1},{4,6},{5,7},{6,4},{7,5},{8,10},{9,11},{10,... | collective-permute-start | bytes 196616 | tf_op jit(solution)/shard_map/ppermute | solution.py:467
  70.2 0.4 collective-permute-done.17.refs_9_
  70.6 0.3 subtract_clamp_fusion.spot_ref
  70.9 3.8 %collective-permute-done.18.refs_10_ = f32[128,128]{1,0:T(8,128)S(1)} collective-permute-done((f32[128,128]{1,0:T(8,128)S(1)}, f32[128,128]{1,0:T(8,128)S(1)}, u32[]{:S(2)}, u32[]{:S(2)}) %collective-permute-start.18) | collective-permute-done | bytes 65568 | tf_op jit(solution)/shard_map/ppermute | solution.py:467
  74.7 0.3 collective-permute-done.19.refs_11_
  75.0 1.2 %unpack.1 = (f32[16,32,128]{2,1,0:T(8,128)}, f32[3,16,32,128]{3,2,1,0:T(8,128)}) custom-call(f32[272,128]{1,0:T(8,128)S(1)} %get-tuple-element.37.refs_0_, f32[144,128]{1,0:T(8,128)S(1)} %collective-permute-done.9.refs_1_, f32[144,128]{1,0:T(8,128)S(1)} %collective-permute-done.10.refs_2_, f32[144,128]{1,0:T(8,128)S(1)} %collective-permute-done.11.refs_3_, ...), custom_call_target="tpu_custom_call" | custom-call | tf_op jit(solution)/shard_map/unpack/pallas_call | solution.py:600
  76.3 4.6 %image.1 = f32[32,1024]{1,0:T(8,128)} custom-call(s32[256]{0:T(256)S(1)} %get-tuple-element.56.start_ref, s32[256]{0:T(256)S(1)} %get-tuple-element.52.window_ref, s32[256,128]{1,0:T(8,128)S(1)} %subtract_clamp_fusion.spot_ref, f32[256,128]{1,0:T(8,128)S(1)} %get-tuple-element.54.frac_ref, f32[256,128]{1,0:T(8,128)S(1)} %get-tuple-element.53.vpos_ref, ...), custom_call_target="tpu_custom_call" | custom-call | tf_op jit(solution)/shard_map/image/pallas_call | solution.py:443
  (25 shorter events, 0.1 us)
Async XLA Ops:
  3.2 29.9 %copy-start = (f32[256,128]{1,0:T(8,128)S(1)}, f32[256,128]{1,0:T(8,128)}, u32[]{:S(2)}) copy-start(f32[256,128]{1,0:T(8,128)} %get-tuple-element.27.refs_0_) | copy-start | bytes 393220
  3.2 11.8 %collective-permute-start = (f32[256,128]{1,0:T(8,128)}, f32[256,128]{1,0:T(8,128)S(1)}, u32[]{:S(2)}, u32[]{:S(2)}) collective-permute-start(f32[256,128]{1,0:T(8,128)} %get-tuple-element.28), channel_id=1, source_target_pairs={{0,28},{4,24},{8,20},{12,16},{16,12},{20,8},{24,4},{28,0},{1,29},{... | collective-permute-start | bytes 393224 | tf_op jit(solution)/shard_map/ppermute | solution.py:467
  9.2 15.9 %collective-permute-start.1 = (f32[256,128]{1,0:T(8,128)}, f32[256,128]{1,0:T(8,128)S(1)}, u32[]{:S(2)}, u32[]{:S(2)}) collective-permute-start(f32[256,128]{1,0:T(8,128)} %get-tuple-element.29), channel_id=1, source_target_pairs={{0,24},{4,28},{8,16},{12,20},{16,8},{20,12},{24,0},{28,4},{1,25},{... | collective-permute-start | bytes 393224 | tf_op jit(solution)/shard_map/ppermute | solution.py:467
  9.5 20.5 %collective-permute-start.2 = (f32[256,128]{1,0:T(8,128)}, f32[256,128]{1,0:T(8,128)S(1)}, u32[]{:S(2)}, u32[]{:S(2)}) collective-permute-start(f32[256,128]{1,0:T(8,128)} %get-tuple-element.30), channel_id=1, source_target_pairs={{0,20},{4,16},{8,28},{12,24},{16,4},{20,0},{24,12},{28,8},{1,21},{... | collective-permute-start | bytes 393224 | tf_op jit(solution)/shard_map/ppermute | solution.py:467
  10.2 21.6 %collective-permute-start.3 = (f32[256,128]{1,0:T(8,128)}, f32[256,128]{1,0:T(8,128)S(1)}, u32[]{:S(2)}, u32[]{:S(2)}) collective-permute-start(f32[256,128]{1,0:T(8,128)} %get-tuple-element.31), channel_id=1, source_target_pairs={{0,16},{4,20},{8,24},{12,28},{16,0},{20,4},{24,8},{28,12},{1,17},{... | collective-permute-start | bytes 393224 | tf_op jit(solution)/shard_map/ppermute | solution.py:467
  12.2 19.6 %collective-permute-start.4 = (f32[256,128]{1,0:T(8,128)}, f32[256,128]{1,0:T(8,128)S(1)}, u32[]{:S(2)}, u32[]{:S(2)}) collective-permute-start(f32[256,128]{1,0:T(8,128)} %get-tuple-element.32), channel_id=1, source_target_pairs={{0,12},{4,8},{8,4},{12,0},{16,28},{20,24},{24,20},{28,16},{1,13},{... | collective-permute-start | bytes 393224 | tf_op jit(solution)/shard_map/ppermute | solution.py:467
  15.1 18.0 %collective-permute-start.5 = (f32[256,128]{1,0:T(8,128)}, f32[256,128]{1,0:T(8,128)S(1)}, u32[]{:S(2)}, u32[]{:S(2)}) collective-permute-start(f32[256,128]{1,0:T(8,128)} %get-tuple-element.33), channel_id=1, source_target_pairs={{0,8},{4,12},{8,0},{12,4},{16,24},{20,28},{24,16},{28,20},{1,9},{5... | collective-permute-start | bytes 393224 | tf_op jit(solution)/shard_map/ppermute | solution.py:467
  25.2 7.9 %collective-permute-start.6 = (f32[256,128]{1,0:T(8,128)}, f32[256,128]{1,0:T(8,128)S(1)}, u32[]{:S(2)}, u32[]{:S(2)}) collective-permute-start(f32[256,128]{1,0:T(8,128)} %get-tuple-element.34), channel_id=1, source_target_pairs={{0,4},{4,0},{8,12},{12,8},{16,20},{20,16},{24,28},{28,24},{1,5},{5... | collective-permute-start | bytes 393224 | tf_op jit(solution)/shard_map/ppermute | solution.py:467
  26.5 6.6 %copy-start.1 = (s32[16]{0:T(128)S(1)}, s32[16]{0:T(128)}, u32[]{:S(2)}) copy-start(s32[16]{0:T(128)} %shift_ref.5) | copy-start | bytes 196
  26.5 6.6 %copy-start.2 = (f32[16]{0:T(128)S(1)}, f32[16]{0:T(128)}, u32[]{:S(2)}) copy-start(f32[16]{0:T(128)} %frac_ref.5) | copy-start | bytes 196
  33.7 5.1 %collective-permute-start.7 = (f32[264,128]{1,0:T(8,128)S(1)}, f32[264,128]{1,0:T(8,128)S(1)}, u32[]{:S(2)}, u32[]{:S(2)}) collective-permute-start(f32[264,128]{1,0:T(8,128)S(1)} %get-tuple-element.35), channel_id=1, source_target_pairs={{0,4},{8,12},{16,20},{24,28},{1,5},{9,13},{17,21},{25,29},{2,6},{1... | collective-permute-start | bytes 405512 | tf_op jit(solution)/shard_map/ppermute | solution.py:494
  34.4 4.4 %collective-permute-start.8 = (f32[264,128]{1,0:T(8,128)S(1)}, f32[264,128]{1,0:T(8,128)S(1)}, u32[]{:S(2)}, u32[]{:S(2)}) collective-permute-start(f32[264,128]{1,0:T(8,128)S(1)} %get-tuple-element.36), channel_id=1, source_target_pairs={{4,8},{12,16},{20,24},{28,1},{5,9},{13,17},{21,25},{29,2},{6,10},{... | collective-permute-start | bytes 405512 | tf_op jit(solution)/shard_map/ppermute | solution.py:494
  35.5 3.3 %copy-start.3 = (f32[4,128]{1,0:T(4,128)S(1)}, f32[4,128]{1,0:T(4,128)}, u32[]{:S(2)}) copy-start(f32[4,128]{1,0:T(4,128)} %constant.137.clone.tilt_ref) | copy-start | bytes 6148
  43.2 12.6 %collective-permute-start.10 = (f32[144,128]{1,0:T(8,128)S(1)}, f32[144,128]{1,0:T(8,128)S(1)}, u32[]{:S(2)}, u32[]{:S(2)}) collective-permute-start(f32[144,128]{1,0:T(8,128)S(1)} %get-tuple-element.39), channel_id=1, source_target_pairs={{0,24},{4,28},{8,16},{12,20},{16,8},{20,12},{24,0},{28,4},{1,25},{... | collective-permute-start | bytes 221192 | tf_op jit(solution)/shard_map/ppermute | solution.py:467
  49.1 9.5 %collective-permute-start.11 = (f32[144,128]{1,0:T(8,128)S(1)}, f32[144,128]{1,0:T(8,128)S(1)}, u32[]{:S(2)}, u32[]{:S(2)}) collective-permute-start(f32[144,128]{1,0:T(8,128)S(1)} %get-tuple-element.40), channel_id=1, source_target_pairs={{0,20},{4,16},{8,28},{12,24},{16,4},{20,0},{24,12},{28,8},{1,21},{... | collective-permute-start | bytes 221192 | tf_op jit(solution)/shard_map/ppermute | solution.py:467
  49.1 11.4 %collective-permute-start.12 = (f32[144,128]{1,0:T(8,128)S(1)}, f32[144,128]{1,0:T(8,128)S(1)}, u32[]{:S(2)}, u32[]{:S(2)}) collective-permute-start(f32[144,128]{1,0:T(8,128)S(1)} %get-tuple-element.41), channel_id=1, source_target_pairs={{0,16},{4,20},{8,24},{12,28},{16,0},{20,4},{24,8},{28,12},{1,17},{... | collective-permute-start | bytes 221192 | tf_op jit(solution)/shard_map/ppermute | solution.py:467
  54.0 9.8 %collective-permute-start.9 = (f32[144,128]{1,0:T(8,128)S(1)}, f32[144,128]{1,0:T(8,128)S(1)}, u32[]{:S(2)}, u32[]{:S(2)}) collective-permute-start(f32[144,128]{1,0:T(8,128)S(1)} %get-tuple-element.38), channel_id=1, source_target_pairs={{0,28},{4,24},{8,20},{12,16},{16,12},{20,8},{24,4},{28,0},{1,29},{... | collective-permute-start | bytes 221192 | tf_op jit(solution)/shard_map/ppermute | solution.py:467
  54.3 9.7 %collective-permute-start.13 = (f32[272,128]{1,0:T(8,128)S(1)}, f32[272,128]{1,0:T(8,128)S(1)}, u32[]{:S(2)}, u32[]{:S(2)}) collective-permute-start(f32[272,128]{1,0:T(8,128)S(1)} %get-tuple-element.42), channel_id=1, source_target_pairs={{0,12},{4,8},{8,4},{12,0},{16,28},{20,24},{24,20},{28,16},{1,13},{... | collective-permute-start | bytes 417800 | tf_op jit(solution)/shard_map/ppermute | solution.py:467
  55.9 11.2 %collective-permute-start.14 = (f32[272,128]{1,0:T(8,128)S(1)}, f32[272,128]{1,0:T(8,128)S(1)}, u32[]{:S(2)}, u32[]{:S(2)}) collective-permute-start(f32[272,128]{1,0:T(8,128)S(1)} %get-tuple-element.43), channel_id=1, source_target_pairs={{0,8},{4,12},{8,0},{12,4},{16,24},{20,28},{24,16},{28,20},{1,9},{5... | collective-permute-start | bytes 417800 | tf_op jit(solution)/shard_map/ppermute | solution.py:467
  58.7 9.7 %collective-permute-start.15 = (f32[272,128]{1,0:T(8,128)S(1)}, f32[272,128]{1,0:T(8,128)S(1)}, u32[]{:S(2)}, u32[]{:S(2)}) collective-permute-start(f32[272,128]{1,0:T(8,128)S(1)} %get-tuple-element.44), channel_id=1, source_target_pairs={{0,4},{4,0},{8,12},{12,8},{16,20},{20,16},{24,28},{28,24},{1,5},{5... | collective-permute-start | bytes 417800 | tf_op jit(solution)/shard_map/ppermute | solution.py:467
  60.6 7.8 %collective-permute-start.16 = (f32[128,128]{1,0:T(8,128)S(1)}, f32[128,128]{1,0:T(8,128)S(1)}, u32[]{:S(2)}, u32[]{:S(2)}) collective-permute-start(f32[128,128]{1,0:T(8,128)S(1)} %get-tuple-element.45), channel_id=1, source_target_pairs={{0,28},{4,24},{8,20},{12,16},{16,12},{20,8},{24,4},{28,0},{1,29},{... | collective-permute-start | bytes 196616 | tf_op jit(solution)/shard_map/ppermute | solution.py:467
  63.7 6.9 %collective-permute-start.17 = (f32[128,128]{1,0:T(8,128)S(1)}, f32[128,128]{1,0:T(8,128)S(1)}, u32[]{:S(2)}, u32[]{:S(2)}) collective-permute-start(f32[128,128]{1,0:T(8,128)S(1)} %get-tuple-element.46), channel_id=1, source_target_pairs={{0,24},{4,28},{8,16},{12,20},{16,8},{20,12},{24,0},{28,4},{1,25},{... | collective-permute-start | bytes 196616 | tf_op jit(solution)/shard_map/ppermute | solution.py:467
  64.0 10.7 %collective-permute-start.18 = (f32[128,128]{1,0:T(8,128)S(1)}, f32[128,128]{1,0:T(8,128)S(1)}, u32[]{:S(2)}, u32[]{:S(2)}) collective-permute-start(f32[128,128]{1,0:T(8,128)S(1)} %get-tuple-element.47), channel_id=1, source_target_pairs={{0,20},{4,16},{8,28},{12,24},{16,4},{20,0},{24,12},{28,8},{1,21},{... | collective-permute-start | bytes 196616 | tf_op jit(solution)/shard_map/ppermute | solution.py:467
  67.0 8.0 %collective-permute-start.19 = (f32[128,128]{1,0:T(8,128)S(1)}, f32[128,128]{1,0:T(8,128)S(1)}, u32[]{:S(2)}, u32[]{:S(2)}) collective-permute-start(f32[128,128]{1,0:T(8,128)S(1)} %get-tuple-element.48), channel_id=1, source_target_pairs={{0,16},{4,20},{8,24},{12,28},{16,0},{20,4},{24,8},{28,12},{1,17},{... | collective-permute-start | bytes 196616 | tf_op jit(solution)/shard_map/ppermute | solution.py:467
  68.3 7.9 %collective-permute-start.20 = (f32[128,128]{1,0:T(8,128)S(1)}, f32[128,128]{1,0:T(8,128)S(1)}, u32[]{:S(2)}, u32[]{:S(2)}) collective-permute-start(f32[128,128]{1,0:T(8,128)S(1)} %gather.1.refs_0_), channel_id=1, source_target_pairs={{0,3},{1,2},{2,1},{3,0},{4,7},{5,6},{6,5},{7,4},{8,11},{9,10},{10,... | collective-permute-start | bytes 196616 | tf_op jit(solution)/shard_map/ppermute | solution.py:467
  68.4 7.9 %collective-permute-start.21 = (f32[128,128]{1,0:T(8,128)S(1)}, f32[128,128]{1,0:T(8,128)S(1)}, u32[]{:S(2)}, u32[]{:S(2)}) collective-permute-start(f32[128,128]{1,0:T(8,128)S(1)} %gather.1.refs_0_), channel_id=1, source_target_pairs={{0,2},{1,3},{2,0},{3,1},{4,6},{5,7},{6,4},{7,5},{8,10},{9,11},{10,... | collective-permute-start | bytes 196616 | tf_op jit(solution)/shard_map/ppermute | solution.py:467
  70.6 5.7 %collective-permute-start.22 = (f32[128,128]{1,0:T(8,128)S(1)}, f32[128,128]{1,0:T(8,128)S(1)}, u32[]{:S(2)}, u32[]{:S(2)}) collective-permute-start(f32[128,128]{1,0:T(8,128)S(1)} %gather.1.refs_0_), channel_id=1, source_target_pairs={{0,1},{1,0},{2,3},{3,2},{4,5},{5,4},{6,7},{7,6},{8,9},{9,8},{10,11... | collective-permute-start | bytes 196616 | tf_op jit(solution)/shard_map/ppermute | solution.py:467

commit v4 on v3

--- a/solution.py
+++ b/solution.py
@@ -22,6 +22,8 @@
 INNER = 8
 HALO = STEPS
 LANES = 128
+SPLIT = 1
+ORDER = (0, 7, 1, 6, 2, 5, 3, 4)
 VMEM_LIMIT = 48 * 1024 * 1024
 PACK_LIMIT = 62 * 1024 * 1024
 
@@ -49,14 +51,21 @@
     per_column = FIELDS * groups
     stride = radial // len(chunk_refs) * per_column
     place = lax.axis_index("phi")
+    part = cells // SPLIT
     copies = [
-        pltpu.make_async_copy(field_ref(density_ref, velocity_ref, field), field_refs.at[field], arrived.at[field])
+        pltpu.make_async_copy(
+            field_ref(density_ref, velocity_ref, field).at[pl.ds(h * part, part)],
+            field_refs.at[field, pl.ds(h * part, part)],
+            arrived.at[field * SPLIT + h],
+        )
         for field in range(FIELDS)
+        for h in range(SPLIT)
     ]
     for copy in copies:
         copy.start()
     for field in range(FIELDS):
-        copies[field].wait()
+        for copy in copies[field * SPLIT:(field + 1) * SPLIT]:
+            copy.wait()
         for group in range(groups):
             block = field_refs[field, :, pl.ds(group, INNER, stride=groups), :]
             turned = block.reshape(cells * INNER, radial).T
@@ -65,8 +74,8 @@
         chunk_ref[...] = rows_ref[pl.ds(pl.multiple_of(partner(place, j, len(chunk_refs)) * stride, stride), stride), :]
 
 
-def halo_kernel(cycle, columns, shift_ref, frac_ref, *refs):
-    chunk_refs, piece_refs = refs[:cycle], refs[cycle:]
+def halo_kernel(cycle, columns, early, shift_ref, frac_ref, *refs):
+    chunk_refs, piece_refs = refs[:cycle], refs[cycle + early:]
     rows = chunk_refs[0].shape[0]
     edge = HALO * rows // columns
     place = lax.axis_index("phi")
@@ -80,29 +89,30 @@
         ref[pl.ds(edge * cycle, 8), :] = jnp.where(sub == 0, shift_ref[band].astype(jnp.float32), frac_ref[band])
 
 
-def unpack_kernel(cycle, cuts, *refs):
+def unpack_kernel(*refs):
     *chunk_refs, density_ref, velocity_ref, rows_ref, field_refs, leaving = refs
-    first_refs, rest_refs = chunk_refs[:cycle], chunk_refs[cycle:]
     cells, polar, radial = density_ref.shape
     groups = polar // INNER
     per_column = FIELDS * groups
-    stride = radial // cycle * per_column
+    stride = radial // len(chunk_refs) * per_column
     place = lax.axis_index("phi")
-    rest = iter(rest_refs)
-    for j, cut in enumerate(cuts):
-        at = partner(place, j, cycle) * stride
-        rows_ref[pl.ds(pl.multiple_of(at, per_column), cut), :] = first_refs[j][pl.ds(0, cut), :]
-        if cut < stride:
-            rows_ref[pl.ds(pl.multiple_of(at + cut, per_column), stride - cut), :] = next(rest)[...]
+    for j, chunk_ref in enumerate(chunk_refs):
+        at = pl.multiple_of(partner(place, j, len(chunk_refs)) * stride, stride)
+        rows_ref[pl.ds(at, stride), :] = chunk_ref[pl.ds(0, stride), :]
+    part = cells // SPLIT
     copies = []
     for field in range(FIELDS):
         for group in range(groups):
             turned = rows_ref[pl.ds(field * groups + group, radial, stride=per_column), :]
             block = turned.T.reshape(cells, INNER, radial)
             field_refs[field, :, pl.ds(group, INNER, stride=groups), :] = block
-        copy = pltpu.make_async_copy(field_refs.at[field], field_ref(density_ref, velocity_ref, field), leaving.at[field])
-        copy.start()
-        copies.append(copy)
+        for h in range(SPLIT):
+            here = pl.ds(h * part, part)
+            copy = pltpu.make_async_copy(
+                field_refs.at[field, here], field_ref(density_ref, velocity_ref, field).at[here], leaving.at[field * SPLIT + h]
+            )
+            copy.start()
+            copies.append(copy)
     for copy in copies:
         copy.wait()
 
@@ -193,7 +203,13 @@
             write(col - 1, finish(combine(pend, a_rad, -1.0), col - 1))
             return combine(fresh_pend, before, 1.0), b_rad
 
-        pend, _ = lax.fori_loop(low + 2, high - 1, body, (pend, after), unroll=4)
+        carry = (pend, after)
+        if high - low <= 8:
+            for col in range(low + 2, high - 1):
+                carry = body(col, carry)
+        else:
+            carry = lax.fori_loop(low + 2, high - 1, body, carry, unroll=4)
+        pend = carry[0]
         prim = read(high - 1)
         a_rad = face_part(conserved(prim), prim[1], 1, -1.0)
         write(high - 2, finish(combine(pend, a_rad, -1.0), high - 2))
@@ -219,70 +235,8 @@
     return at, reader, writer
 
 
-def inner_kernel(cells, cycle, columns, nrad, groups, shift_ref, frac_ref, *refs):
-    chunk_refs, (work_ref, own_ref) = refs[:cycle], refs[cycle:]
-    per_column = FIELDS * groups
-    _, reader, writer = block_rows(cycle, groups)
-    place = lax.axis_index("phi")
-    for j in range(cycle):
-        own_ref[pl.ds(partner(place, j, cycle), columns * per_column, stride=cycle), :] = chunk_refs[j][...]
-
-    def band_of(col):
-        band = (place * columns + col - HALO) // BAND
-        return shift_ref[band], frac_ref[band]
-
-    step_columns = stepper(cells, cycle, columns, nrad, groups, band_of)
-    if columns > 2:
-        step_columns(reader(own_ref, HALO), writer(work_ref, HALO + 1), HALO, HALO + columns)
-
-
-def outer_kernel(cells, cycle, columns, nrad, groups, cuts, shift_ref, frac_ref, tilt_ref, first_ref, second_ref, inner_ref, *refs):
-    chunk_refs, refs = refs[:cycle], refs[cycle:]
-    *out_refs, strip_ref, work_ref, done_ref = refs
-    first_refs, rest_refs = out_refs[:cycle], out_refs[cycle:]
-    swap = first_refs[0].shape[0] > cuts[0]
-    per_column = FIELDS * groups
-    edge = HALO * per_column * cycle
-    at, reader, writer = block_rows(cycle, groups)
-    place = lax.axis_index("phi")
-    first_global = (lax.axis_index("row") * cycle + place) * columns
-
-    odd = place % 2 == 1
-
-    def carried(rows):
-        return rows.astype(jnp.int32)[0, 0], rows[1, 0]
-
-    tails = [ref[pl.ds(edge, 8), :] for ref in (first_ref, second_ref)]
-    below = carried(jnp.where(odd, tails[0], tails[1]))
-    above = carried(jnp.where(odd, tails[1], tails[0]))
-
-    def band_of(col):
-        band = jnp.clip((place * columns + col - HALO) // BAND, 0, shift_ref.shape[0] - 1)
-        low, high = col < HALO, col >= HALO + columns
-        shift = jnp.where(low, below[0], jnp.where(high, above[0], shift_ref[band]))
-        weight = jnp.where(low, below[1], jnp.where(high, above[1], frac_ref[band]))
-        return shift, weight
-
-    step_columns = stepper(cells, cycle, columns, nrad, groups, band_of)
-    strip_ref[pl.ds(pl.multiple_of(jnp.where(odd, 0, 3 * edge), 8), edge), :] = first_ref[pl.ds(0, edge), :]
-    strip_ref[pl.ds(pl.multiple_of(jnp.where(odd, 3 * edge, 0), 8), edge), :] = second_ref[pl.ds(0, edge), :]
-    rows = columns * per_column
-    for j in range(cycle):
-        slab = partner(place, j, cycle)
-        strip_ref[pl.ds(edge + slab, edge // cycle, stride=cycle), :] = chunk_refs[j][pl.ds(0, edge // cycle), :]
-        strip_ref[pl.ds(2 * edge + slab, edge // cycle, stride=cycle), :] = chunk_refs[j][pl.ds(rows - edge // cycle, edge // cycle), :]
-    kept = (columns - 2) * per_column * cycle
-    if kept:
-        work_ref[pl.ds((HALO + 1) * per_column * cycle, kept), :] = inner_ref[pl.ds(0, kept), :]
-    step_columns(reader(strip_ref), writer(work_ref), 0, 2 * HALO)
-    step_columns(reader(strip_ref, columns - 2 * HALO), writer(work_ref), columns, columns + 2 * HALO)
-    step_columns(reader(work_ref), writer(done_ref, HALO), 1, columns + 2 * HALO - 1)
-    rest = iter(rest_refs)
-    for j, cut in enumerate(cuts):
-        slab = partner(place, j, cycle)
-        first_refs[j][pl.ds(0, cut), :] = done_ref[pl.ds(slab, cut, stride=cycle), :]
-        if cut < rows:
-            next(rest)[...] = done_ref[pl.ds(cut * cycle + slab, rows - cut, stride=cycle), :]
+def lit_columns(cycle, nrad, groups, first_global, tilt_ref, done_ref, cols, total_columns):
+    at, _, _ = block_rows(cycle, groups)
     lane = lax.broadcasted_iota(jnp.int32, (cycle, LANES), 1)
     inner = lane % INNER
 
@@ -305,11 +259,97 @@
         radius = R_INNER + (number + 0.5) * (1.0 - R_INNER) / nrad
         return pltpu.roll(light * (1.0 / jnp.sqrt(radius)), own % INNER, 1)
 
-    for h in range(-(-columns // INNER)):
-        slots = range(min(INNER, columns - h * INNER))
+    blocks = []
+    for h in range(-(-total_columns // INNER)):
         x = jnp.zeros((cycle, LANES), jnp.float32)
-        for slot, light in [(slot, column_light(h * INNER + slot)) for slot in slots]:
-            x = jnp.where(inner == slot, light, x)
+        for own, light in [(own, column_light(own)) for own in cols if own // INNER == h]:
+            x = jnp.where(inner == own % INNER, light, x)
+        blocks.append(x)
+    return blocks
+
+
+def inner_kernel(cells, cycle, columns, nrad, groups, margin, shift_ref, frac_ref, tilt_ref, *refs):
+    chunk_refs, (done_ref, side_ref, light_ref, own_ref, work_ref) = refs[:cycle], refs[cycle:]
+    per_column = FIELDS * groups
+    side = HALO * per_column * cycle
+    _, reader, writer = block_rows(cycle, groups)
+    place = lax.axis_index("phi")
+    for j in range(cycle):
+        own_ref[pl.ds(partner(place, j, cycle), columns * per_column, stride=cycle), :] = chunk_refs[j][...]
+
+    def band_of(col):
+        band = (place * columns + col - HALO) // BAND
+        return shift_ref[band], frac_ref[band]
+
+    first_global = (lax.axis_index("row") * cycle + place) * columns
+    step_columns = stepper(cells, cycle, columns, nrad, groups, band_of)
+    last = HALO + columns
+    step_columns(reader(own_ref, HALO), writer(work_ref, HALO), HALO, last)
+    step_columns(reader(work_ref, HALO), writer(done_ref, HALO), HALO + 1, last - 1)
+    one = side // HALO
+    side_ref[pl.ds(0, side), :] = work_ref[pl.ds(one, side), :]
+    side_ref[pl.ds(side, side), :] = work_ref[pl.ds((columns - 1) * one - side, side), :]
+    blocks = lit_columns(cycle, nrad, groups, first_global, tilt_ref, done_ref, range(margin, columns - margin), columns)
+    for h, x in enumerate(blocks):
+        light_ref[h] = x
+
+
+def outer_kernel(cells, cycle, columns, nrad, groups, margin, swap, shift_ref, frac_ref, tilt_ref, first_ref, second_ref, *refs):
+    chunk_refs, refs = refs[:cycle], refs[cycle:]
+    if margin:
+        inner_ref, side_ref, lit_ref, *refs = refs
+    *out_refs, strip_ref, work_ref, done_ref = refs
+    out_refs, light_refs = out_refs[:cycle], out_refs[cycle:]
+    per_column = FIELDS * groups
+    column_rows = per_column * cycle
+    edge = HALO * column_rows
+    _, reader, writer = block_rows(cycle, groups)
+    place = lax.axis_index("phi")
+    first_global = (lax.axis_index("row") * cycle + place) * columns
+
+    odd = place % 2 == 1
+
+    def carried(rows):
+        return rows.astype(jnp.int32)[0, 0], rows[1, 0]
+
+    tails = [ref[pl.ds(edge, 8), :] for ref in (first_ref, second_ref)]
+    below = carried(jnp.where(odd, tails[0], tails[1]))
+    above = carried(jnp.where(odd, tails[1], tails[0]))
+
+    def band_of(col):
+        band = jnp.clip((place * columns + col - HALO) // BAND, 0, shift_ref.shape[0] - 1)
+        low, high = col < HALO, col >= HALO + columns
+        shift = jnp.where(low, below[0], jnp.where(high, above[0], shift_ref[band]))
+        weight = jnp.where(low, below[1], jnp.where(high, above[1], frac_ref[band]))
+        return shift, weight
+
+    step_columns = stepper(cells, cycle, columns, nrad, groups, band_of)
+    strip_ref[pl.ds(pl.multiple_of(jnp.where(odd, 0, 3 * edge), 8), edge), :] = first_ref[pl.ds(0, edge), :]
+    strip_ref[pl.ds(pl.multiple_of(jnp.where(odd, 3 * edge, 0), 8), edge), :] = second_ref[pl.ds(0, edge), :]
+    rows = columns * per_column
+    for j in range(cycle):
+        slab = partner(place, j, cycle)
+        strip_ref[pl.ds(edge + slab, edge // cycle, stride=cycle), :] = chunk_refs[j][pl.ds(0, edge // cycle), :]
+        strip_ref[pl.ds(2 * edge + slab, edge // cycle, stride=cycle), :] = chunk_refs[j][pl.ds(rows - edge // cycle, edge // cycle), :]
+    step_columns(reader(strip_ref), writer(work_ref), 0, 2 * HALO)
+    step_columns(reader(strip_ref, columns - 2 * HALO), writer(work_ref), columns, columns + 2 * HALO)
+    if margin:
+        work_ref[pl.ds((HALO + 1) * column_rows, edge), :] = side_ref[pl.ds(0, edge), :]
+        work_ref[pl.ds((columns - 1) * column_rows, edge), :] = side_ref[pl.ds(edge, edge), :]
+        kept = pl.ds(margin * column_rows, (columns - 2 * margin) * column_rows)
+        done_ref[kept, :] = inner_ref[kept, :]
+        step_columns(reader(work_ref), writer(done_ref, HALO), 1, 1 + 2 * HALO)
+        step_columns(reader(work_ref), writer(done_ref, HALO), columns - 1, columns - 1 + 2 * HALO)
+        cols = [*range(margin), *range(columns - margin, columns)]
+    else:
+        step_columns(reader(work_ref), writer(done_ref, HALO), 1, columns + 2 * HALO - 1)
+        cols = range(columns)
+    for j, out_ref in enumerate(out_refs):
+        out_ref[pl.ds(0, rows), :] = done_ref[pl.ds(partner(place, j, cycle), rows, stride=cycle), :]
+    lane = lax.broadcasted_iota(jnp.int32, (cycle, LANES), 1)
+    for h, x in enumerate(lit_columns(cycle, nrad, groups, first_global, tilt_ref, done_ref, cols, columns)):
+        if margin:
+            x = x + lit_ref[h]
         if swap:
             sub = lax.broadcasted_iota(jnp.int32, (cycle, LANES), 0)
             for d in (1, 2, 4):
@@ -318,10 +358,10 @@
                 ahead = pltpu.roll(pltpu.roll(x, cycle - d, 0), d, 1)
                 back = pltpu.roll(pltpu.roll(x, d, 0), LANES - d, 1)
                 x = jnp.where(low_sub == low_lane, x, jnp.where(low_sub, ahead, back))
-            for ref, cut in zip(first_refs, cuts):
-                ref[pl.ds(cut + h * INNER, INNER), :] = x
+            for out_ref in out_refs:
+                out_ref[pl.ds(rows + h * INNER, INNER), :] = x
         else:
-            rest_refs[0][h] = x
+            light_refs[0][h] = x
 
 
 def pixel_tiles(first_row, rows_dev, npix, nphi, nrad):
@@ -344,9 +384,10 @@
     vpos = (angle + jnp.pi) / (2.0 * jnp.pi) * nphi - 0.5
     window = jnp.min(lower, axis=1) // (LANES // 2)
     window = jnp.clip(window, 0, (nrad + LANES) // (LANES // 2))
-    start = jnp.clip(jnp.floor(jnp.min(vpos, axis=1)).astype(jnp.int32) + 8, 0, nphi + 8)
+    above = jnp.where(first_row >= npix // 2, nphi // 2, 0) - 8
+    start = jnp.clip(jnp.floor(jnp.min(vpos, axis=1)).astype(jnp.int32) - above, 0, nphi // 2 + 8)
     spot = jnp.clip(lower - window[:, None] * (LANES // 2), 0, LANES - 2)
-    return start, window, spot, frac_u, vpos + 8.0 - start[:, None].astype(jnp.float32)
+    return start, window, spot, frac_u, vpos - (start[:, None] + above).astype(jnp.float32)
 
 
 def window_rows(rows_dev, npix, nphi):
@@ -357,34 +398,24 @@
     return -(-int(np.ceil(span) + 2) // 8) * 8
 
 
-def image_kernel(cells, cycle, nphi, nrad, rows, tile_rows, across, start_ref, window_ref, spot_ref, frac_ref, vpos_ref, *refs):
-    *table_refs, out_ref, turned_ref, wide_ref = refs
-    blocks = nrad // LANES
-    each = blocks // len(table_refs)
-    for j, table_ref in enumerate(table_refs):
-        for k in range(each):
-            block = partner(lax.axis_index("row"), j, len(table_refs)) * each + k
-            for l in range(nphi // LANES):
-                at = pl.multiple_of(block * nphi + l * LANES, LANES)
-                turned_ref[pl.ds(at, LANES), :] = table_ref[pl.ds(k * LANES, LANES), pl.ds(l * LANES, LANES)].T
+def image_kernel(rows, tile_rows, across, start_ref, window_ref, spot_ref, frac_ref, vpos_ref, *refs):
+    *table_refs, out_ref, wide_ref = refs
+    blocks = len(table_refs)
+    tall = table_refs[0].shape[0]
     half = LANES // 2
     windows = 2 * (blocks + 2) - 1
-    tall = wide_ref.shape[0] // windows
-
-    def fill(s, carry):
-        zero = jnp.zeros((cells, LANES), jnp.float32)
-        value = [zero] + [turned_ref[pl.ds(k * nphi + s, cells, stride=cycle), :] for k in range(blocks)] + [zero]
-        for w in range(windows):
-            piece = value[w // 2]
-            if w % 2:
-                piece = jnp.concatenate([piece[:, half:], value[w // 2 + 1][:, :half]], axis=1)
-            wide_ref[pl.ds((8 + s * cells) * windows + w, cells, stride=windows), :] = piece
-        return carry
-
-    lax.fori_loop(0, cycle, fill, 0, unroll=8)
-    pad = tall - nphi - 8
-    wide_ref[pl.ds(0, 8 * windows), :] = wide_ref[pl.ds(nphi * windows, 8 * windows), :]
-    wide_ref[pl.ds((nphi + 8) * windows, pad * windows), :] = wide_ref[pl.ds(8 * windows, pad * windows), :]
+    row = lax.axis_index("row")
+    for j in range(blocks):
+        block = partner(row, j, blocks)
+        value = table_refs[j][...]
+        wide_ref[pl.ds(2 * block + 2, tall, stride=windows), :] = value
+    zero = jnp.zeros((tall, LANES), jnp.float32)
+    wide_ref[pl.ds(0, tall, stride=windows), :] = zero
+    wide_ref[pl.ds(windows - 1, tall, stride=windows), :] = zero
+    for w in range(1, windows, 2):
+        left = wide_ref[pl.ds(w - 1, tall, stride=windows), :]
+        right = wide_ref[pl.ds(w + 1, tall, stride=windows), :]
+        wide_ref[pl.ds(w, tall, stride=windows), :] = jnp.concatenate([left[:, half:], right[:, :half]], axis=1)
 
     sub = lax.broadcasted_iota(jnp.int32, (8, LANES), 0)
     lane = lax.broadcasted_iota(jnp.int32, (8, LANES), 1)
@@ -431,24 +462,20 @@
     lax.fori_loop(0, spot_ref.shape[0] // 8, group, 0, unroll=min(8, spot_ref.shape[0] // 8))
 
 
-def draw_image(tables, geometry, cells, cycle, rows_dev, npix, nphi, nrad):
+def draw_image(tables, geometry, rows, rows_dev, npix, nrad):
     start, window, spot, frac_u, vpos = geometry
     tiles = spot.shape[0]
     tile_rows = min(8, rows_dev)
     tile_cols = LANES // tile_rows
     across = npix // tile_cols
-    rows = window_rows(rows_dev, npix, nphi)
     windows = 2 * (nrad // LANES + 2) - 1
     shape = (rows_dev, npix) if tile_rows == 8 else (tiles, LANES)
     image = pl.pallas_call(
-        functools.partial(image_kernel, cells, cycle, nphi, nrad, rows, tile_rows, across),
+        functools.partial(image_kernel, rows, tile_rows, across),
         out_shape=jax.ShapeDtypeStruct(shape, jnp.float32),
         in_specs=smem(2) + vmem(3 + len(tables)),
         out_specs=pl.BlockSpec(memory_space=pltpu.VMEM),
-        scratch_shapes=[
-            pltpu.VMEM((nphi * (nrad // LANES), LANES), jnp.float32),
-            pltpu.VMEM(((nphi + 16 + rows) * windows, LANES), jnp.float32),
-        ],
+        scratch_shapes=[pltpu.VMEM((tables[0].shape[0] * windows, LANES), jnp.float32)],
         compiler_params=params(),
         name="image",
     )(start, window, spot, frac_u, vpos, *tables)
@@ -458,8 +485,12 @@
     return jnp.swapaxes(image, 1, 2).reshape(rows_dev, npix)
 
 
+def order(size):
+    return ORDER if size == len(ORDER) else tuple(range(size))
+
+
 def partner(place, index, size):
-    return place ^ ((size - index) % size)
+    return place ^ order(size)[index]
 
 
 def swapped(piece, axis, index):
@@ -471,18 +502,31 @@
     size = lax.axis_size(axis)
     if size > INNER:
         place, every = lax.axis_index(axis), jnp.arange(size)
-        sent = jnp.stack(chunks)[(size - (place ^ every)) % size]
-        got = lax.all_to_all(sent, axis, 0, 0, tiled=True)[partner(place, every, size)]
+        sent = jnp.stack(chunks)[place ^ every]
+        got = lax.all_to_all(sent, axis, 0, 0, tiled=True)[place ^ every]
         return [got[i] for i in range(size)]
     return [chunks[0]] + [swapped(chunks[i], axis, i) for i in range(1, size)]
 
 
-def gather_kernel(cuts, *refs):
-    *piece_refs, out_ref = refs
-    size = len(cuts)
-    count = out_ref.shape[0] // size
-    for j, cut in enumerate(cuts):
-        out_ref[pl.ds(pl.multiple_of(partner(lax.axis_index("phi"), j, size) * count, count), count), :] = piece_refs[j][pl.ds(cut, count), :]
+def gather_kernel(cells, cycle, half_rows, cut, *refs):
+    *piece_refs, out_ref, light_ref, turned_ref = refs
+    count = piece_refs[0].shape[0] - cut
+    place = lax.axis_index("phi")
+    for j in range(len(piece_refs)):
+        at = partner(place, j, len(piece_refs)) * count
+        light_ref[pl.ds(pl.multiple_of(at, 8), count), :] = piece_refs[j][pl.ds(cut, count), :]
+    for l in range(light_ref.shape[1] // LANES):
+        turned_ref[pl.ds(l * LANES, LANES), :] = light_ref[:, pl.ds(l * LANES, LANES)].T
+
+    def slab(index):
+        return turned_ref[pl.ds(lax.rem(index + cycle, cycle), cells, stride=cycle), :]
+
+    first = jnp.where(place >= cycle // 2, cycle // 2, 0)
+    out_ref[...] = jnp.zeros_like(out_ref)
+    for s in range(cycle // 2):
+        out_ref[pl.ds(8 + s * cells, cells), :] = slab(first + s)
+    out_ref[pl.ds(0, 8), :] = slab(first - 1)[cells - 8:, :]
+    out_ref[pl.ds(8 + half_rows, 8), :] = slab(first + cycle // 2)[:8, :]
 
 
 def neighbour_columns(first, second):
@@ -508,6 +552,7 @@
     place = lax.axis_index("phi")
     row = lax.axis_index("row")
     block = (FIELDS, cells, polar, radial)
+    shifts, fractions = jnp.clip(shifts, 0, nphi - 1), jnp.clip(fractions, 0.0, 1.0)
     hbm = pl.BlockSpec(memory_space=pltpu.HBM)
 
     def f32(*shape):
@@ -522,51 +567,51 @@
         scratch_shapes=[
             pltpu.VMEM((radial * per_column, LANES), jnp.float32),
             pltpu.VMEM(block, jnp.float32),
-            pltpu.SemaphoreType.DMA((FIELDS,)),
+            pltpu.SemaphoreType.DMA((FIELDS * SPLIT,)),
         ],
         compiler_params=pltpu.CompilerParams(vmem_limit_bytes=PACK_LIMIT),
         name="pack",
     )(density, velocity)
     ring = exchange(chunks, "phi")
+    rows_dev = NPIX // (cycle * bands)
+    geometry = pixel_tiles((place * bands + row) * rows_dev, rows_dev, NPIX, nphi, nrad)
 
     column_rows = per_column * cycle
     edge = HALO * column_rows
     pieces = pl.pallas_call(
-        functools.partial(halo_kernel, cycle, columns),
+        functools.partial(halo_kernel, cycle, columns, len(geometry)),
         out_shape=[f32(edge + 8, LANES)] * 2,
-        in_specs=smem(2) + vmem(cycle),
+        in_specs=smem(2) + vmem(cycle) + [pl.BlockSpec(memory_space=pl.ANY)] * len(geometry),
         out_specs=vmem(2),
         compiler_params=params(),
         name="halo",
-    )(shifts, fractions, *ring)
+    )(shifts, fractions, *ring, *geometry)
     first, second = neighbour_columns(*pieces)
-    inner = pl.pallas_call(
-        functools.partial(inner_kernel, cells, cycle, columns, nrad, groups),
-        out_shape=f32(max(columns - 2, 1) * column_rows, LANES),
-        in_specs=smem(2) + vmem(cycle),
-        out_specs=pl.BlockSpec(memory_space=pltpu.VMEM),
-        scratch_shapes=[pltpu.VMEM((columns * column_rows, LANES), jnp.float32)],
-        compiler_params=params(),
-        name="inner",
-    )(shifts, fractions, *ring)
     theta = (np.arange(polar) + 0.5) / polar
     tilt = (1.0 + 0.5 * np.cos(np.pi * theta)).reshape(INNER, groups).T
     tilt = jnp.asarray(np.tile(tilt, (1, LANES // INNER)), jnp.float32)
+    margin = HALO if columns >= INNER else 0
+    inner = []
+    if margin:
+        inner = pl.pallas_call(
+            functools.partial(inner_kernel, cells, cycle, columns, nrad, groups, margin),
+            out_shape=[
+                f32(columns * column_rows, LANES), f32(2 * edge, LANES), f32(-(-columns // INNER), cycle, LANES)
+            ],
+            in_specs=smem(2) + vmem(1 + cycle),
+            out_specs=vmem(3),
+            scratch_shapes=[pltpu.VMEM((columns * column_rows, LANES), jnp.float32) for _ in range(2)],
+            compiler_params=params(),
+            name="inner",
+        )(shifts, fractions, tilt, *ring)
     swap = cycle == INNER and columns % INNER == 0
     rows = columns * per_column
-    cuts = [rows] * cycle
-    if swap:
-        for j in range(1, cycle // 2 + 1):
-            cuts[j] = columns // 2 * per_column
-        extra = [f32(rows - cut, LANES) for cut in cuts if cut < rows]
-    else:
-        slots = -(-columns // INNER)
-        extra = [f32(slots, cycle, LANES)]
+    slots = -(-columns // INNER)
     out = pl.pallas_call(
-        functools.partial(outer_kernel, cells, cycle, columns, nrad, groups, cuts),
-        out_shape=[f32(cut + (columns if swap else 0), LANES) for cut in cuts] + extra,
-        in_specs=smem(2) + vmem(4 + cycle),
-        out_specs=vmem(cycle + len(extra)),
+        functools.partial(outer_kernel, cells, cycle, columns, nrad, groups, margin, swap),
+        out_shape=[f32(rows + columns, LANES)] * cycle if swap else [f32(rows, LANES)] * cycle + [f32(slots, cycle, LANES)],
+        in_specs=smem(2) + vmem(3 + cycle + len(inner)),
+        out_specs=vmem(cycle + (not swap)),
         scratch_shapes=[
             pltpu.VMEM((4 * edge, LANES), jnp.float32),
             pltpu.VMEM(((columns + 2 * HALO) * column_rows, LANES), jnp.float32),
@@ -574,43 +619,40 @@
         ],
         compiler_params=params(),
         name="outer",
-    )(shifts, fractions, tilt, first, second, inner, *ring)
+    )(shifts, fractions, tilt, first, second, *ring, *inner)
     back = exchange(out[:cycle], "phi")
     if swap:
-        table = pl.pallas_call(
-            functools.partial(gather_kernel, cuts),
-            out_shape=f32(radial, nphi),
-            in_specs=vmem(cycle),
-            out_specs=pl.BlockSpec(memory_space=pltpu.VMEM),
-            compiler_params=params(),
-            name="gather",
-        )(*back)
-        back += [
-            swapped(piece, "phi", j) for piece, j in zip(out[cycle:], [j for j in range(cycle) if cuts[j] < rows])
-        ]
+        light_pieces, cut = back, rows
     else:
         light = out[cycle].reshape(slots, cycle, cells, INNER).transpose(0, 3, 2, 1).reshape(slots * INNER, nphi)[:columns]
-        table = lax.all_gather(light, "phi", axis=0, tiled=True)
+        light_pieces, cut = [lax.all_gather(light, "phi", axis=0, tiled=True)], 0
+    window = window_rows(rows_dev, NPIX, nphi)
+    table = pl.pallas_call(
+        functools.partial(gather_kernel, cells, cycle, nphi // 2, cut),
+        out_shape=f32(nphi // 2 + 16 + window, LANES),
+        in_specs=vmem(len(light_pieces)),
+        out_specs=pl.BlockSpec(memory_space=pltpu.VMEM),
+        scratch_shapes=[pltpu.VMEM((radial, nphi), jnp.float32), pltpu.VMEM((nphi, LANES), jnp.float32)],
+        compiler_params=params(),
+        name="gather",
+    )(*light_pieces)
     tables = exchange([table] * bands, "row")
 
-    rows_dev = NPIX // (cycle * bands)
-    first_row = (place * bands + row) * rows_dev
-    geometry = pixel_tiles(first_row, rows_dev, NPIX, nphi, nrad)
-    image = draw_image(tables, geometry, cells, cycle, rows_dev, NPIX, nphi, nrad)
     density_out, velocity_out = pl.pallas_call(
-        functools.partial(unpack_kernel, cycle, cuts),
+        unpack_kernel,
         out_shape=(f32(*density.shape), f32(*velocity.shape)),
-        in_specs=vmem(len(back)),
+        in_specs=vmem(cycle),
         out_specs=[hbm] * 2,
         scratch_shapes=[
             pltpu.VMEM((radial * per_column, LANES), jnp.float32),
             pltpu.VMEM(block, jnp.float32),
-            pltpu.SemaphoreType.DMA((FIELDS,)),
+            pltpu.SemaphoreType.DMA((FIELDS * SPLIT,)),
         ],
         compiler_params=params(),
         name="unpack",
     )(*back)
 
+    image = draw_image(tables, geometry, window, rows_dev, NPIX, nrad)
     return (density_out, velocity_out, image)
 
 

time: 81.1 us -> 78.9 us (0.973)
  starting transfers between devices: 47.7 us -> 35.7 us
  waiting for transfers between devices: 14.6 us -> 23.7 us
    ppermute x21 -> x17, starting transfers between devices: 46.3 us -> 34.4 us  [swapped(): lax.ppermute(piece, axis, [(p, partner(p, index, size)) for p in range(si...]
    ppermute x21 -> x17, waiting for transfers between devices: 14.1 us -> 23.7 us  [swapped(): lax.ppermute(piece, axis, [(p, partner(p, index, size)) for p in range(si...]
    pallas_call x1, Pallas kernels: 2.73 us -> 4.95 us  [body(): pl.pallas_call(functools.partial(inner_kernel, cells, cycle, columns, nra...]
    pallas_call x1, Pallas kernels: 4.39 us -> 2.64 us  [body(): pl.pallas_call(functools.partial(outer_kernel, cells, cycle, columns, nra...]
  transfers between devices with their start and end apart: 23 -> 19, of which waited for: 10 -> 6; matrix products, arithmetic and copies ran while one was open for 2% -> 2% of each run, Pallas kernels for 5% -> 8%
where the time goes in v4:
time: 78.9 us; the launch traced here: 78.7 us
  starting transfers between devices  35.7 us (45%)
  waiting for transfers between devices  23.7 us (30%)
  Pallas kernels  16.7 us (21%)
  other arithmetic  1.67 us (2%)
  between operations  0.86 us (1%)
    ppermute x17, starting transfers between devices, swapped(): lax.ppermute(piece, axis, [(p, partner(p, index, size)) for p in range(si...  34.4 us
    ppermute x17, waiting for transfers between devices, swapped(): lax.ppermute(piece, axis, [(p, partner(p, index, size)) for p in range(si...  23.7 us
    pallas_call x1, Pallas kernels, body(): pl.pallas_call(functools.partial(inner_kernel, cells, cycle, columns, nra...  4.95 us
    pallas_call x1, Pallas kernels, draw_image(): pl.pallas_call(functools.partial(image_kernel, rows, tile_rows, across),...  4.56 us
    pallas_call x1, Pallas kernels, body(): pl.pallas_call(functools.partial(outer_kernel, cells, cycle, columns, nra...  2.64 us
    pallas_call x1, Pallas kernels, body(): pl.pallas_call(pack_kernel, out_shape=[chunk] * cycle, in_specs=[hbm] * 2...  2.54 us
  transfers between devices with their start and end apart: 19, of which 6 were waited for; matrix products, arithmetic and copies ran while one was open for 2% of the time, Pallas kernels for 8%

profile of v4, /device:TPU:0, one launch (start us, length us, event | category | flops | bytes accessed | tf_op | source)
XLA Modules:
  0.0 78.7 jit_solution(13224277333366943890)
XLA Ops:
  0.6 2.5 %pack.1 = (f32[256,128]{1,0:T(8,128)}, f32[256,128]{1,0:T(8,128)}, f32[256,128]{1,0:T(8,128)}, f32[256,128]{1,0:T(8,128)}, f32[256,128]{1,0:T(8,128)}, /*index=5...) custom-call(f32[16,32,128]{2,1,0:T(8,128)} %density_ref.1, f32[3,16,32,128]{3,2,1,0:T(8,128)} %velocity_ref.1), custom_call_target="tpu_custom_call" | custom-call | tf_op jit(solution)/shard_map/pack/pallas_call | solution.py:562
  3.2 6.0 %collective-permute-start = (f32[256,128]{1,0:T(8,128)}, f32[256,128]{1,0:T(8,128)S(1)}, u32[]{:S(2)}, u32[]{:S(2)}) collective-permute-start(f32[256,128]{1,0:T(8,128)} %get-tuple-element.27), channel_id=1, source_target_pairs={{0,28},{4,24},{8,20},{12,16},{16,12},{20,8},{24,4},{28,0},{1,29},{... | collective-permute-start | bytes 393224 | tf_op jit(solution)/shard_map/ppermute | solution.py:498
  9.2 0.5 collective-permute-start.1
  9.8 0.1 collective-permute-start.2
  9.9 5.2 %collective-permute-start.4 = (f32[256,128]{1,0:T(8,128)}, f32[256,128]{1,0:T(8,128)S(1)}, u32[]{:S(2)}, u32[]{:S(2)}) collective-permute-start(f32[256,128]{1,0:T(8,128)} %get-tuple-element.31), channel_id=1, source_target_pairs={{0,20},{4,16},{8,28},{12,24},{16,4},{20,0},{24,12},{28,8},{1,21},{... | collective-permute-start | bytes 393224 | tf_op jit(solution)/shard_map/ppermute | solution.py:498
  15.1 0.4 fusion.2
  15.5 0.5 fusion.3
  16.0 0.3 subtract_clamp_fusion.refs_10_.spot_ref
  16.4 0.0 copy-start.4
  16.4 0.0 copy-start
  16.4 0.4 broadcast_subtract_fusion
  16.8 0.2 copy-done.4
  17.0 0.0 collective-permute-done.refs_1_
  17.0 0.0 copy-start.5
  17.0 4.0 %collective-permute-start.5 = (f32[256,128]{1,0:T(8,128)S(1)}, f32[256,128]{1,0:T(8,128)S(1)}, u32[]{:S(2)}, u32[]{:S(2)}) collective-permute-start(f32[256,128]{1,0:T(8,128)S(1)} %copy-done.3), channel_id=1, source_target_pairs={{0,12},{4,8},{8,4},{12,0},{16,28},{20,24},{24,20},{28,16},{1,13},{... | collective-permute-start | bytes 393224 | tf_op jit(solution)/shard_map/ppermute | solution.py:498
  21.1 0.0 collective-permute-done.1.refs_2_
  21.1 0.0 collective-permute-start.6
  21.1 0.0 collective-permute-done.2.refs_3_
  21.1 0.0 collective-permute-done.3.refs_4_
  21.1 8.8 %collective-permute-done.4.refs_5_ = f32[256,128]{1,0:T(8,128)S(1)} collective-permute-done((f32[256,128]{1,0:T(8,128)}, f32[256,128]{1,0:T(8,128)S(1)}, u32[]{:S(2)}, u32[]{:S(2)}) %collective-permute-start.4) | collective-permute-done | bytes 131104 | tf_op jit(solution)/shard_map/ppermute | solution.py:498
  29.9 1.8 %collective-permute-done.6.refs_7_ = f32[256,128]{1,0:T(8,128)S(1)} collective-permute-done((f32[256,128]{1,0:T(8,128)S(1)}, f32[256,128]{1,0:T(8,128)S(1)}, u32[]{:S(2)}, u32[]{:S(2)}) %collective-permute-start.6) | collective-permute-done | bytes 131104 | tf_op jit(solution)/shard_map/ppermute | solution.py:498
  31.7 0.6 halo.1
  32.4 0.0 copy-start.1
  32.4 0.6 collective-permute-start.7
  33.0 0.7 collective-permute-start.8
  33.7 4.9 %inner.1 = (f32[2048,128]{1,0:T(8,128)S(1)}, f32[512,128]{1,0:T(8,128)S(1)}, f32[2,8,128]{2,1,0:T(8,128)S(1)}) custom-call(s32[16]{0:T(128)S(1)} %broadcast_clamp_fusion.1.shift_ref, f32[16]{0:T(128)S(1)} %broadcast_clamp_fusion.frac_ref, f32[4,128]{1,0:T(4,128)S(1)} %copy-done.1, f32[256,128]{1,0:T(8,128)S(1)} %copy-done, ...), custom_call_target="tpu_custom_call" | custom-call | tf_op jit(solution)/shard_map/inner/pallas_call | solution.py:596
  38.6 0.0 collective-permute-done.7.first_ref
  38.6 0.0 collective-permute-done.8.second_ref
  38.6 2.6 %outer.1 = (f32[272,128]{1,0:T(8,128)S(1)}, f32[272,128]{1,0:T(8,128)S(1)}, f32[272,128]{1,0:T(8,128)S(1)}, f32[272,128]{1,0:T(8,128)S(1)}, f32[272,128]{1,0:T(8...) custom-call(s32[16]{0:T(128)S(1)} %broadcast_clamp_fusion.1.shift_ref, ...), custom_call_target="tpu_custom_call" | custom-call | tf_op jit(solution)/shard_map/outer/pallas_call | solution.py:610
  41.3 6.9 %collective-permute-start.9 = (f32[272,128]{1,0:T(8,128)S(1)}, f32[272,128]{1,0:T(8,128)S(1)}, u32[]{:S(2)}, u32[]{:S(2)}) collective-permute-start(f32[272,128]{1,0:T(8,128)S(1)} %get-tuple-element.40), channel_id=1, source_target_pairs={{0,28},{4,24},{8,20},{12,16},{16,12},{20,8},{24,4},{28,0},{1,29},{... | collective-permute-start | bytes 417800 | tf_op jit(solution)/shard_map/ppermute | solution.py:498
  48.1 0.0 collective-permute-start.10
  48.1 0.6 collective-permute-start.11
  48.8 0.2 collective-permute-start.12
  49.0 5.0 %collective-permute-start.13 = (f32[272,128]{1,0:T(8,128)S(1)}, f32[272,128]{1,0:T(8,128)S(1)}, u32[]{:S(2)}, u32[]{:S(2)}) collective-permute-start(f32[272,128]{1,0:T(8,128)S(1)} %get-tuple-element.44), channel_id=1, source_target_pairs={{0,20},{4,16},{8,28},{12,24},{16,4},{20,0},{24,12},{28,8},{1,21},{... | collective-permute-start | bytes 417800 | tf_op jit(solution)/shard_map/ppermute | solution.py:498
  54.0 0.0 collective-permute-done.9.refs_1_
  54.0 2.5 %collective-permute-start.14 = (f32[272,128]{1,0:T(8,128)S(1)}, f32[272,128]{1,0:T(8,128)S(1)}, u32[]{:S(2)}, u32[]{:S(2)}) collective-permute-start(f32[272,128]{1,0:T(8,128)S(1)} %get-tuple-element.45), channel_id=1, source_target_pairs={{0,12},{4,8},{8,4},{12,0},{16,28},{20,24},{24,20},{28,16},{1,13},{... | collective-permute-start | bytes 417800 | tf_op jit(solution)/shard_map/ppermute | solution.py:498
  56.5 0.0 collective-permute-done.10.refs_2_
  56.5 1.4 %collective-permute-start.15 = (f32[272,128]{1,0:T(8,128)S(1)}, f32[272,128]{1,0:T(8,128)S(1)}, u32[]{:S(2)}, u32[]{:S(2)}) collective-permute-start(f32[272,128]{1,0:T(8,128)S(1)} %get-tuple-element.46), channel_id=1, source_target_pairs={{0,16},{4,20},{8,24},{12,28},{16,0},{20,4},{24,8},{28,12},{1,17},{... | collective-permute-start | bytes 417800 | tf_op jit(solution)/shard_map/ppermute | solution.py:498
  57.9 1.5 %collective-permute-done.12.refs_4_ = f32[272,128]{1,0:T(8,128)S(1)} collective-permute-done((f32[272,128]{1,0:T(8,128)S(1)}, f32[272,128]{1,0:T(8,128)S(1)}, u32[]{:S(2)}, u32[]{:S(2)}) %collective-permute-start.12) | collective-permute-done | bytes 139296 | tf_op jit(solution)/shard_map/ppermute | solution.py:498
  59.3 10.1 %collective-permute-done.13.refs_5_ = f32[272,128]{1,0:T(8,128)S(1)} collective-permute-done((f32[272,128]{1,0:T(8,128)S(1)}, f32[272,128]{1,0:T(8,128)S(1)}, u32[]{:S(2)}, u32[]{:S(2)}) %collective-permute-start.13) | collective-permute-done | bytes 139296 | tf_op jit(solution)/shard_map/ppermute | solution.py:498
  69.5 0.1 gather.1.refs_0_
  69.6 0.1 collective-permute-start.18
  69.7 1.3 %collective-permute-start.17 = (f32[88,128]{1,0:T(8,128)S(1)}, f32[88,128]{1,0:T(8,128)S(1)}, u32[]{:S(2)}, u32[]{:S(2)}) collective-permute-start(f32[88,128]{1,0:T(8,128)S(1)} %gather.1.refs_0_), channel_id=1, source_target_pairs={{0,2},{1,3},{2,0},{3,1},{4,6},{5,7},{6,4},{7,5},{8,10},{9,11},{10,... | collective-permute-start | bytes 135176 | tf_op jit(solution)/shard_map/ppermute | solution.py:498
  71.0 0.5 collective-permute-start.16
  71.5 1.2 %unpack.1 = (f32[16,32,128]{2,1,0:T(8,128)}, f32[3,16,32,128]{3,2,1,0:T(8,128)}) custom-call(f32[272,128]{1,0:T(8,128)S(1)} %get-tuple-element.39.refs_0_, f32[272,128]{1,0:T(8,128)S(1)} %collective-permute-done.9.refs_1_, f32[272,128]{1,0:T(8,128)S(1)} %collective-permute-done.10.refs_2_, f32[272,128]{1,0:T(8,128)S(1)} %collective-permute-done.11.refs_3_, ...), custom_call_target="tpu_custom_call" | custom-call | tf_op jit(solution)/shard_map/unpack/pallas_call | solution.py:641
  72.8 0.8 %collective-permute-done.18.refs_3_ = f32[88,128]{1,0:T(8,128)S(1)} collective-permute-done((f32[88,128]{1,0:T(8,128)S(1)}, f32[88,128]{1,0:T(8,128)S(1)}, u32[]{:S(2)}, u32[]{:S(2)}) %collective-permute-start.18) | collective-permute-done | bytes 45088 | tf_op jit(solution)/shard_map/ppermute | solution.py:498
  73.6 0.6 collective-permute-done.17.refs_2_
  74.2 4.6 %image.1 = f32[32,1024]{1,0:T(8,128)} custom-call(s32[256]{0:T(256)S(1)} %get-tuple-element.54.refs_8_.start_ref, s32[256]{0:T(256)S(1)} %get-tuple-element.50.refs_9_.window_ref, s32[256,128]{1,0:T(8,128)S(1)} %subtract_clamp_fusion.refs_10_.spot_ref, f32[256,128]{1,0:T(8,128)S(1)} %get-tuple-element.52.refs_11_.frac_ref, ...), custom_call_target="tpu_custom_call" | custom-call | tf_op jit(solution)/shard_map/image/pallas_call | solution.py:473
  (23 shorter events, 0.1 us)
Async XLA Ops:
  3.2 13.8 %collective-permute-start = (f32[256,128]{1,0:T(8,128)}, f32[256,128]{1,0:T(8,128)S(1)}, u32[]{:S(2)}, u32[]{:S(2)}) collective-permute-start(f32[256,128]{1,0:T(8,128)} %get-tuple-element.27), channel_id=1, source_target_pairs={{0,28},{4,24},{8,20},{12,16},{16,12},{20,8},{24,4},{28,0},{1,29},{... | collective-permute-start | bytes 393224 | tf_op jit(solution)/shard_map/ppermute | solution.py:498
  9.2 11.9 %collective-permute-start.1 = (f32[256,128]{1,0:T(8,128)}, f32[256,128]{1,0:T(8,128)S(1)}, u32[]{:S(2)}, u32[]{:S(2)}) collective-permute-start(f32[256,128]{1,0:T(8,128)} %get-tuple-element.28), channel_id=1, source_target_pairs={{0,4},{4,0},{8,12},{12,8},{16,20},{20,16},{24,28},{28,24},{1,5},{5... | collective-permute-start | bytes 393224 | tf_op jit(solution)/shard_map/ppermute | solution.py:498
  9.8 11.4 %collective-permute-start.2 = (f32[256,128]{1,0:T(8,128)}, f32[256,128]{1,0:T(8,128)S(1)}, u32[]{:S(2)}, u32[]{:S(2)}) collective-permute-start(f32[256,128]{1,0:T(8,128)} %get-tuple-element.29), channel_id=1, source_target_pairs={{0,24},{4,28},{8,16},{12,20},{16,8},{20,12},{24,0},{28,4},{1,25},{... | collective-permute-start | bytes 393224 | tf_op jit(solution)/shard_map/ppermute | solution.py:498
  9.9 11.3 %collective-permute-start.3 = (f32[256,128]{1,0:T(8,128)}, f32[256,128]{1,0:T(8,128)S(1)}, u32[]{:S(2)}, u32[]{:S(2)}) collective-permute-start(f32[256,128]{1,0:T(8,128)} %get-tuple-element.30), channel_id=1, source_target_pairs={{0,8},{4,12},{8,0},{12,4},{16,24},{20,28},{24,16},{28,20},{1,9},{5... | collective-permute-start | bytes 393224 | tf_op jit(solution)/shard_map/ppermute | solution.py:498
  9.9 20.0 %collective-permute-start.4 = (f32[256,128]{1,0:T(8,128)}, f32[256,128]{1,0:T(8,128)S(1)}, u32[]{:S(2)}, u32[]{:S(2)}) collective-permute-start(f32[256,128]{1,0:T(8,128)} %get-tuple-element.31), channel_id=1, source_target_pairs={{0,20},{4,16},{8,28},{12,24},{16,4},{20,0},{24,12},{28,8},{1,21},{... | collective-permute-start | bytes 393224 | tf_op jit(solution)/shard_map/ppermute | solution.py:498
  16.0 1.0 %copy-start.3 = (f32[256,128]{1,0:T(8,128)S(1)}, f32[256,128]{1,0:T(8,128)}, u32[]{:S(2)}) copy-start(f32[256,128]{1,0:T(8,128)} %get-tuple-element.32) | copy-start | bytes 393220
  16.4 0.7 copy-start.4
  16.4 4.7 %copy-start.2 = (f32[256,128]{1,0:T(8,128)S(1)}, f32[256,128]{1,0:T(8,128)}, u32[]{:S(2)}) copy-start(f32[256,128]{1,0:T(8,128)} %get-tuple-element.33) | copy-start | bytes 393220
  16.4 15.4 %copy-start = (f32[256,128]{1,0:T(8,128)S(1)}, f32[256,128]{1,0:T(8,128)}, u32[]{:S(2)}) copy-start(f32[256,128]{1,0:T(8,128)} %get-tuple-element.26.refs_0_) | copy-start | bytes 393220
  17.0 4.1 %copy-start.5 = (f32[16]{0:T(128)S(1)}, f32[16]{0:T(128)}, u32[]{:S(2)}) copy-start(f32[16]{0:T(128)} %param.8) | copy-start | bytes 196
  17.0 12.8 %collective-permute-start.5 = (f32[256,128]{1,0:T(8,128)S(1)}, f32[256,128]{1,0:T(8,128)S(1)}, u32[]{:S(2)}, u32[]{:S(2)}) collective-permute-start(f32[256,128]{1,0:T(8,128)S(1)} %copy-done.3), channel_id=1, source_target_pairs={{0,12},{4,8},{8,4},{12,0},{16,28},{20,24},{24,20},{28,16},{1,13},{... | collective-permute-start | bytes 393224 | tf_op jit(solution)/shard_map/ppermute | solution.py:498
  21.1 10.7 %collective-permute-start.6 = (f32[256,128]{1,0:T(8,128)S(1)}, f32[256,128]{1,0:T(8,128)S(1)}, u32[]{:S(2)}, u32[]{:S(2)}) collective-permute-start(f32[256,128]{1,0:T(8,128)S(1)} %copy-done.2), channel_id=1, source_target_pairs={{0,16},{4,20},{8,24},{12,28},{16,0},{20,4},{24,8},{28,12},{1,17},{... | collective-permute-start | bytes 393224 | tf_op jit(solution)/shard_map/ppermute | solution.py:498
  32.4 1.3 %copy-start.1 = (f32[4,128]{1,0:T(4,128)S(1)}, f32[4,128]{1,0:T(4,128)}, u32[]{:S(2)}) copy-start(f32[4,128]{1,0:T(4,128)} %constant.142.clone.tilt_ref) | copy-start | bytes 6148
  32.4 6.2 %collective-permute-start.7 = (f32[264,128]{1,0:T(8,128)S(1)}, f32[264,128]{1,0:T(8,128)S(1)}, u32[]{:S(2)}, u32[]{:S(2)}) collective-permute-start(f32[264,128]{1,0:T(8,128)S(1)} %get-tuple-element.34), channel_id=1, source_target_pairs={{0,4},{8,12},{16,20},{24,28},{1,5},{9,13},{17,21},{25,29},{2,6},{1... | collective-permute-start | bytes 405512 | tf_op jit(solution)/shard_map/ppermute | solution.py:538
  33.0 5.6 %collective-permute-start.8 = (f32[264,128]{1,0:T(8,128)S(1)}, f32[264,128]{1,0:T(8,128)S(1)}, u32[]{:S(2)}, u32[]{:S(2)}) collective-permute-start(f32[264,128]{1,0:T(8,128)S(1)} %get-tuple-element.35), channel_id=1, source_target_pairs={{4,8},{12,16},{20,24},{28,1},{5,9},{13,17},{21,25},{29,2},{6,10},{... | collective-permute-start | bytes 405512 | tf_op jit(solution)/shard_map/ppermute | solution.py:538
  41.3 12.7 %collective-permute-start.9 = (f32[272,128]{1,0:T(8,128)S(1)}, f32[272,128]{1,0:T(8,128)S(1)}, u32[]{:S(2)}, u32[]{:S(2)}) collective-permute-start(f32[272,128]{1,0:T(8,128)S(1)} %get-tuple-element.40), channel_id=1, source_target_pairs={{0,28},{4,24},{8,20},{12,16},{16,12},{20,8},{24,4},{28,0},{1,29},{... | collective-permute-start | bytes 417800 | tf_op jit(solution)/shard_map/ppermute | solution.py:498
  48.1 8.3 %collective-permute-start.10 = (f32[272,128]{1,0:T(8,128)S(1)}, f32[272,128]{1,0:T(8,128)S(1)}, u32[]{:S(2)}, u32[]{:S(2)}) collective-permute-start(f32[272,128]{1,0:T(8,128)S(1)} %get-tuple-element.41), channel_id=1, source_target_pairs={{0,4},{4,0},{8,12},{12,8},{16,20},{20,16},{24,28},{28,24},{1,5},{5... | collective-permute-start | bytes 417800 | tf_op jit(solution)/shard_map/ppermute | solution.py:498
  48.1 9.7 %collective-permute-start.11 = (f32[272,128]{1,0:T(8,128)S(1)}, f32[272,128]{1,0:T(8,128)S(1)}, u32[]{:S(2)}, u32[]{:S(2)}) collective-permute-start(f32[272,128]{1,0:T(8,128)S(1)} %get-tuple-element.42), channel_id=1, source_target_pairs={{0,24},{4,28},{8,16},{12,20},{16,8},{20,12},{24,0},{28,4},{1,25},{... | collective-permute-start | bytes 417800 | tf_op jit(solution)/shard_map/ppermute | solution.py:498
  48.8 10.6 %collective-permute-start.12 = (f32[272,128]{1,0:T(8,128)S(1)}, f32[272,128]{1,0:T(8,128)S(1)}, u32[]{:S(2)}, u32[]{:S(2)}) collective-permute-start(f32[272,128]{1,0:T(8,128)S(1)} %get-tuple-element.43), channel_id=1, source_target_pairs={{0,8},{4,12},{8,0},{12,4},{16,24},{20,28},{24,16},{28,20},{1,9},{5... | collective-permute-start | bytes 417800 | tf_op jit(solution)/shard_map/ppermute | solution.py:498
  49.0 20.5 %collective-permute-start.13 = (f32[272,128]{1,0:T(8,128)S(1)}, f32[272,128]{1,0:T(8,128)S(1)}, u32[]{:S(2)}, u32[]{:S(2)}) collective-permute-start(f32[272,128]{1,0:T(8,128)S(1)} %get-tuple-element.44), channel_id=1, source_target_pairs={{0,20},{4,16},{8,28},{12,24},{16,4},{20,0},{24,12},{28,8},{1,21},{... | collective-permute-start | bytes 417800 | tf_op jit(solution)/shard_map/ppermute | solution.py:498
  54.0 15.5 %collective-permute-start.14 = (f32[272,128]{1,0:T(8,128)S(1)}, f32[272,128]{1,0:T(8,128)S(1)}, u32[]{:S(2)}, u32[]{:S(2)}) collective-permute-start(f32[272,128]{1,0:T(8,128)S(1)} %get-tuple-element.45), channel_id=1, source_target_pairs={{0,12},{4,8},{8,4},{12,0},{16,28},{20,24},{24,20},{28,16},{1,13},{... | collective-permute-start | bytes 417800 | tf_op jit(solution)/shard_map/ppermute | solution.py:498
  56.5 13.0 %collective-permute-start.15 = (f32[272,128]{1,0:T(8,128)S(1)}, f32[272,128]{1,0:T(8,128)S(1)}, u32[]{:S(2)}, u32[]{:S(2)}) collective-permute-start(f32[272,128]{1,0:T(8,128)S(1)} %get-tuple-element.46), channel_id=1, source_target_pairs={{0,16},{4,20},{8,24},{12,28},{16,0},{20,4},{24,8},{28,12},{1,17},{... | collective-permute-start | bytes 417800 | tf_op jit(solution)/shard_map/ppermute | solution.py:498
  69.6 4.0 %collective-permute-start.18 = (f32[88,128]{1,0:T(8,128)S(1)}, f32[88,128]{1,0:T(8,128)S(1)}, u32[]{:S(2)}, u32[]{:S(2)}) collective-permute-start(f32[88,128]{1,0:T(8,128)S(1)} %gather.1.refs_0_), channel_id=1, source_target_pairs={{0,3},{1,2},{2,1},{3,0},{4,7},{5,6},{6,5},{7,4},{8,11},{9,10},{10,... | collective-permute-start | bytes 135176 | tf_op jit(solution)/shard_map/ppermute | solution.py:498
  69.7 4.5 %collective-permute-start.17 = (f32[88,128]{1,0:T(8,128)S(1)}, f32[88,128]{1,0:T(8,128)S(1)}, u32[]{:S(2)}, u32[]{:S(2)}) collective-permute-start(f32[88,128]{1,0:T(8,128)S(1)} %gather.1.refs_0_), channel_id=1, source_target_pairs={{0,2},{1,3},{2,0},{3,1},{4,6},{5,7},{6,4},{7,5},{8,10},{9,11},{10,... | collective-permute-start | bytes 135176 | tf_op jit(solution)/shard_map/ppermute | solution.py:498
  71.0 3.2 %collective-permute-start.16 = (f32[88,128]{1,0:T(8,128)S(1)}, f32[88,128]{1,0:T(8,128)S(1)}, u32[]{:S(2)}, u32[]{:S(2)}) collective-permute-start(f32[88,128]{1,0:T(8,128)S(1)} %gather.1.refs_0_), channel_id=1, source_target_pairs={{0,1},{1,0},{2,3},{3,2},{4,5},{5,4},{6,7},{7,6},{8,9},{9,8},{10,11... | collective-permute-start | bytes 135176 | tf_op jit(solution)/shard_map/ppermute | solution.py:498
